TPU v7x, 256 devices: a whole 4x4x8 slice. The times are simulated.
256 devices in a mesh: row: 32 (over y, z), col: 8 (over x, core).
Axes of the slice: x: 4, y: 4, z: 8, core: 2. Of those that a mesh axis runs over, the one named last changes fastest.
Arguments:
- near_tiles: bfloat16 [64, 2, 8, 512, 512], P('row', None, 'col'), may hold values from -3 to 3
- basis_u: bfloat16 [64, 2, 8, 64, 512], P('row', None, 'col'), may hold values from -1.75 to 1.75
- basis_v: bfloat16 [64, 2, 8, 64, 512], P('row', None, 'col'), may hold values from -1.75 to 1.75
- near_mask: int32 [64, 2, 8], P('row', None, 'col'), may hold values from 0 to 1, as said below
- ranks: int32 [64, 2, 8], P('row', None, 'col'), may hold values from 1 to 64
- row_map: int32 [64], replicated, may hold values from 0 to 63, as said below
Outputs:
- factored: bfloat16 [64, 2, 8, 512, 512], P('row', None, 'col')
Inputs may be any that keep to these rules, and one draw needn't show every extreme that they name: row_map is a permutation of 0 to 63. near_mask is 1 on every tile whose tile row and tile column differ by at most one.
All inputs are finite; a program needn't handle non-finite values.
Results may differ from a plain program's by a relative error of at most 0.0045.
Values may be sent and summed in bfloat16 or wider, within the bound.
No kernel may reach another device: no remote copies, remote signals or barrier semaphores. Data moves between devices by JAX's collectives and lax.ppermute only.
A program may use at most 64 MiB of HBM per device.

v0:
```python
import math

import jax
import jax.numpy as jnp
from jax import lax
from jax.sharding import PartitionSpec as P

TILE = 512
KMAX = 64
NS_STEPS = 3
PANELS = 2


shift_factor = 1.1


def broadcast(block, axis, owner):
    block = jnp.where(lax.axis_index(axis) == owner, block, jnp.zeros_like(block))
    return lax.psum(block, axis)


def newton_inverse(pivot_tile):
    identity = jnp.eye(TILE, dtype=jnp.float32)
    approx = identity / (shift_factor * math.sqrt(TILE))
    for sweep in range(NS_STEPS):
        product = jnp.dot(pivot_tile, approx, precision=lax.Precision.HIGHEST)
        approx = jnp.dot(approx, 2.0 * identity - product, precision=lax.Precision.HIGHEST)
    return approx.astype(jnp.bfloat16)


def body(near_tiles, basis_u, basis_v, near_mask, ranks, row_map):
    slot_count = near_tiles.shape[0]
    col_slots = near_tiles.shape[1]
    col_count = lax.axis_size("col")
    row_index = lax.axis_index("row")
    col_index = lax.axis_index("col")
    total_rows = row_map.shape[0]
    diag_shift = shift_factor * math.sqrt(TILE)
    identity = jnp.eye(TILE, dtype=jnp.float32)
    near_local = near_tiles.reshape(slot_count, col_slots, TILE, TILE)
    near_flags = near_mask.reshape(slot_count, col_slots)
    rank_rows = ranks.reshape(slot_count, col_slots)
    kept_cols = (jnp.arange(KMAX, dtype=jnp.int32)[None, None, :] < rank_rows[:, :, None]).astype(
        jnp.bfloat16
    )
    left_basis = basis_u.reshape(slot_count, col_slots, KMAX, TILE) * kept_cols[..., None]
    right_basis = basis_v.reshape(slot_count, col_slots, KMAX, TILE)
    lowrank = jnp.einsum(
        "stkp,stkq->stpq", left_basis, right_basis, preferred_element_type=jnp.float32
    )
    held_rows = lax.dynamic_slice_in_dim(row_map, row_index * slot_count, slot_count)
    held_cols = jnp.arange(col_slots, dtype=jnp.int32) * col_count + col_index
    on_diag = (held_rows[:, None] == held_cols[None, :]).astype(jnp.float32)
    dense = jnp.where(near_flags[..., None, None] > 0, near_local.astype(jnp.float32), 0.0)
    working = dense + lowrank + diag_shift * on_diag[..., None, None] * identity
    for elimination in range(PANELS):
        owner_slot = jnp.sum(
            jnp.where(row_map == elimination, jnp.arange(total_rows, dtype=jnp.int32), 0)
        )
        owner_row = owner_slot // slot_count
        local_slot = owner_slot % slot_count
        col_root = elimination % col_count
        col_slot = elimination // col_count
        owner_tiles = lax.dynamic_index_in_dim(working, local_slot, 0, keepdims=False)
        candidate = owner_tiles[col_slot]
        column_tiles = working[:, col_slot].astype(jnp.bfloat16)
        row_tiles = owner_tiles.astype(jnp.bfloat16)
        pivot_tile = broadcast(candidate, "row", owner_row)
        inverse = newton_inverse(pivot_tile)
        local_mult = jnp.einsum(
            "spq,qr->spr", column_tiles, inverse, preferred_element_type=jnp.float32
        ).astype(jnp.bfloat16)
        multipliers = broadcast(local_mult, "col", col_root)
        pivot_row = broadcast(row_tiles, "row", owner_row)
        update = jnp.einsum(
            "spq,tqr->stpr", multipliers, pivot_row, preferred_element_type=jnp.float32
        )
        live_tiles = (held_rows > elimination)[:, None] & (held_cols > elimination)[None, :]
        working = working - jnp.where(live_tiles[..., None, None], update, 0.0)
    return working.astype(jnp.bfloat16).reshape(slot_count, col_slots, 1, TILE, TILE)


def solution(mesh):
    return jax.shard_map(
        body,
        mesh=mesh,
        in_specs=(
            P("row", None, "col", None, None),
            P("row", None, "col", None, None),
            P("row", None, "col", None, None),
            P("row", None, "col"),
            P("row", None, "col"),
            P(),
        ),
        out_specs=P("row", None, "col", None, None),
        check_vma=False,
    )
```

profile of v0, /device:TPU:12, one launch (start us, length us, event | category | flops | bytes accessed | tf_op | source)
XLA Modules:
  0.0 771.0 jit_solution(214500814724899634)
XLA Ops:
  6.5 0.0 copy-start
  6.5 0.0 all-reduce.9.cloned.1.call-start
  6.5 1.4 fusion.48
  10.5 0.1 fusion.36
  10.7 0.7 broadcast_compare_fusion.2
  11.4 0.7 broadcast_compare_fusion
  12.1 0.8 compare_convert_fusion
  12.8 0.1 compare_select_fusion.2
  12.9 0.0 copy-done
  12.9 3.1 fusion.1
  16.1 0.0 copy-start.1
  16.1 1.9 copy-done.1
  18.0 1.1 fusion.31
  19.1 0.0 all-reduce.9.cloned.1.call-update
  19.1 0.0 all-reduce.7.cloned.1.call-start
  19.1 2.7 fusion.23
  21.8 0.0 all-reduce.7.cloned.1.call-update
  21.9 0.0 all-reduce.11.cloned.1.call-start
  21.9 148.4 %all-reduce.9.cloned.1.call-done = f32[512,512]{1,0:T(8,128)} async-done(((f32[512,512]{1,0:T(8,128)}), f32[512,512]{1,0:T(8,128)}) %all-reduce.9.cloned.1.call-update) | async-done | bytes 1048592 | tf_op jit(solution)/shard_map/psum | solution.py:19
  170.3 0.0 copy-start.6
  170.3 3.1 select_subtract_fusion.5
  173.4 1.8 fusion.9
  175.2 0.0 copy-done.6
  175.2 1.9 select_subtract_fusion.4
  177.1 0.0 copy-start.2
  177.1 1.8 fusion.57
  179.0 1.9 select_subtract_fusion.3
  180.8 1.9 fusion.20
  182.7 0.0 copy-done.2
  182.7 1.7 fusion.18
  184.4 0.0 all-reduce.11.cloned.1.call-update
  184.4 0.0 all-reduce.15.cloned.1.call-start
  187.0 0.1 broadcast_and_fusion.1
  187.1 133.6 %all-reduce.7.cloned.1.call-done = bf16[2,512,512]{2,1,0:T(8,128)(2,1)} async-done(((bf16[2,512,512]{2,1,0:T(8,128)(2,1)}), bf16[2,512,512]{2,1,0:T(8,128)(2,1)}) %all-reduce.7.cloned.1.call-update) | async-done | bytes 1048592 | tf_op jit(solution)/shard_map/psum | solution.py:19
  320.7 64.5 %all-reduce.11.cloned.1.call-done = bf16[2,512,512]{2,1,0:T(8,128)(2,1)} async-done(((bf16[2,512,512]{2,1,0:T(8,128)(2,1)}), bf16[2,512,512]{2,1,0:T(8,128)(2,1)}) %all-reduce.11.cloned.1.call-update) | async-done | bytes 1048592 | tf_op jit(solution)/shard_map/psum | solution.py:19
  385.2 4.2 fusion.4
  389.4 0.0 copy-start.3
  389.4 1.9 copy-done.3
  391.3 1.1 fusion.30
  392.4 0.0 all-reduce.15.cloned.1.call-update
  392.4 0.0 all-reduce.13.cloned.1.call-start
  392.4 2.7 fusion.25
  395.1 0.0 all-reduce.13.cloned.1.call-update
  395.2 0.2 all-reduce.17.cloned.1.call-start
  395.4 148.8 %all-reduce.15.cloned.1.call-done = f32[512,512]{1,0:T(8,128)} async-done(((f32[512,512]{1,0:T(8,128)}), f32[512,512]{1,0:T(8,128)}) %all-reduce.15.cloned.1.call-update) | async-done | bytes 1048592 | tf_op jit(solution)/shard_map/psum | solution.py:19
  544.2 0.0 copy-start.5
  544.2 3.1 select_subtract_fusion.2
  547.3 1.8 fusion.5
  549.1 0.0 copy-done.5
  549.1 1.9 select_subtract_fusion.1
  551.0 0.0 copy-start.4
  551.0 1.9 fusion.58
  552.8 1.9 select_subtract_fusion
  554.7 1.9 fusion.21
  556.5 0.0 copy-done.4
  556.6 1.7 fusion.19
  558.2 0.0 all-reduce.17.cloned.1.call-update
  558.3 0.1 broadcast_and_fusion
  558.3 136.0 %all-reduce.13.cloned.1.call-done = bf16[2,512,512]{2,1,0:T(8,128)(2,1)} async-done(((bf16[2,512,512]{2,1,0:T(8,128)(2,1)}), bf16[2,512,512]{2,1,0:T(8,128)(2,1)}) %all-reduce.13.cloned.1.call-update) | async-done | bytes 1048592 | tf_op jit(solution)/shard_map/psum | solution.py:19
  694.4 64.4 %all-reduce.17.cloned.1.call-done = bf16[2,512,512]{2,1,0:T(8,128)(2,1)} async-done(((bf16[2,512,512]{2,1,0:T(8,128)(2,1)}), bf16[2,512,512]{2,1,0:T(8,128)(2,1)}) %all-reduce.17.cloned.1.call-update) | async-done | bytes 1048592 | tf_op jit(solution)/shard_map/psum | solution.py:19
  758.8 5.4 fusion.13
  (4 shorter events, 0.0 us)
Async XLA Ops:
  6.5 6.4 copy-start
  6.5 163.7 %all-reduce.9.cloned.1.call-start = ((), (), s32[]{:S(2)}) async-start(), calls=%async_computation.1 | async-start | bytes 2097152 | tf_op jit(solution)/shard_map/psum | solution.py:19
  16.1 1.9 copy-start.1
  19.1 301.6 %all-reduce.7.cloned.1.call-start = ((), (), s32[]{:S(2)}) async-start(), calls=%async_computation | async-start | bytes 2097152 | tf_op jit(solution)/shard_map/psum | solution.py:19
  21.9 363.3 %all-reduce.11.cloned.1.call-start = ((), (), s32[]{:S(2)}) async-start(), calls=%async_computation.2 | async-start | bytes 2097152 | tf_op jit(solution)/shard_map/psum | solution.py:19
  170.3 4.9 copy-start.6
  177.1 5.6 copy-start.2
  184.4 359.8 %all-reduce.15.cloned.1.call-start = ((), (), s32[]{:S(2)}) async-start(), calls=%async_computation.4 | async-start | bytes 2097152 | tf_op jit(solution)/shard_map/psum | solution.py:19
  389.4 1.9 copy-start.3
  392.4 302.0 %all-reduce.13.cloned.1.call-start = ((), (), s32[]{:S(2)}) async-start(), calls=%async_computation.3 | async-start | bytes 2097152 | tf_op jit(solution)/shard_map/psum | solution.py:19
  395.2 363.6 %all-reduce.17.cloned.1.call-start = ((), (), s32[]{:S(2)}) async-start(), calls=%async_computation.5 | async-start | bytes 2097152 | tf_op jit(solution)/shard_map/psum | solution.py:19
  544.2 4.9 copy-start.5
  551.0 5.6 copy-start.4
Sparse Core Ops, SparseCore 0:
  19.2 151.0 all-reduce.8
  173.7 146.8 all-reduce.6
  323.0 62.1 all-reduce.10
  392.5 151.6 all-reduce.14
  547.4 146.9 all-reduce.12
  696.6 62.1 all-reduce.16
where the time goes:
time: 775 us; the launch traced here: 771 us
  waiting for transfers between devices  696 us (90%)
  matrix products  40.7 us (5%)
  between operations  18.9 us (2%)
  other arithmetic  11.4 us (1%)
    psum x6, waiting for transfers between devices, broadcast(): return lax.psum(block, axis)  696 us
  transfers between devices with their start and end apart: 6, of which 6 were waited for; matrix products, arithmetic and copies ran while one was open for 4% of the time, Pallas kernels for 0%

commit v1 on v0

v1 whole, which is shorter than its diff:
```python
import math

import jax
import jax.numpy as jnp
from jax import lax
from jax.sharding import PartitionSpec as P

TILE = 512
KMAX = 64
RAW = TILE + 2 * KMAX
LANES = 128
BLOCKS = TILE // LANES
SHIFT = 1.1 * math.sqrt(TILE)
NY, NZ, NX = 4, 8, 4
BF = jnp.bfloat16
F32 = jnp.float32


def dot(a, b):
    return jnp.dot(a, b, preferred_element_type=F32)


def dot_hi(a, b):
    return jnp.dot(a, b, precision=lax.Precision.HIGHEST)


def pack(raw):
    lead = raw.shape[:-2]
    raw = raw.reshape(*lead, RAW, BLOCKS, LANES)
    return jnp.swapaxes(raw, -3, -2).reshape(*lead, BLOCKS * RAW, LANES)


def unpack(packed):
    lead = packed.shape[:-2]
    packed = packed.reshape(*lead, BLOCKS, RAW, LANES)
    return jnp.swapaxes(packed, -3, -2).reshape(*lead, RAW, TILE)


def build(raw, diag):
    near = raw[:TILE].astype(F32)
    left, right = raw[TILE : TILE + KMAX], raw[TILE + KMAX :]
    low = lax.dot_general(left, right, (((0,), (0,)), ((), ())), preferred_element_type=F32)
    return near + low + jnp.where(diag, SHIFT, 0.0) * jnp.eye(TILE, dtype=F32)


def inverse(pivot):
    eye = jnp.eye(TILE, dtype=F32)
    e = eye - pivot * (1.0 / SHIFT)
    e2 = dot_hi(e, e)
    s = eye + e + e2 + dot_hi(e, e2)
    e4 = dot_hi(e2, e2)
    return ((s + dot_hi(s, e4)) * (1.0 / SHIFT)).astype(BF)


def col_pairs(dx):
    return [(core, dx * 2 + core) for core in range(2)]


def spread_x(value, x):
    parts = [lax.ppermute(value, "col", col_pairs(dx)) for dx in (1, 3, 2)]
    return jnp.where(x == 0, value, parts[0] + parts[1] + parts[2])


def swap_cores(value, core):
    other = lax.ppermute(value, "col", [(c, c ^ 1) for c in range(2 * NX)])
    return jnp.where(core == 0, value, other), jnp.where(core == 0, other, value)


def body(near_tiles, basis_u, basis_v, near_mask, ranks, row_map):
    row = lax.axis_index("row")
    col = lax.axis_index("col")
    x, core = col // 2, col % 2
    near = near_tiles.reshape(2, 2, TILE, TILE)
    kept = jnp.arange(KMAX, dtype=jnp.int32)[None, None, :] < ranks.reshape(2, 2)[:, :, None]
    left = jnp.where(kept[..., None], basis_u.reshape(2, 2, KMAX, TILE), 0)
    near = jnp.where(near_mask.reshape(2, 2, 1, 1) > 0, near, 0)
    raw = jnp.concatenate([near, left, basis_v.reshape(2, 2, KMAX, TILE)], axis=2)
    slots = jnp.arange(64, dtype=jnp.int32)
    owner = [jnp.sum(jnp.where(row_map == k, slots, 0)) for k in range(2)]
    owner_row = [o // 2 for o in owner]
    held = lax.dynamic_slice_in_dim(row_map, row * 2, 2)

    cols = spread_x(raw[:, 0], x)
    cols = swap_cores(cols, core)

    def payload(slot):
        tiles = lax.dynamic_index_in_dim(raw, slot, 0, keepdims=False)
        return jnp.swapaxes(pack(tiles).reshape(2, 32, -1, LANES), 0, 1)

    def scatter(slot):
        return lax.all_to_all(payload(slot), "row", 0, 0)

    def take(got, k):
        return lax.dynamic_index_in_dim(got, owner_row[k], 0, keepdims=False)

    def apart():
        return jnp.stack([take(scatter(owner[k] % 2), k) for k in range(2)])

    def merged():
        slot = jnp.where(row == owner_row[0], owner[0], owner[1]) % 2
        got = scatter(slot)
        return jnp.stack([take(got, k) for k in range(2)])

    chunk = lax.cond(owner_row[0] == owner_row[1], apart, merged)
    pivots = spread_x(chunk[:, 0], x)
    bundle = jnp.concatenate([pivots, chunk.reshape(4, -1, LANES)])
    z_groups = [[y * NZ + z for z in range(NZ)] for y in range(NY)]
    y_groups = [[y * NZ + z for y in range(NY)] for z in range(NZ)]

    def gather(value, count, groups):
        return lax.all_to_all(
            jnp.broadcast_to(value[None], (count, *value.shape)), "row", 0, 0, axis_index_groups=groups
        )

    line = gather(bundle, NZ, z_groups)

    def whole(part):
        got = gather(part, NY, y_groups)
        got = got.reshape(32, *got.shape[2:])
        return unpack(jnp.swapaxes(got, 0, 1).reshape(got.shape[1], -1, LANES))

    piv = whole(line[:, :2])
    rows = whole(line[:, 2:]).reshape(2, 2, RAW, TILE)
    piv = swap_cores(piv, core)

    inv0 = inverse(build(piv[0][0], True))
    pivot_row1 = build(piv[1][0], False).astype(BF)
    mult_p1 = dot(build(piv[0][1], False).astype(BF), inv0).astype(BF)
    inv1 = inverse(build(piv[1][1], True) - dot(mult_p1, pivot_row1))

    mult = []
    for s in range(2):
        first = dot(build(cols[0][s], held[s] == 0).astype(BF), inv0).astype(BF)
        second = build(cols[1][s], held[s] == 1) - jnp.where(held[s] > 0, dot(first, pivot_row1), 0.0)
        mult.append((first, dot(second.astype(BF), inv1).astype(BF)))
    out = []
    for t in range(2):
        j = t * 8 + col
        row0 = build(rows[0, t], j == 0).astype(BF)
        row1 = build(rows[1, t], j == 1) - jnp.where(j > 0, dot(mult_p1, row0), 0.0)
        row1 = row1.astype(BF)
        for s in range(2):
            tile = build(raw[s, t], held[s] == j)
            tile = tile - jnp.where((held[s] > 0) & (j > 0), dot(mult[s][0], row0), 0.0)
            tile = tile - jnp.where((held[s] > 1) & (j > 1), dot(mult[s][1], row1), 0.0)
            out.append(tile.astype(BF))
    out = jnp.stack([out[0], out[2], out[1], out[3]])
    return out.reshape(2, 2, 1, TILE, TILE)


def solution(mesh):
    return jax.shard_map(
        body,
        mesh=mesh,
        in_specs=(
            P("row", None, "col", None, None),
            P("row", None, "col", None, None),
            P("row", None, "col", None, None),
            P("row", None, "col"),
            P("row", None, "col"),
            P(),
        ),
        out_specs=P("row", None, "col", None, None),
        check_vma=False,
    )
```

time: 775 us -> 263 us (0.34)
  the two profiles are of different devices: /device:TPU:12 before, /device:TPU:34 now
where the time goes in v1:
time: 263 us; the launch traced here: 262 us
  waiting for transfers between devices  104 us (40%)
  matrix products  54.8 us (21%)
  local copies, waits for them, and re-layouts  39.3 us (15%)
  starting transfers between devices  32 us (12%)
  other arithmetic  16.5 us (6%)
  between operations  13.4 us (5%)
    ppermute x6, waiting for transfers between devices, spread_x(): parts = [lax.ppermute(value, 'col', col_pairs(dx)) for dx in (1, 3, 2)]  38.1 us
    all_to_all x1, waiting for transfers between devices, scatter(): return lax.all_to_all(payload(slot), 'row', 0, 0)  33.9 us
    all_to_all x3, waiting for transfers between devices, gather(): lax.all_to_all(jnp.broadcast_to(value[None], (count, *value.shape)), 'row...  32.3 us
    dot_general x16, matrix products, dot(): return jnp.dot(a, b, preferred_element_type=F32)  25.5 us
    dot_general x8, matrix products, dot_hi(): return jnp.dot(a, b, precision=lax.Precision.HIGHEST)  17.3 us
    all_to_all x3, starting transfers between devices, gather(): lax.all_to_all(jnp.broadcast_to(value[None], (count, *value.shape)), 'row...  12.8 us
    dot_general x13, matrix products, build(): lax.dot_general(left, right, (((0,), (0,)), ((), ())), preferred_element_...  12 us
    all_to_all x1, starting transfers between devices, scatter(): return lax.all_to_all(payload(slot), 'row', 0, 0)  11.4 us
  transfers between devices with their start and end apart: 12, of which 5 were waited for; matrix products, arithmetic and copies ran while one was open for 11% of the time, Pallas kernels for 0%

profile of v1, /device:TPU:34, one launch (start us, length us, event | category | flops | bytes accessed | tf_op | source)
XLA Modules:
  0.0 261.7 jit_solution(801804617272377654)
XLA Ops:
  0.0 1.4 fusion.82
  8.1 1.0 copy.73
  9.1 1.1 bitcast_select_fusion.1
  10.1 1.9 bitcast_select_fusion
  12.2 1.1 copy-done
  13.3 60.4 %conditional.1 = (bf16[2,2,80,128]{3,2,1,0:T(8,128)(2,1)}, bf16[2,2,80,128]{3,2,1,0:T(8,128)(2,1)S(1)}, bf16[2,1,80,128]{3,2,1,0:T(8,128)(2,1)}, bf16[2,1,80,128]{3,2,1,0:T(8,128)(2,1)S(1)}) conditional(s32[]{:T(128)} %convert_element_type.198, (s32[]{:T(128)}, s32[]{:T(128)}, s32[]{:T(128)}, s32[]{:T(128)}, bf16[2,2,640,512]{3,2,0,1:T(8,128)(2,1)S(1)}, ...), branch_computations={%region_2.3_spmd, %region_3.4_spmd} | conditional | flops 61474 | bytes 29532624 | solution.py:104
  14.6 2.6 copy.51
  17.3 2.5 constant_dynamic-slice_fusion.2
  19.7 2.5 copy.40
  22.2 2.5 copy.41
  24.7 11.4 %all-to-all-start = ((bf16[32,2,80,128]{3,2,1,0:T(8,128)(2,1)}), bf16[32,2,80,128]{3,2,1,0:T(8,128)(2,1)}, u32[]{:S(2)}, u32[]{:S(2)}) async-start(bf16[32,2,80,128]{3,2,1,0:T(8,128)(2,1)} %copy.41), calls=%async_computation | async-start | bytes 2621440 | tf_op jit(solution)/shard_map/cond/branch_0_fun/all_to_all | solution.py:91
  36.1 33.9 %all-to-all-done = bf16[32,2,80,128]{3,2,1,0:T(8,128)(2,1)} async-done(((bf16[32,2,80,128]{3,2,1,0:T(8,128)(2,1)}), bf16[32,2,80,128]{3,2,1,0:T(8,128)(2,1)}, u32[]{:S(2)}, u32[]{:S(2)}) %all-to-all-start) | async-done | bytes 1310752 | tf_op jit(solution)/shard_map/cond/branch_0_fun/all_to_all | solution.py:91
  74.4 1.3 collective-permute-start.4
  76.4 5.8 %collective-permute-done.4 = bf16[2,80,128]{2,1,0:T(8,128)(2,1)S(1)} collective-permute-done((bf16[2,80,128]{2,1,0:T(8,128)(2,1)S(1)}, bf16[2,80,128]{2,1,0:T(8,128)(2,1)S(1)}, u32[]{:S(2)}, u32[]{:S(2)}) %collective-permute-start.4) | collective-permute-done | bytes 40992 | tf_op jit(solution)/shard_map/ppermute | solution.py:60
  82.2 1.1 broadcast_in_dim.64
  83.3 4.6 %all-to-all-start.3 = ((bf16[8,6,80,128]{3,2,1,0:T(8,128)(2,1)}), bf16[8,6,80,128]{3,2,1,0:T(8,128)(2,1)}, u32[]{:S(2)}, u32[]{:S(2)}) async-start(bf16[8,6,80,128]{3,2,1,0:T(8,128)(2,1)} %broadcast_in_dim.64), calls=%async_computation.3 | async-start | bytes 1966080 | tf_op jit(solution)/shard_map/all_to_all | solution.py:111
  87.9 1.2 slice_bitcast_fusion
  89.1 1.7 collective-permute-start.2
  90.8 1.8 collective-permute-start.1
  92.6 1.3 collective-permute-start
  93.9 17.0 %all-to-all-done.3 = bf16[8,6,80,128]{3,2,1,0:T(8,128)(2,1)} async-done(((bf16[8,6,80,128]{3,2,1,0:T(8,128)(2,1)}), bf16[8,6,80,128]{3,2,1,0:T(8,128)(2,1)}, u32[]{:S(2)}, u32[]{:S(2)}) %all-to-all-start.3) | async-done | bytes 983072 | tf_op jit(solution)/shard_map/all_to_all | solution.py:111
  110.8 1.0 slice.466
  111.9 1.3 broadcast_in_dim.65
  113.1 4.3 %all-to-all-start.4 = ((bf16[4,8,2,80,128]{4,3,1,2,0:T(8,128)(2,1)}), bf16[4,8,2,80,128]{4,3,1,2,0:T(8,128)(2,1)}, u32[]{:S(2)}, u32[]{:S(2)}) async-start(bf16[4,8,2,80,128]{4,3,1,2,0:T(8,128)(2,1)} %broadcast_in_dim.65), calls=%async_computation.4 | async-start | bytes 2621440 | tf_op jit(solution)/shard_map/all_to_all | solution.py:111
  117.5 32.3 %collective-permute-done = bf16[2,640,512]{2,1,0:T(8,128)(2,1)} collective-permute-done((bf16[2,640,512]{2,1,0:T(8,128)(2,1)}, bf16[2,640,512]{2,1,0:T(8,128)(2,1)}, u32[]{:S(2)}, u32[]{:S(2)}) %collective-permute-start) | collective-permute-done | bytes 1310752 | tf_op jit(solution)/shard_map/ppermute | solution.py:60
  149.8 3.4 %add_select_fusion = bf16[2,640,512]{2,1,0:T(8,128)(2,1)} fusion(bf16[2,640,512]{2,1,0:T(8,128)(2,1)} %collective-permute-done.2, bf16[2,640,512]{2,1,0:T(8,128)(2,1)} %collective-permute-done, bf16[2,640,512]{2,1,0:T(8,128)(2,1)} %collective-permute-done.1, pred[]{:T(512)S(6)} %eq.126, bf16[2,2,640,512]{3,2,0,1:T(8,128)(2,1)S(1)} %pad_maximum_fusion.2), kind=kLoop, calls=%fused_computation.74 | loop fusion | flops 1966080 | bytes 6553601 | tf_op jit(solution)/shard_map/jit(_where)/select_n | solution.py:61
  153.2 1.1 slice.470
  154.4 2.0 broadcast_in_dim.66
  156.4 3.9 %all-to-all-start.5 = ((bf16[4,8,4,80,128]{4,3,1,2,0:T(8,128)(2,1)}), bf16[4,8,4,80,128]{4,3,1,2,0:T(8,128)(2,1)S(1)}, u32[]{:S(2)}, u32[]{:S(2)}) async-start(bf16[4,8,4,80,128]{4,3,1,2,0:T(8,128)(2,1)} %broadcast_in_dim.66), calls=%async_computation.5 | async-start | bytes 5242880 | tf_op jit(solution)/shard_map/all_to_all | solution.py:111
  168.9 2.7 %copy.72 = bf16[4,2,80,8,128]{4,3,0,2,1:T(8,128)(2,1)} copy(bf16[4,2,80,8,128]{4,3,2,1,0:T(8,128)(2,1)} %bitcast.109) | data formatting | bytes 2621440 | tf_op jit(solution)/shard_map/reshape | solution.py:36
  172.0 3.0 %broadcast_select_fusion.1 = (bf16[2,640,512]{2,1,0:T(8,128)(2,1)S(1)}, bf16[2,640,512]{2,1,0:T(8,128)(2,1)}) fusion(bf16[2,640,512]{2,1,0:T(8,128)(2,1)} %collective-permute-done.3, bf16[2,640,512]{2,1,0:T(8,128)(2,1)} %add_select_fusion, pred[]{:T(512)S(6)} %eq.125), kind=kLoop, calls=%fused_computation.76 | loop fusion | flops 1310720 | bytes 5242881 | tf_op jit(solution)/shard_map/jit(_where)/select_n | solution.py:66
  175.0 1.4 fusion.79
  176.4 1.3 fusion.76
  177.7 15.3 %all-to-all-done.5 = bf16[4,8,4,80,128]{4,3,1,2,0:T(8,128)(2,1)S(1)} async-done(((bf16[4,8,4,80,128]{4,3,1,2,0:T(8,128)(2,1)}), bf16[4,8,4,80,128]{4,3,1,2,0:T(8,128)(2,1)S(1)}, u32[]{:S(2)}, u32[]{:S(2)}) %all-to-all-start.5) | async-done | bytes 2621472 | tf_op jit(solution)/shard_map/all_to_all | solution.py:111
  193.1 3.5 %copy.58 = bf16[4,640,4,128]{3,2,1,0:T(4,128)(2,1)} copy(bf16[4,640,4,128]{3,1,0,2:T(8,128)(2,1)S(1)} %bitcast.303) | data formatting | bytes 5242880 | tf_op jit(solution)/shard_map/transpose | solution.py:36
  196.6 3.9 %reshape_reshape.11 = bf16[2,2,640,512]{3,2,1,0:T(8,128)(2,1)S(1)} reshape(bf16[4,640,4,128]{3,2,1,0:T(4,128)(2,1)} %copy.58) | data formatting | bytes 5242880 | tf_op jit(solution)/shard_map/reshape;reshape | solution.py:123
  200.5 1.5 copy-done.6
  202.3 1.4 fusion.35
  203.8 1.9 broadcast_select_fusion
  206.0 2.1 fusion.75
  208.1 2.2 convolution_add_fusion.10
  210.3 1.9 fusion.94
  212.1 1.2 fusion.49
  213.3 1.3 fusion.77
  214.6 2.7 %fusion.26 = bf16[512,512]{1,0:T(8,128)(2,1)} fusion(f32[512,512]{1,0:T(8,128)S(1)} %convolution_add_fusion.10, f32[512,512]{1,0:T(8,128)S(1)} %fusion.94), kind=kOutput, calls=%fused_computation.80 | convolution fusion | flops 1611399168 | bytes 2621440 | tf_op jit(solution)/shard_map/dot_general | solution.py:24
  217.3 1.9 convolution_convert_fusion.3
  219.2 2.0 convert_subtract_fusion
  221.2 1.8 fusion.95
  223.1 2.2 convolution_add_fusion.8
  225.2 1.8 fusion.96
  227.1 2.7 %convolution_convert_fusion.1 = bf16[512,512]{1,0:T(8,128)(2,1)} fusion(bf16[512,512]{1,0:T(8,128)(2,1)} %fusion.26, bf16[2,640,512]{2,1,0:T(8,128)(2,1)} %get-tuple-element.106, f32[]{:T(128)S(6)} %select_n.265), kind=kOutput, calls=%fused_computation.82 | convolution fusion | flops 303824896 | bytes 1703940 | tf_op jit(solution)/shard_map/dot_general | solution.py:20
  229.8 2.7 %convolution_convert_fusion.4 = bf16[512,512]{1,0:T(8,128)(2,1)} fusion(bf16[512,512]{1,0:T(8,128)(2,1)} %fusion.26, bf16[2,640,512]{2,1,0:T(8,128)(2,1)} %get-tuple-element.106, f32[]{:T(128)S(6)} %select_n.234), kind=kOutput, calls=%fused_computation.85 | convolution fusion | flops 303824896 | bytes 1703940 | tf_op jit(solution)/shard_map/dot_general | solution.py:20
  232.4 2.5 convolution_select_fusion.9
  235.0 1.5 convolution_select_fusion.6
  236.5 1.4 convolution_select_fusion.4
  237.9 1.5 convolution_select_fusion.1
  239.5 1.4 convolution_select_fusion.11
  240.9 1.4 convolution_select_fusion.7
  242.3 2.7 %fusion.25 = bf16[512,512]{1,0:T(8,128)(2,1)} fusion(f32[512,512]{1,0:T(8,128)S(1)} %convolution_add_fusion.8, f32[512,512]{1,0:T(8,128)S(1)} %fusion.96), kind=kOutput, calls=%fused_computation.79 | convolution fusion | flops 1611399168 | bytes 2621440 | tf_op jit(solution)/shard_map/dot_general | solution.py:24
  245.0 2.7 %convolution_convert_fusion.2 = bf16[512,512]{1,0:T(8,128)(2,1)S(1)} fusion(bf16[512,512]{1,0:T(8,128)(2,1)} %fusion.25, bf16[512,512]{1,0:T(8,128)(2,1)} %convolution_convert_fusion.4, bf16[512,512]{1,0:T(8,128)(2,1)} %fusion.49, f32[512,512]{1,0:T(8,128)} %fusion.79, bf16[2,640,512]{2,1,0:T(8,128)(2,1)} %copy-done.14, f32[]{:T(128)S(6)} %select_n.246, ...), kind=kOutput, calls=%fused_computation.83 | convolution fusion | flops 539230208 | bytes 3670021 | tf_op jit(solution)/shard_map/dot_general | solution.py:20
  247.7 1.9 convolution_convert_fusion
  249.6 1.9 fusion.33
  251.5 1.5 fusion.31
  260.1 1.6 pad_maximum_fusion.3
  (75 shorter events, 15.8 us)
Async XLA Ops:
  10.1 1.9 copy-start.7
  12.0 1.3 copy-start
  24.7 45.4 %all-to-all-start = ((bf16[32,2,80,128]{3,2,1,0:T(8,128)(2,1)}), bf16[32,2,80,128]{3,2,1,0:T(8,128)(2,1)}, u32[]{:S(2)}, u32[]{:S(2)}) async-start(bf16[32,2,80,128]{3,2,1,0:T(8,128)(2,1)} %copy.41), calls=%async_computation | async-start | bytes 2621440 | tf_op jit(solution)/shard_map/cond/branch_0_fun/all_to_all | solution.py:91
  73.8 2.6 %collective-permute-start.5 = (bf16[2,80,128]{2,1,0:T(8,128)(2,1)S(1)}, bf16[2,80,128]{2,1,0:T(8,128)(2,1)S(1)}, u32[]{:S(2)}, u32[]{:S(2)}) collective-permute-start(bf16[2,80,128]{2,1,0:T(8,128)(2,1)S(1)} %bitcast.316), channel_id=1, source_target_pairs={{0,6},{1,7},{8,14},{9,15},{16,22},{17,23},{24,30},{25,31},{32,38},... | collective-permute-start | bytes 122888 | tf_op jit(solution)/shard_map/ppermute | solution.py:60
  74.4 7.8 %collective-permute-start.4 = (bf16[2,80,128]{2,1,0:T(8,128)(2,1)S(1)}, bf16[2,80,128]{2,1,0:T(8,128)(2,1)S(1)}, u32[]{:S(2)}, u32[]{:S(2)}) collective-permute-start(bf16[2,80,128]{2,1,0:T(8,128)(2,1)S(1)} %bitcast.317), channel_id=1, source_target_pairs={{0,2},{1,3},{8,10},{9,11},{16,18},{17,19},{24,26},{25,27},{32,34},... | collective-permute-start | bytes 122888 | tf_op jit(solution)/shard_map/ppermute | solution.py:60
  75.7 6.5 %collective-permute-start.6 = (bf16[2,80,128]{2,1,0:T(8,128)(2,1)S(1)}, bf16[2,80,128]{2,1,0:T(8,128)(2,1)S(1)}, u32[]{:S(2)}, u32[]{:S(2)}) collective-permute-start(bf16[2,80,128]{2,1,0:T(8,128)(2,1)S(1)} %bitcast.318), channel_id=1, source_target_pairs={{0,4},{1,5},{8,12},{9,13},{16,20},{17,21},{24,28},{25,29},{32,36},... | collective-permute-start | bytes 122888 | tf_op jit(solution)/shard_map/ppermute | solution.py:60
  83.3 27.5 %all-to-all-start.3 = ((bf16[8,6,80,128]{3,2,1,0:T(8,128)(2,1)}), bf16[8,6,80,128]{3,2,1,0:T(8,128)(2,1)}, u32[]{:S(2)}, u32[]{:S(2)}) async-start(bf16[8,6,80,128]{3,2,1,0:T(8,128)(2,1)} %broadcast_in_dim.64), calls=%async_computation.3 | async-start | bytes 1966080 | tf_op jit(solution)/shard_map/all_to_all | solution.py:111
  89.1 28.3 %collective-permute-start.2 = (bf16[2,640,512]{2,1,0:T(8,128)(2,1)}, bf16[2,640,512]{2,1,0:T(8,128)(2,1)}, u32[]{:S(2)}, u32[]{:S(2)}) collective-permute-start(bf16[2,640,512]{2,1,0:T(8,128)(2,1)} %slice_bitcast_fusion), channel_id=1, source_target_pairs={{0,4},{1,5},{8,12},{9,13},{16,20},{17,21},{24,28},{25,29},{32,36},... | collective-permute-start | bytes 3932168 | tf_op jit(solution)/shard_map/ppermute | solution.py:60
  90.8 26.6 %collective-permute-start.1 = (bf16[2,640,512]{2,1,0:T(8,128)(2,1)}, bf16[2,640,512]{2,1,0:T(8,128)(2,1)}, u32[]{:S(2)}, u32[]{:S(2)}) collective-permute-start(bf16[2,640,512]{2,1,0:T(8,128)(2,1)} %slice_bitcast_fusion), channel_id=1, source_target_pairs={{0,6},{1,7},{8,14},{9,15},{16,22},{17,23},{24,30},{25,31},{32,38},... | collective-permute-start | bytes 3932168 | tf_op jit(solution)/shard_map/ppermute | solution.py:60
  92.6 57.2 %collective-permute-start = (bf16[2,640,512]{2,1,0:T(8,128)(2,1)}, bf16[2,640,512]{2,1,0:T(8,128)(2,1)}, u32[]{:S(2)}, u32[]{:S(2)}) collective-permute-start(bf16[2,640,512]{2,1,0:T(8,128)(2,1)} %slice_bitcast_fusion), channel_id=1, source_target_pairs={{0,2},{1,3},{8,10},{9,11},{16,18},{17,19},{24,26},{25,27},{32,34},... | collective-permute-start | bytes 3932168 | tf_op jit(solution)/shard_map/ppermute | solution.py:60
  113.1 41.3 %all-to-all-start.4 = ((bf16[4,8,2,80,128]{4,3,1,2,0:T(8,128)(2,1)}), bf16[4,8,2,80,128]{4,3,1,2,0:T(8,128)(2,1)}, u32[]{:S(2)}, u32[]{:S(2)}) async-start(bf16[4,8,2,80,128]{4,3,1,2,0:T(8,128)(2,1)} %broadcast_in_dim.65), calls=%async_computation.4 | async-start | bytes 2621440 | tf_op jit(solution)/shard_map/all_to_all | solution.py:111
  153.2 18.8 %collective-permute-start.3 = (bf16[2,640,512]{2,1,0:T(8,128)(2,1)}, bf16[2,640,512]{2,1,0:T(8,128)(2,1)}, u32[]{:S(2)}, u32[]{:S(2)}) collective-permute-start(bf16[2,640,512]{2,1,0:T(8,128)(2,1)} %add_select_fusion), channel_id=1, source_target_pairs={{0,1},{1,0},{2,3},{3,2},{4,5},{5,4},{6,7},{7,6},{8,9},{9,8},{10,11... | collective-permute-start | bytes 3932168 | tf_op jit(solution)/shard_map/ppermute | solution.py:65
  156.4 3.9 %copy-start.19 = (s32[64]{0:T(128)S(1)}, s32[64]{0:T(128)}, u32[]{:S(2)}) copy-start(s32[64]{0:T(128)} %param.13) | copy-start | bytes 772
  156.4 36.7 %all-to-all-start.5 = ((bf16[4,8,4,80,128]{4,3,1,2,0:T(8,128)(2,1)}), bf16[4,8,4,80,128]{4,3,1,2,0:T(8,128)(2,1)S(1)}, u32[]{:S(2)}, u32[]{:S(2)}) async-start(bf16[4,8,4,80,128]{4,3,1,2,0:T(8,128)(2,1)} %broadcast_in_dim.66), calls=%async_computation.5 | async-start | bytes 5242880 | tf_op jit(solution)/shard_map/all_to_all | solution.py:111
  171.6 32.1 %collective-permute-start.7 = (bf16[2,640,512]{2,1,0:T(8,128)(2,1)}, bf16[2,640,512]{2,1,0:T(8,128)(2,1)}, u32[]{:S(2)}, u32[]{:S(2)}) collective-permute-start(bf16[2,640,512]{2,1,0:T(8,128)(2,1)} %bitcast.301), channel_id=1, source_target_pairs={{0,1},{1,0},{2,3},{3,2},{4,5},{5,4},{6,7},{7,6},{8,9},{9,8},{10,11... | collective-permute-start | bytes 3932168 | tf_op jit(solution)/shard_map/ppermute | solution.py:65
  175.0 1.4 copy-start.14
  200.5 1.5 copy-start.6
  205.7 2.4 copy-start.15
  219.1 2.1 copy-start.12
  232.4 2.5 copy-start.13
  235.0 1.5 copy-start.9
  237.9 1.5 copy-start.11
  245.0 2.7 %copy-start.10 = (bf16[512,512]{1,0:T(8,128)(2,1)S(1)}, bf16[512,512]{1,0:T(8,128)(2,1)}, u32[]{:S(2)}) copy-start(bf16[512,512]{1,0:T(8,128)(2,1)} %convolution_convert_fusion.1) | copy-start | bytes 1572868
  245.0 2.7 %copy-start.17 = (f32[512,512]{1,0:T(8,128)S(1)}, f32[512,512]{1,0:T(8,128)}, u32[]{:S(2)}) copy-start(f32[512,512]{1,0:T(8,128)} %fusion.76) | copy-start | bytes 3145732
  245.0 2.7 %copy-start.18 = (bf16[512,512]{1,0:T(8,128)(2,1)S(1)}, bf16[512,512]{1,0:T(8,128)(2,1)}, u32[]{:S(2)}) copy-start(bf16[512,512]{1,0:T(8,128)(2,1)} %fusion.25) | copy-start | bytes 1572868
  249.6 1.9 copy-start.16
  253.9 1.2 copy-start.4
  253.9 1.3 copy-start.8
  254.3 1.7 copy-start.1
  256.0 1.2 copy-start.5
  257.2 1.2 copy-start.3
  258.5 1.2 copy-start.2

commit v2 on v1

v2 whole, which is shorter than its diff:
```python
import functools
import math

import jax
import jax.numpy as jnp
from jax import lax
from jax.experimental import pallas as pl
from jax.experimental.pallas import tpu as pltpu
from jax.sharding import PartitionSpec as P

TILE = 512
KMAX = 64
LANES = 128
WIDE = TILE + LANES
BLOCKS = TILE // LANES
CHUNK = 16
PARTS = TILE // CHUNK
SHIFT = 1.1 * math.sqrt(TILE)
NY, NZ, NX = 4, 8, 4
BF = jnp.bfloat16
F32 = jnp.float32

SMEM = pl.BlockSpec(memory_space=pltpu.SMEM)
VMEM = pl.BlockSpec(memory_space=pltpu.VMEM)
PARAMS = pltpu.CompilerParams(vmem_limit_bytes=40 << 20)


def dot(a, b):
    return jnp.dot(a, b, preferred_element_type=F32)


def split(a):
    high = a.astype(BF)
    return high, (a - high.astype(F32)).astype(BF)


def dot_hi(a, b):
    return dot(a[0], b[0]) + (dot(a[0], b[1]) + dot(a[1], b[0]))


def eye():
    rows = lax.broadcasted_iota(jnp.int32, (TILE, TILE), 0)
    cols = lax.broadcasted_iota(jnp.int32, (TILE, TILE), 1)
    return (rows == cols).astype(F32)


def low_rank(left, right):
    return lax.dot_general(left, right, (((0,), (0,)), ((), ())), preferred_element_type=F32)


def build(wide, diag):
    factors = wide[:, TILE:].reshape(BLOCKS, 2, KMAX, LANES)
    left = jnp.concatenate([factors[k, 0] for k in range(BLOCKS)], axis=1)
    right = jnp.concatenate([factors[k, 1] for k in range(BLOCKS)], axis=1)
    tile = wide[:, :TILE].astype(F32) + low_rank(left, right)
    return tile + jnp.where(diag, SHIFT, 0.0) * eye()


def inverse(pivot):
    ident = eye()
    e = ident - pivot * (1.0 / SHIFT)
    es = split(e)
    e2 = dot_hi(es, es)
    e2s = split(e2)
    total = split(ident + e + e2 + dot_hi(es, e2s))
    e4 = dot_hi(e2s, e2s)
    whole = total[0].astype(F32) + total[1].astype(F32) + dot_hi(total, split(e4))
    return (whole * (1.0 / SHIFT)).astype(BF)


def kept_left(u, rank):
    rows = lax.broadcasted_iota(jnp.int32, (KMAX, TILE), 0)
    return jnp.where(rows < rank, u.astype(F32), 0.0).astype(BF)


def wide_tile(near, u, v, mask, rank):
    near = near * mask.astype(F32).astype(BF)
    left = kept_left(u, rank)
    factors = []
    for k in range(BLOCKS):
        cut = slice(k * LANES, (k + 1) * LANES)
        factors += [left[:, cut], v[:, cut]]
    return near, jnp.concatenate(factors, axis=0)


def head_kernel(slot, mask, ranks, near, u, v, cols, send):
    for s in range(2):
        near_part, factors = wide_tile(near[s, 0], u[s, 0], v[s, 0], mask[s, 0], ranks[s, 0])
        cols[s, :, :TILE] = near_part
        cols[s, :, TILE:] = factors
    s = slot[0]
    for t in range(2):
        near_part, factors = wide_tile(near[s, t], u[s, t], v[s, t], mask[s, t], ranks[s, t])
        send[:, t, :, :TILE] = near_part.reshape(PARTS, CHUNK, TILE)
        send[:, t, :, TILE:] = factors.reshape(PARTS, CHUNK, LANES)


def head(slot, mask, ranks, near, u, v):
    return pl.pallas_call(
        head_kernel,
        out_shape=(
            jax.ShapeDtypeStruct((2, TILE, WIDE), BF),
            jax.ShapeDtypeStruct((PARTS, 2, CHUNK, WIDE), BF),
        ),
        in_specs=[SMEM] * 3 + [VMEM] * 3,
        out_specs=(VMEM, VMEM),
        compiler_params=PARAMS,
        name="head",
    )(slot.reshape(1), mask, ranks, near, u, v)


def chain_kernel(place, held, own, other, cols_own, cols_other, out, piv, cols):
    core = place[0]
    piv[core] = own[...]
    piv[1 - core] = other[...]
    cols[core] = cols_own[...]
    cols[1 - core] = cols_other[...]

    def pivot(j, k):
        return build(piv[j, :, :, k].reshape(TILE, WIDE), j == k)

    inv0 = inverse(pivot(0, 0))
    row1 = pivot(1, 0).astype(BF)
    mult_p1 = dot(pivot(0, 1).astype(BF), inv0).astype(BF)
    inv1 = inverse(pivot(1, 1) - dot(mult_p1, row1))
    out[0] = mult_p1
    for s in range(2):
        first = dot(build(cols[0, s], held[s] == 0).astype(BF), inv0).astype(BF)
        second = build(cols[1, s], held[s] == 1)
        second = second - jnp.where(held[s] > 0, 1.0, 0.0) * dot(first, row1)
        out[1 + 2 * s] = first
        out[2 + 2 * s] = dot(second.astype(BF), inv1).astype(BF)


def chain(place, held, own, other, cols_own, cols_other):
    return pl.pallas_call(
        chain_kernel,
        out_shape=jax.ShapeDtypeStruct((5, TILE, TILE), BF),
        in_specs=[SMEM] * 2 + [VMEM] * 4,
        out_specs=VMEM,
        scratch_shapes=[
            pltpu.VMEM((2, NY, NZ, 2, CHUNK, WIDE), BF),
            pltpu.VMEM((2, 2, TILE, WIDE), BF),
        ],
        compiler_params=PARAMS,
        cost_estimate=pl.CostEstimate(
            flops=38 * 2 * TILE**3, bytes_accessed=8 << 20, transcendentals=0
        ),
        name="chain",
    )(place, held, own, other, cols_own, cols_other)


def last_kernel(place, held, mask, ranks, near, u, v, rows, mult, out):
    col = place[1]
    for t in range(2):
        j = t * 2 * NX + col
        row0 = build(rows[:, :, t].reshape(TILE, WIDE), j == 0).astype(BF)
        row1 = build(rows[:, :, 2 + t].reshape(TILE, WIDE), j == 1)
        row1 = (row1 - jnp.where(j > 0, 1.0, 0.0) * dot(mult[0], row0)).astype(BF)
        for s in range(2):
            tile = near[s, t].astype(F32) * mask[s, t].astype(F32)
            tile = tile + low_rank(kept_left(u[s, t], ranks[s, t]), v[s, t])
            tile = tile + jnp.where(held[s] == j, SHIFT, 0.0) * eye()
            for k, row in enumerate((row0, row1)):
                live = jnp.where((held[s] > k) & (j > k), 1.0, 0.0)
                tile = tile - live * dot(mult[1 + 2 * s + k], row)
            out[s, t] = tile.astype(BF)


def last(place, held, mask, ranks, near, u, v, rows, mult):
    return pl.pallas_call(
        last_kernel,
        out_shape=jax.ShapeDtypeStruct((2, 2, TILE, TILE), BF),
        in_specs=[SMEM] * 4 + [VMEM] * 5,
        out_specs=VMEM,
        compiler_params=PARAMS,
        cost_estimate=pl.CostEstimate(
            flops=16 * 2 * TILE**3, bytes_accessed=10 << 20, transcendentals=0
        ),
        name="last",
    )(place, held, mask, ranks, near, u, v, rows, mult)


def pairs(source, target):
    return [(source * 2 + core, target * 2 + core) for core in range(2)]


def body(near_tiles, basis_u, basis_v, near_mask, ranks, row_map):
    row = lax.axis_index("row")
    col = lax.axis_index("col")
    x, core = col // 2, col % 2
    place = jnp.stack([core, col])
    near = near_tiles.reshape(2, 2, TILE, TILE)
    u = basis_u.reshape(2, 2, KMAX, TILE)
    v = basis_v.reshape(2, 2, KMAX, TILE)
    mask = near_mask.reshape(2, 2)
    ranks = ranks.reshape(2, 2)
    slots = jnp.arange(64, dtype=jnp.int32)
    owner = [jnp.sum(jnp.where(row_map == k, slots, 0)) for k in range(2)]
    owner_row = [o // 2 for o in owner]
    held = lax.dynamic_slice_in_dim(row_map, row * 2, 2)

    slot = jnp.where(row == owner_row[0], owner[0], owner[1]) % 2
    cols, send = head(slot, mask, ranks, near, u, v)

    def first_hop(cols):
        return [lax.ppermute(cols, "col", pairs(0, to)) for to in (1, 3)]

    def take(got, k):
        return lax.dynamic_index_in_dim(got, owner_row[k], 0, keepdims=False)

    def apart():
        hop = first_hop(cols)
        again = head(owner[1] % 2, mask, ranks, near, u, v)[1]
        got = [lax.all_to_all(part, "row", 0, 0) for part in (send, again)]
        return jnp.stack([take(got[k], k) for k in range(2)]), hop

    def merged():
        hop = first_hop(cols)
        got = lax.all_to_all(send, "row", 0, 0)
        return jnp.stack([take(got, k) for k in range(2)]), hop

    chunk, hop = lax.cond(owner_row[0] == owner_row[1], apart, merged)

    pivots = chunk[:, 0]
    parts = [lax.ppermute(pivots, "col", pairs(0, to)) for to in (1, 3, 2)]
    pivots = jnp.where(x == 0, pivots, parts[0] + parts[1] + parts[2])

    cols = jnp.where(x == 0, cols, hop[0] + hop[1])
    hop = [lax.ppermute(cols[s], "col", pairs(source, 2)) for s, source in enumerate((1, 3))]
    cols = jnp.where(x == 2, jnp.stack(hop), cols)
    swap = [(c, c ^ 1) for c in range(2 * NX)]
    cols_other = lax.ppermute(cols, "col", swap)

    z_groups = [[y * NZ + z for z in range(NZ)] for y in range(NY)]
    y_groups = [[y * NZ + z for y in range(NY)] for z in range(NZ)]

    def gather(value, count, groups):
        return lax.all_to_all(
            jnp.broadcast_to(value[None], (count, *value.shape)), "row", 0, 0, axis_index_groups=groups
        )

    bundle = jnp.concatenate([pivots, chunk.reshape(4, CHUNK, WIDE)])
    line = gather(bundle, NZ, z_groups)
    piv = gather(line[:, :2], NY, y_groups)
    rows = gather(line[:, 2:], NY, y_groups)
    piv_other = lax.ppermute(piv, "col", swap)
    mult = chain(place, held, piv, piv_other, cols, cols_other)
    out = last(place, held, mask, ranks, near, u, v, rows, mult)
    return out.reshape(2, 2, 1, TILE, TILE)


def solution(mesh):
    return jax.shard_map(
        body,
        mesh=mesh,
        in_specs=(
            P("row", None, "col", None, None),
            P("row", None, "col", None, None),
            P("row", None, "col", None, None),
            P("row", None, "col"),
            P("row", None, "col"),
            P(),
        ),
        out_specs=P("row", None, "col", None, None),
        check_vma=False,
    )
```

time: 263 us -> 172 us (0.65)
  the two profiles are of different devices: /device:TPU:34 before, /device:TPU:12 now
where the time goes in v2:
time: 172 us; the launch traced here: 170 us
  waiting for transfers between devices  86 us (50%)
  starting transfers between devices  36 us (21%)
  Pallas kernels  24.4 us (14%)
  local copies, waits for them, and re-layouts  10.2 us (6%)
  other arithmetic  7.18 us (4%)
  between operations  6.54 us (4%)
    all_to_all x3, waiting for transfers between devices, gather(): lax.all_to_all(jnp.broadcast_to(value[None], (count, *value.shape)), 'row...  38.7 us
    all_to_all x1, waiting for transfers between devices, merged(): got = lax.all_to_all(send, 'row', 0, 0)  28.1 us
    all_to_all x3, starting transfers between devices, gather(): lax.all_to_all(jnp.broadcast_to(value[None], (count, *value.shape)), 'row...  15.1 us
    ppermute x2, waiting for transfers between devices, body(): lax.ppermute(cols[s], 'col', pairs(source, 2))  14.4 us
    pallas_call x1, Pallas kernels, chain(): pl.pallas_call(chain_kernel, out_shape=jax.ShapeDtypeStruct((5, TILE, TIL...  13.7 us
    all_to_all x1, starting transfers between devices, merged(): got = lax.all_to_all(send, 'row', 0, 0)  11.7 us
    pallas_call x1, Pallas kernels, last(): pl.pallas_call(last_kernel, out_shape=jax.ShapeDtypeStruct((2, 2, TILE, T...  7.3 us
    ppermute x3, waiting for transfers between devices, body(): parts = [lax.ppermute(pivots, 'col', pairs(0, to)) for to in (1, 3, 2)]  4.74 us
  transfers between devices with their start and end apart: 13, of which 6 were waited for; matrix products, arithmetic and copies ran while one was open for 6% of the time, Pallas kernels for 8%

profile of v2, /device:TPU:12, one launch (start us, length us, event | category | flops | bytes accessed | tf_op | source)
XLA Modules:
  0.0 170.3 jit_solution(5361071501552170414)
XLA Ops:
  0.0 1.3 fusion.3
  7.7 0.0 copy-start.2
  7.7 0.0 copy-start.5
  7.8 0.0 copy-start.6
  7.8 3.5 %head.3 = (bf16[2,512,640]{2,1,0:T(8,128)(2,1)}, bf16[32,2,16,640]{3,2,1,0:T(8,128)(2,1)}) custom-call(s32[1]{0:T(128)} %bitcast.10.slot, s32[2,2]{1,0:T(2,128)} %bitcast.31, s32[2,2]{1,0:T(2,128)} %bitcast.34, bf16[2,2,512,512]{3,2,1,0:T(8,128)(2,1)} %bitcast.21, bf16[2,2,64,512]{3,2,1,0:T(8,128)(2,1)} %bitcast.24, bf16[2,2,64,512]{3,2,1,0:T(8,128)(2,1)} %bitcast.27), custom_call_target="tpu_custom_call" | custom-call | tf_op jit(solution)/shard_map/head/pallas_call | solution.py:99
  11.2 0.0 copy-done.2
  11.2 0.0 copy-done.5
  11.2 0.0 copy-done.6
  11.3 46.3 %conditional.1 = (bf16[2,2,16,640]{3,2,1,0:T(8,128)(2,1)}, bf16[2,2,16,640]{3,2,1,0:T(8,128)(2,1)S(1)}, bf16[2,512,640]{2,1,0:T(8,128)(2,1)}, bf16[2,512,640]{2,...) conditional(s32[]{:T(128)} %convert_element_type.3, ...), branch_computations={%region_2.3_spmd, %region_3.4_spmd} | conditional | flops 61457 | bytes 19046776 | solution.py:223
  11.3 11.7 %all-to-all-start = ((bf16[32,2,16,640]{3,2,1,0:T(8,128)(2,1)}), bf16[32,2,16,640]{3,2,1,0:T(8,128)(2,1)S(1)}, u32[]{:S(2)}, u32[]{:S(2)}) async-start(bf16[32,2,16,640]{3,2,1,0:T(8,128)(2,1)} %get-tuple-element.43), calls=%async_computation | async-start | bytes 2621440 | tf_op jit(solution)/shard_map/cond/branch_0_fun/all_to_all | solution.py:220
  23.0 1.8 %collective-permute-start.1 = (bf16[2,512,640]{2,1,0:T(8,128)(2,1)}, bf16[2,512,640]{2,1,0:T(8,128)(2,1)}, u32[]{:S(2)}, u32[]{:S(2)}) collective-permute-start(bf16[2,512,640]{2,1,0:T(8,128)(2,1)} %get-tuple-element.46), channel_id=1, source_target_pairs={{0,6},{1,7},{8,14},{9,15},{16,22},{17,23},{24,30},{25,31},{32,38},... | collective-permute-start | bytes 3932168 | tf_op jit(solution)/shard_map/cond/branch_0_fun/ppermute | solution.py:207
  24.8 1.7 %collective-permute-start = (bf16[2,512,640]{2,1,0:T(8,128)(2,1)}, bf16[2,512,640]{2,1,0:T(8,128)(2,1)}, u32[]{:S(2)}, u32[]{:S(2)}) collective-permute-start(bf16[2,512,640]{2,1,0:T(8,128)(2,1)} %get-tuple-element.46), channel_id=1, source_target_pairs={{0,2},{1,3},{8,10},{9,11},{16,18},{17,19},{24,26},{25,27},{32,34},... | collective-permute-start | bytes 3932168 | tf_op jit(solution)/shard_map/cond/branch_0_fun/ppermute | solution.py:207
  26.5 28.1 %all-to-all-done = bf16[32,2,16,640]{3,2,1,0:T(8,128)(2,1)S(1)} async-done(((bf16[32,2,16,640]{3,2,1,0:T(8,128)(2,1)}), bf16[32,2,16,640]{3,2,1,0:T(8,128)(2,1)S(1)}, u32[]{:S(2)}, u32[]{:S(2)}) %all-to-all-start) | async-done | bytes 1310752 | tf_op jit(solution)/shard_map/cond/branch_0_fun/all_to_all | solution.py:220
  54.6 0.6 fusion
  55.2 0.8 copy.13
  56.0 0.6 pad_maximum_fusion
  56.6 0.0 collective-permute-done.1
  56.6 0.0 collective-permute-done
  56.6 0.9 copy.22
  57.5 1.3 collective-permute-start.6
  58.8 0.7 collective-permute-start.5
  59.5 0.7 collective-permute-start.4
  60.2 4.7 %collective-permute-done.6 = bf16[2,16,640]{2,1,0:T(8,128)(2,1)S(1)} collective-permute-done((bf16[2,16,640]{2,1,0:T(8,128)(2,1)S(1)}, bf16[2,16,640]{2,1,0:T(8,128)(2,1)S(1)}, u32[]{:S(2)}, u32[]{:S(2)}) %collective-permute-start.6) | collective-permute-done | bytes 40992 | tf_op jit(solution)/shard_map/ppermute | solution.py:226
  64.9 0.0 collective-permute-done.5
  64.9 0.0 collective-permute-done.4
  65.0 1.0 broadcast_in_dim.9
  66.0 5.2 %all-to-all-start.3 = ((bf16[8,6,16,640]{3,2,1,0:T(8,128)(2,1)}), bf16[8,6,16,640]{3,2,1,0:T(8,128)(2,1)S(1)}, u32[]{:S(2)}, u32[]{:S(2)}) async-start(bf16[8,6,16,640]{3,2,1,0:T(8,128)(2,1)} %broadcast_in_dim.9), calls=%async_computation.3 | async-start | bytes 1966080 | tf_op jit(solution)/shard_map/all_to_all | solution.py:239
  71.2 1.9 %add_select_fusion = bf16[2,512,640]{2,1,0:T(8,128)(2,1)S(1)} fusion(bf16[2,512,640]{2,1,0:T(8,128)(2,1)} %get-tuple-element.65, bf16[2,512,640]{2,1,0:T(8,128)(2,1)} %get-tuple-element.72, bf16[2,512,640]{2,1,0:T(8,128)(2,1)} %get-tuple-element.73, pred[]{:T(512)S(6)} %eq.29), kind=kLoop, calls=%fused_computation.13 | loop fusion | flops 1310720 | bytes 5242881 | tf_op jit(solution)/shard_map/jit(_where)/select_n | solution.py:229
  73.1 23.5 %all-to-all-done.3 = bf16[8,6,16,640]{3,2,1,0:T(8,128)(2,1)S(1)} async-done(((bf16[8,6,16,640]{3,2,1,0:T(8,128)(2,1)}), bf16[8,6,16,640]{3,2,1,0:T(8,128)(2,1)S(1)}, u32[]{:S(2)}, u32[]{:S(2)}) %all-to-all-start.3) | async-done | bytes 983072 | tf_op jit(solution)/shard_map/all_to_all | solution.py:239
  96.6 1.2 broadcast_in_dim.11
  97.8 4.9 %all-to-all-start.5 = ((bf16[4,8,2,16,640]{4,3,2,1,0:T(8,128)(2,1)}), bf16[4,8,2,16,640]{4,3,2,1,0:T(8,128)(2,1)}, u32[]{:S(2)}, u32[]{:S(2)}) async-start(bf16[4,8,2,16,640]{4,3,2,1,0:T(8,128)(2,1)} %broadcast_in_dim.11), calls=%async_computation.5 | async-start | bytes 2621440 | tf_op jit(solution)/shard_map/all_to_all | solution.py:239
  102.7 1.0 slice_bitcast_fusion.1
  103.6 1.3 collective-permute-start.8
  104.9 1.3 collective-permute-start.9
  106.2 13.7 %collective-permute-done.8 = bf16[512,640]{1,0:T(8,128)(2,1)} collective-permute-done((bf16[512,640]{1,0:T(8,128)(2,1)}, bf16[512,640]{1,0:T(8,128)(2,1)}, u32[]{:S(2)}, u32[]{:S(2)}) %collective-permute-start.8) | collective-permute-done | bytes 655392 | tf_op jit(solution)/shard_map/ppermute | solution.py:230
  119.9 0.7 collective-permute-done.9
  120.6 2.6 %maximum_select_fusion.cols_own = bf16[2,512,640]{2,1,0:T(8,128)(2,1)} fusion(bf16[2,512,640]{2,1,0:T(8,128)(2,1)S(1)} %add_select_fusion, bf16[1,512,640]{2,1,0:T(8,128)(2,1)} %bitcast.15, bf16[1,512,640]{2,1,0:T(8,128)(2,1)} %bitcast.13, pred[]{:T(512)S(6)} %eq.36), kind=kLoop, calls=%fused_computation.12 | loop fusion | flops 1310720 | bytes 3932161 | tf_op jit(solution)/shard_map/jit(_where)/select_n | solution.py:231
  123.2 0.0 collective-permute-start.10
  123.2 0.0 all-to-all-done.5.own
  123.2 0.5 collective-permute-start.7
  123.7 0.1 slice.27
  123.8 1.9 %broadcast_in_dim.10 = bf16[4,8,4,16,640]{4,3,2,1,0:T(8,128)(2,1)} broadcast(bf16[8,4,16,640]{3,2,1,0:T(8,128)(2,1)S(1)} %slice.27), dimensions={1,2,3,4} | broadcast | bytes 3276800 | tf_op jit(solution)/shard_map/broadcast_in_dim | solution.py:240
  125.6 0.0 copy-start.7
  125.6 5.0 %all-to-all-start.4 = ((bf16[4,8,4,16,640]{4,3,2,1,0:T(8,128)(2,1)}), bf16[4,8,4,16,640]{4,3,2,1,0:T(8,128)(2,1)S(1)}, u32[]{:S(2)}, u32[]{:S(2)}) async-start(bf16[4,8,4,16,640]{4,3,2,1,0:T(8,128)(2,1)} %broadcast_in_dim.10), calls=%async_computation.4 | async-start | bytes 5242880 | tf_op jit(solution)/shard_map/all_to_all | solution.py:239
  130.6 0.0 copy-done.7
  130.6 0.1 dynamic_slice.16.held
  130.7 0.1 pad_add_fusion.place
  130.8 0.0 copy-start.3
  130.8 0.0 copy-start.4
  130.8 0.0 collective-permute-done.10.cols_other
  130.8 0.0 collective-permute-done.7.other
  130.8 13.7 %chain.1.mult = bf16[5,512,512]{2,1,0:T(8,128)(2,1)S(1)} custom-call(s32[2]{0:T(128)S(1)} %pad_add_fusion.place, s32[2]{0:T(128)S(1)} %dynamic_slice.16.held, bf16[4,8,2,16,640]{4,3,2,1,0:T(8,128)(2,1)} %all-to-all-done.5.own, bf16[4,8,2,16,640]{4,3,2,1,0:T(8,128)(2,1)} %collective-permute-done.7.other, bf16[2,512,640]{2,1,0:T(8,128)(2,1)} %maximum_select_fusion.cols_own, ...), custom_call_target="tpu_custom_call" | custom-call | flops 10200547328 | bytes 8388608 | tf_op jit(solution)/shard_map/chain/pallas_call | solution.py:136
  144.5 0.0 copy-start
  144.5 1.5 copy-done
  146.0 15.3 %all-to-all-done.4.rows = bf16[4,8,4,16,640]{4,3,2,1,0:T(8,128)(2,1)S(1)} async-done(((bf16[4,8,4,16,640]{4,3,2,1,0:T(8,128)(2,1)}), bf16[4,8,4,16,640]{4,3,2,1,0:T(8,128)(2,1)S(1)}, u32[]{:S(2)}, u32[]{:S(2)}) %all-to-all-start.4) | async-done | bytes 2621472 | tf_op jit(solution)/shard_map/all_to_all | solution.py:239
  161.3 0.0 copy-done.3
  161.3 0.0 copy-done.4
  161.3 0.0 copy-start.1
  161.3 1.7 %copy-done.1 = bf16[5,512,512]{2,1,0:T(8,128)(2,1)S(1)} copy-done((bf16[5,512,512]{2,1,0:T(8,128)(2,1)S(1)}, bf16[5,512,512]{2,1,0:T(8,128)(2,1)}, u32[]{:S(2)}) %copy-start.1) | copy-done | bytes 2621464
  163.0 7.3 %last.1 = bf16[2,2,512,512]{3,2,1,0:T(8,128)(2,1)} custom-call(s32[2]{0:T(128)S(1)} %pad_add_fusion.place, s32[2]{0:T(128)S(1)} %dynamic_slice.16.held, s32[2,2]{1,0:T(2,128)S(1)} %bitcast.33, s32[2,2]{1,0:T(2,128)S(1)} %bitcast.36, bf16[2,2,512,512]{3,2,1,0:T(8,128)(2,1)} %bitcast.22, bf16[2,2,64,512]{3,2,1,0:T(8,128)(2,1)S(1)} %bitcast.26, ...), custom_call_target="tpu_custom_call" | custom-call | flops 4294967296 | bytes 10485760 | tf_op jit(solution)/shard_map/last/pallas_call | solution.py:171
  (4 shorter events, 0.1 us)
Async XLA Ops:
  7.7 3.5 %copy-start.2 = (bf16[2,2,1,512,512]{4,3,2,1,0:T(8,128)(2,1)S(1)}, bf16[2,2,1,512,512]{4,3,2,1,0:T(8,128)(2,1)}, u32[]{:S(2)}) copy-start(bf16[2,2,1,512,512]{4,3,2,1,0:T(8,128)(2,1)} %param.8) | copy-start | bytes 6291460
  7.7 3.5 %copy-start.5 = (s32[2,2,1]{1,2,0:T(1,128)S(1)}, s32[2,2,1]{1,2,0:T(1,128)}, u32[]{:S(2)}) copy-start(s32[2,2,1]{1,2,0:T(1,128)} %param.11) | copy-start | bytes 52
  7.8 3.5 %copy-start.6 = (s32[2,2,1]{1,2,0:T(1,128)S(1)}, s32[2,2,1]{1,2,0:T(1,128)}, u32[]{:S(2)}) copy-start(s32[2,2,1]{1,2,0:T(1,128)} %param.12) | copy-start | bytes 52
  11.3 43.3 %all-to-all-start = ((bf16[32,2,16,640]{3,2,1,0:T(8,128)(2,1)}), bf16[32,2,16,640]{3,2,1,0:T(8,128)(2,1)S(1)}, u32[]{:S(2)}, u32[]{:S(2)}) async-start(bf16[32,2,16,640]{3,2,1,0:T(8,128)(2,1)} %get-tuple-element.43), calls=%async_computation | async-start | bytes 2621440 | tf_op jit(solution)/shard_map/cond/branch_0_fun/all_to_all | solution.py:220
  23.0 33.6 %collective-permute-start.1 = (bf16[2,512,640]{2,1,0:T(8,128)(2,1)}, bf16[2,512,640]{2,1,0:T(8,128)(2,1)}, u32[]{:S(2)}, u32[]{:S(2)}) collective-permute-start(bf16[2,512,640]{2,1,0:T(8,128)(2,1)} %get-tuple-element.46), channel_id=1, source_target_pairs={{0,6},{1,7},{8,14},{9,15},{16,22},{17,23},{24,30},{25,31},{32,38},... | collective-permute-start | bytes 3932168 | tf_op jit(solution)/shard_map/cond/branch_0_fun/ppermute | solution.py:207
  24.8 31.9 %collective-permute-start = (bf16[2,512,640]{2,1,0:T(8,128)(2,1)}, bf16[2,512,640]{2,1,0:T(8,128)(2,1)}, u32[]{:S(2)}, u32[]{:S(2)}) collective-permute-start(bf16[2,512,640]{2,1,0:T(8,128)(2,1)} %get-tuple-element.46), channel_id=1, source_target_pairs={{0,2},{1,3},{8,10},{9,11},{16,18},{17,19},{24,26},{25,27},{32,34},... | collective-permute-start | bytes 3932168 | tf_op jit(solution)/shard_map/cond/branch_0_fun/ppermute | solution.py:207
  57.5 7.4 %collective-permute-start.6 = (bf16[2,16,640]{2,1,0:T(8,128)(2,1)S(1)}, bf16[2,16,640]{2,1,0:T(8,128)(2,1)S(1)}, u32[]{:S(2)}, u32[]{:S(2)}) collective-permute-start(bf16[2,16,640]{2,1,0:T(8,128)(2,1)S(1)} %get-tuple-element.76), channel_id=1, source_target_pairs={{0,4},{1,5},{8,12},{9,13},{16,20},{17,21},{24,28},{25,29},{32,36},... | collective-permute-start | bytes 122888 | tf_op jit(solution)/shard_map/ppermute | solution.py:226
  58.8 6.1 %collective-permute-start.5 = (bf16[2,16,640]{2,1,0:T(8,128)(2,1)S(1)}, bf16[2,16,640]{2,1,0:T(8,128)(2,1)S(1)}, u32[]{:S(2)}, u32[]{:S(2)}) collective-permute-start(bf16[2,16,640]{2,1,0:T(8,128)(2,1)S(1)} %get-tuple-element.76), channel_id=1, source_target_pairs={{0,6},{1,7},{8,14},{9,15},{16,22},{17,23},{24,30},{25,31},{32,38},... | collective-permute-start | bytes 122888 | tf_op jit(solution)/shard_map/ppermute | solution.py:226
  59.5 5.4 %collective-permute-start.4 = (bf16[2,16,640]{2,1,0:T(8,128)(2,1)S(1)}, bf16[2,16,640]{2,1,0:T(8,128)(2,1)S(1)}, u32[]{:S(2)}, u32[]{:S(2)}) collective-permute-start(bf16[2,16,640]{2,1,0:T(8,128)(2,1)S(1)} %get-tuple-element.76), channel_id=1, source_target_pairs={{0,2},{1,3},{8,10},{9,11},{16,18},{17,19},{24,26},{25,27},{32,34},... | collective-permute-start | bytes 122888 | tf_op jit(solution)/shard_map/ppermute | solution.py:226
  66.0 30.6 %all-to-all-start.3 = ((bf16[8,6,16,640]{3,2,1,0:T(8,128)(2,1)}), bf16[8,6,16,640]{3,2,1,0:T(8,128)(2,1)S(1)}, u32[]{:S(2)}, u32[]{:S(2)}) async-start(bf16[8,6,16,640]{3,2,1,0:T(8,128)(2,1)} %broadcast_in_dim.9), calls=%async_computation.3 | async-start | bytes 1966080 | tf_op jit(solution)/shard_map/all_to_all | solution.py:239
  97.8 25.4 %all-to-all-start.5 = ((bf16[4,8,2,16,640]{4,3,2,1,0:T(8,128)(2,1)}), bf16[4,8,2,16,640]{4,3,2,1,0:T(8,128)(2,1)}, u32[]{:S(2)}, u32[]{:S(2)}) async-start(bf16[4,8,2,16,640]{4,3,2,1,0:T(8,128)(2,1)} %broadcast_in_dim.11), calls=%async_computation.5 | async-start | bytes 2621440 | tf_op jit(solution)/shard_map/all_to_all | solution.py:239
  103.6 16.3 %collective-permute-start.8 = (bf16[512,640]{1,0:T(8,128)(2,1)}, bf16[512,640]{1,0:T(8,128)(2,1)}, u32[]{:S(2)}, u32[]{:S(2)}) collective-permute-start(bf16[512,640]{1,0:T(8,128)(2,1)} %get-tuple-element.81), channel_id=1, source_target_pairs={{2,4},{3,5},{10,12},{11,13},{18,20},{19,21},{26,28},{27,29},{34,36... | collective-permute-start | bytes 1966088 | tf_op jit(solution)/shard_map/ppermute | solution.py:230
  104.9 15.7 %collective-permute-start.9 = (bf16[512,640]{1,0:T(8,128)(2,1)S(1)}, bf16[512,640]{1,0:T(8,128)(2,1)}, u32[]{:S(2)}, u32[]{:S(2)}) collective-permute-start(bf16[512,640]{1,0:T(8,128)(2,1)S(1)} %get-tuple-element.82), channel_id=1, source_target_pairs={{6,4},{7,5},{14,12},{15,13},{22,20},{23,21},{30,28},{31,29},{38,36... | collective-permute-start | bytes 1966088 | tf_op jit(solution)/shard_map/ppermute | solution.py:230
  123.2 7.6 %collective-permute-start.10 = (bf16[2,512,640]{2,1,0:T(8,128)(2,1)}, bf16[2,512,640]{2,1,0:T(8,128)(2,1)}, u32[]{:S(2)}, u32[]{:S(2)}) collective-permute-start(bf16[2,512,640]{2,1,0:T(8,128)(2,1)} %maximum_select_fusion.cols_own), channel_id=1, source_target_pairs={{0,1},{1,0},{2,3},{3,2},{4,5},{5,4},{6,7},{7,6},{8,9},{9,8},{10,11... | collective-permute-start | bytes 3932168 | tf_op jit(solution)/shard_map/ppermute | solution.py:233
  123.2 7.6 %collective-permute-start.7 = (bf16[4,8,2,16,640]{4,3,2,1,0:T(8,128)(2,1)}, bf16[4,8,2,16,640]{4,3,2,1,0:T(8,128)(2,1)}, u32[]{:S(2)}, u32[]{:S(2)}) collective-permute-start(bf16[4,8,2,16,640]{4,3,2,1,0:T(8,128)(2,1)} %all-to-all-done.5.own), channel_id=1, source_target_pairs={{0,1},{1,0},{2,3},{3,2},{4,5},{5,4},{6,7},{7,6},{8,9},{9,8},{10,11... | collective-permute-start | bytes 3932168 | tf_op jit(solution)/shard_map/ppermute | solution.py:247
  125.6 5.0 %copy-start.7 = (s32[64]{0:T(128)S(1)}, s32[64]{0:T(128)}, u32[]{:S(2)}) copy-start(s32[64]{0:T(128)} %param.13) | copy-start | bytes 772
  125.6 35.6 %all-to-all-start.4 = ((bf16[4,8,4,16,640]{4,3,2,1,0:T(8,128)(2,1)}), bf16[4,8,4,16,640]{4,3,2,1,0:T(8,128)(2,1)S(1)}, u32[]{:S(2)}, u32[]{:S(2)}) async-start(bf16[4,8,4,16,640]{4,3,2,1,0:T(8,128)(2,1)} %broadcast_in_dim.10), calls=%async_computation.4 | async-start | bytes 5242880 | tf_op jit(solution)/shard_map/all_to_all | solution.py:239
  130.8 30.5 %copy-start.3 = (bf16[2,2,1,64,512]{4,3,2,1,0:T(8,128)(2,1)S(1)}, bf16[2,2,1,64,512]{4,3,2,1,0:T(8,128)(2,1)}, u32[]{:S(2)}) copy-start(bf16[2,2,1,64,512]{4,3,2,1,0:T(8,128)(2,1)} %param.9) | copy-start | bytes 786436
  130.8 30.5 %copy-start.4 = (bf16[2,2,1,64,512]{4,3,2,1,0:T(8,128)(2,1)S(1)}, bf16[2,2,1,64,512]{4,3,2,1,0:T(8,128)(2,1)}, u32[]{:S(2)}) copy-start(bf16[2,2,1,64,512]{4,3,2,1,0:T(8,128)(2,1)} %param.10) | copy-start | bytes 786436
  144.5 1.5 copy-start
  161.3 1.7 %copy-start.1 = (bf16[5,512,512]{2,1,0:T(8,128)(2,1)S(1)}, bf16[5,512,512]{2,1,0:T(8,128)(2,1)}, u32[]{:S(2)}) copy-start(bf16[5,512,512]{2,1,0:T(8,128)(2,1)} %copy-done) | copy-start | bytes 7864324

commit v3 on v2

v3 whole, which is shorter than its diff:
```python
import math

import jax
import jax.numpy as jnp
from jax import lax
from jax.experimental import pallas as pl
from jax.experimental.pallas import tpu as pltpu
from jax.sharding import PartitionSpec as P

TILE = 512
KMAX = 64
LANES = 128
WIDE = TILE + LANES
PAIR = TILE + WIDE
BLOCKS = TILE // LANES
CHUNK = 16
PARTS = TILE // CHUNK
NROWS = 64
SHIFT = 1.1 * math.sqrt(TILE)
NY, NZ, NX = 4, 8, 4
BF = jnp.bfloat16
F32 = jnp.float32

SMEM = pl.BlockSpec(memory_space=pltpu.SMEM)
VMEM = pl.BlockSpec(memory_space=pltpu.VMEM)
ANY = pl.BlockSpec(memory_space=pl.ANY)
PARAMS = pltpu.CompilerParams(vmem_limit_bytes=40 << 20)


def dot(a, b):
    return jnp.dot(a, b, preferred_element_type=F32)


def split(a):
    high = a.astype(BF)
    return high, (a - high.astype(F32)).astype(BF)


def dot_hi(a, b):
    return dot(a[0], b[0]) + (dot(a[0], b[1]) + dot(a[1], b[0]))


def eye():
    rows = lax.broadcasted_iota(jnp.int32, (TILE, TILE), 0)
    cols = lax.broadcasted_iota(jnp.int32, (TILE, TILE), 1)
    return (rows == cols).astype(F32)


def low_rank(left, right):
    return lax.dot_general(left, right, (((0,), (0,)), ((), ())), preferred_element_type=F32)


def build(wide, diag):
    factors = wide[:, TILE:].reshape(BLOCKS, 2, KMAX, LANES)
    left = jnp.concatenate([factors[k, 0] for k in range(BLOCKS)], axis=1)
    right = jnp.concatenate([factors[k, 1] for k in range(BLOCKS)], axis=1)
    tile = wide[:, :TILE].astype(F32) + low_rank(left, right)
    return tile + jnp.where(diag, SHIFT, 0.0) * eye()


def inverse(pivot):
    ident = eye()
    e = ident - pivot * (1.0 / SHIFT)
    es = split(e)
    e2 = dot_hi(es, es)
    e2s = split(e2)
    total = split(ident + e + e2 + dot_hi(es, e2s))
    e4 = dot_hi(e2s, e2s)
    whole = total[0].astype(F32) + total[1].astype(F32) + dot_hi(total, split(e4))
    return (whole * (1.0 / SHIFT)).astype(BF)


def kept_left(u, rank):
    rows = lax.broadcasted_iota(jnp.int32, (KMAX, TILE), 0)
    return jnp.where(rows < rank, u.astype(F32), 0.0).astype(BF)


def lane_blocks(left, right):
    parts = []
    for k in range(BLOCKS):
        cut = slice(k * LANES, (k + 1) * LANES)
        parts += [left[:, cut], right[:, cut]]
    return jnp.concatenate(parts, axis=0)


def find_owners(row_map):
    def step(slot, found):
        held = row_map[slot]
        return jnp.where(held == 0, slot, found[0]), jnp.where(held == 1, slot, found[1])

    return lax.fori_loop(0, NROWS, step, (0, 0), unroll=8)


def head_kernel(second, row_map, mask, ranks, near, u, v, cols, send):
    row = lax.axis_index("row")
    col = lax.axis_index("col")
    for s in range(2):
        cols[s, :, :TILE] = near[s, 0] * mask[s, 0].astype(F32).astype(BF)
        cols[s, :, TILE:] = lane_blocks(kept_left(u[s, 0], ranks[s, 0]), v[s, 0])
    owners = find_owners(row_map)
    panel = 1 if second else jnp.where(row == owners[0] >> 1, 0, 1)
    s = jnp.where(panel == 0, owners[0], owners[1]) & 1
    for t in range(2):
        low = low_rank(kept_left(u[s, t], ranks[s, t]), v[s, t])
        tile = (near[s, t].astype(F32) * mask[s, t].astype(F32) + low).astype(BF)
        start = t * WIDE
        send[:, :, start : start + TILE] = tile.reshape(PARTS, CHUNK, TILE)

    @pl.when(col == panel)
    def _():
        send[:, :, :WIDE] = cols[s].reshape(PARTS, CHUNK, WIDE)


def head(second, row_map, mask, ranks, near, u, v):
    def kernel(*refs):
        head_kernel(second, *refs)

    return pl.pallas_call(
        kernel,
        out_shape=(
            jax.ShapeDtypeStruct((2, TILE, WIDE), BF),
            jax.ShapeDtypeStruct((PARTS, CHUNK, WIDE + TILE), BF),
        ),
        in_specs=[SMEM] * 3 + [VMEM] * 3,
        out_specs=(VMEM, VMEM),
        compiler_params=PARAMS,
        name="head_again" if second else "head",
    )(row_map, mask, ranks, near, u, v)


def take_kernel(row_map, got0, got1, pivots, rows, chunk, sems):
    copies = []
    for k, (got, owner) in enumerate(zip((got0, got1), find_owners(row_map))):
        copies.append(pltpu.make_async_copy(got.at[owner >> 1], chunk.at[k], sems.at[k]))
        copies[-1].start()
    for copy in copies:
        copy.wait()
    core = lax.axis_index("col") & 1
    pivots[:, :TILE] = chunk[1 - core, :, :TILE]
    pivots[:, TILE:] = chunk[core, :, :WIDE]
    for t in range(2):
        for k in range(2):
            rows[:, (2 * t + k) * TILE : (2 * t + k + 1) * TILE] = chunk[k, :, t * WIDE : t * WIDE + TILE]


def take(row_map, got0, got1):
    return pl.pallas_call(
        take_kernel,
        out_shape=(
            jax.ShapeDtypeStruct((CHUNK, PAIR), BF),
            jax.ShapeDtypeStruct((CHUNK, 4 * TILE), BF),
        ),
        in_specs=[SMEM, ANY, ANY],
        out_specs=(VMEM, VMEM),
        scratch_shapes=[pltpu.VMEM((2, CHUNK, WIDE + TILE), BF), pltpu.SemaphoreType.DMA((2,))],
        compiler_params=PARAMS,
        name="take",
    )(row_map, got0, got1)


def bundle_kernel(own, hop1, hop3, hop2, rows, out):
    x = lax.axis_index("col") >> 1

    @pl.when(x == 0)
    def _():
        for z in range(NZ):
            out[z, :, :PAIR] = own[...]

    @pl.when(x != 0)
    def _():
        pivots = hop1[...] + hop3[...] + hop2[...]
        for z in range(NZ):
            out[z, :, :PAIR] = pivots

    for z in range(NZ):
        out[z, :, PAIR:] = rows[...]


def bundle(own, hops, rows):
    return pl.pallas_call(
        bundle_kernel,
        out_shape=jax.ShapeDtypeStruct((NZ, CHUNK, PAIR + 4 * TILE), BF),
        in_specs=[VMEM] * 5,
        out_specs=VMEM,
        compiler_params=PARAMS,
        name="bundle",
    )(own, *hops, rows)


def chain_kernel(own, other, out, piv):
    core = lax.axis_index("col") & 1
    piv[core] = own[...].reshape(TILE, PAIR)
    piv[1 - core] = other[...].reshape(TILE, PAIR)
    inv0 = inverse(build(piv[0, :, TILE:], True))
    row1 = piv[1, :, :TILE]
    mult_p1 = dot(piv[0, :, :TILE], inv0).astype(BF)
    out[0] = inv0
    out[1] = row1
    out[2] = mult_p1
    out[3] = inverse(build(piv[1, :, TILE:], True) - dot(mult_p1, row1))


def chain(own, other):
    return pl.pallas_call(
        chain_kernel,
        out_shape=jax.ShapeDtypeStruct((4, TILE, TILE), BF),
        in_specs=[VMEM] * 2,
        out_specs=VMEM,
        scratch_shapes=[pltpu.VMEM((2, TILE, PAIR), BF)],
        compiler_params=PARAMS,
        cost_estimate=pl.CostEstimate(flops=28 * 2 * TILE**3, bytes_accessed=5 << 20, transcendentals=0),
        name="chain",
    )(own, other)


def mults_kernel(row_map, own, other, lead, out, cols):
    core = lax.axis_index("col") & 1
    row = lax.axis_index("row")
    cols[core] = own[...]
    cols[1 - core] = other[...]
    for s in range(2):
        held = row_map[2 * row + s]
        first = dot(build(cols[0, s], held == 0).astype(BF), lead[0]).astype(BF)
        second = build(cols[1, s], held == 1)
        second = jnp.where(held > 0, second - dot(first, lead[1]), second)
        out[s, 0] = first
        out[s, 1] = dot(second.astype(BF), lead[3]).astype(BF)


def mults(row_map, own, other, lead):
    return pl.pallas_call(
        mults_kernel,
        out_shape=jax.ShapeDtypeStruct((2, 2, TILE, TILE), BF),
        in_specs=[SMEM] + [VMEM] * 3,
        out_specs=VMEM,
        scratch_shapes=[pltpu.VMEM((2, 2, TILE, WIDE), BF)],
        compiler_params=PARAMS,
        cost_estimate=pl.CostEstimate(flops=7 * 2 * TILE**3, bytes_accessed=7 << 20, transcendentals=0),
        name="mults",
    )(row_map, own, other, lead)


def last_kernel(row_map, mask, ranks, near, u, v, rows, lead, mult, out):
    row = lax.axis_index("row")
    col = lax.axis_index("col")
    t = pl.program_id(0)
    j = t * 2 * NX + col
    row0 = rows[:, :, :, :TILE].reshape(TILE, TILE).astype(F32)
    row0 = jnp.where(j == 1, lead[1].astype(F32), row0).astype(BF)
    row1 = rows[:, :, :, TILE:].reshape(TILE, TILE).astype(F32)
    row1 = (row1 - dot(lead[2], row0)).astype(BF)
    for s in range(2):
        held = row_map[2 * row + s]
        tile = near[s, 0].astype(F32) * mask[s, t].astype(F32)
        tile = tile + low_rank(kept_left(u[s, 0], ranks[s, t]), v[s, 0])
        tile = tile + jnp.where(held == j, SHIFT, 0.0) * eye()
        for k, pivot_row in enumerate((row0, row1)):
            live = (held > k) & (j > k)
            tile = jnp.where(live, tile - dot(mult[s, k], pivot_row), tile)
        out[s, 0] = tile.astype(BF)


def last(row_map, mask, ranks, near, u, v, rows, lead, mult):
    def tiles(height):
        return pl.BlockSpec((2, 1, height, TILE), lambda t: (0, t, 0, 0))

    return pl.pallas_call(
        last_kernel,
        grid=(2,),
        out_shape=jax.ShapeDtypeStruct((2, 2, TILE, TILE), BF),
        in_specs=[SMEM] * 3
        + [tiles(TILE), tiles(KMAX), tiles(KMAX)]
        + [pl.BlockSpec((NY, NZ, CHUNK, 2 * TILE), lambda t: (0, 0, 0, t)), VMEM, VMEM],
        out_specs=tiles(TILE),
        compiler_params=PARAMS,
        cost_estimate=pl.CostEstimate(flops=12 * 2 * TILE**3, bytes_accessed=10 << 20, transcendentals=0),
        name="last",
    )(row_map, mask, ranks, near, u, v, rows, lead, mult)


def pairs(source, target):
    return [(source * 2 + core, target * 2 + core) for core in range(2)]


def body(near_tiles, basis_u, basis_v, near_mask, ranks, row_map):
    near = near_tiles.reshape(2, 2, TILE, TILE)
    u = basis_u.reshape(2, 2, KMAX, TILE)
    v = basis_v.reshape(2, 2, KMAX, TILE)
    mask = near_mask.reshape(2, 2)
    ranks = ranks.reshape(2, 2)
    x = lax.axis_index("col") >> 1

    cols, send = head(False, row_map, mask, ranks, near, u, v)

    def scatter(part):
        return lax.all_to_all(part, "row", 0, 0)

    def first_hop(cols):
        return [lax.ppermute(cols, "col", pairs(0, to)) for to in (1, 3)]

    def apart():
        again = head(True, row_map, mask, ranks, near, u, v)[1]
        hop = first_hop(cols)
        return take(row_map, scatter(send), scatter(again)), hop

    def merged():
        hop = first_hop(cols)
        got = scatter(send)
        return take(row_map, got, got), hop

    one_device = jnp.any(row_map.reshape(-1, 2).sum(axis=1) == 1)
    (own, rows), hop = lax.cond(one_device, apart, merged)

    hops = [lax.ppermute(own, "col", pairs(0, to)) for to in (1, 3, 2)]
    line = bundle(own, hops, rows)

    cols = jnp.where(x == 0, cols, hop[0] + hop[1])
    hop = [lax.ppermute(cols[s], "col", pairs(source, 2)) for s, source in enumerate((1, 3))]
    cols = jnp.where(x == 2, jnp.stack(hop), cols)
    swap = [(c, c ^ 1) for c in range(2 * NX)]

    z_groups = [[y * NZ + z for z in range(NZ)] for y in range(NY)]
    y_groups = [[y * NZ + z for y in range(NY)] for z in range(NZ)]
    line = lax.all_to_all(line, "row", 0, 0, axis_index_groups=z_groups)

    def gather(part):
        part = jnp.broadcast_to(part[None], (NY, *part.shape))
        return lax.all_to_all(part, "row", 0, 0, axis_index_groups=y_groups)

    piv = gather(line[:, :, :PAIR])
    rows = gather(line[:, :, PAIR:])
    lead = chain(piv, lax.ppermute(piv, "col", swap))
    mult = mults(row_map, cols, lax.ppermute(cols, "col", swap), lead)
    out = last(row_map, mask, ranks, near, u, v, rows, lead, mult)
    return out.reshape(2, 2, 1, TILE, TILE)


def solution(mesh):
    return jax.shard_map(
        body,
        mesh=mesh,
        in_specs=(
            P("row", None, "col", None, None),
            P("row", None, "col", None, None),
            P("row", None, "col", None, None),
            P("row", None, "col"),
            P("row", None, "col"),
            P(),
        ),
        out_specs=P("row", None, "col", None, None),
        check_vma=False,
    )
```

time: 172 us -> 152 us (0.88)
  waiting for transfers between devices: 86 us -> 72.4 us
  between operations: 6.54 us -> 0.77 us
  other arithmetic: 7.18 us -> 4.11 us
    ppermute x2, waiting for transfers between devices: 14.4 us -> 1.09 us  [body(): lax.ppermute(cols[s], 'col', pairs(source, 2))]
    all_to_all x4, waiting for transfers between devices: 66.8 us -> 59.5 us  [the longest x1 25.3 us: scatter(): return lax.all_to_all(part, 'row', 0, 0)]
    ppermute x5, waiting for transfers between devices: 4.75 us -> 11.9 us  [the longest x3 11.9 us: body(): hops = [lax.ppermute(own, 'col', pairs(0, to)) for to in (1, 3, 2)]]
    unnamed x16 -> x24, local copies, waits for them, and re-layouts: 3.31 us -> 6.08 us
    broadcast_in_dim x3 -> x2, local copies, waits for them, and re-layouts: 4.08 us -> 2.71 us  [gather(): part = jnp.broadcast_to(part[None], (NY, *part.shape))]
    pallas_call x3 -> x6, Pallas kernels: 24.4 us -> 25.2 us  [the longest x1 9.78 us: chain(): pl.pallas_call(chain_kernel, out_shape=jax.ShapeDtypeStruct((4, TILE, TIL...]
  transfers between devices with their start and end apart: 13 -> 13, of which waited for: 6 -> 6; matrix products, arithmetic and copies ran while one was open for 6% -> 4% of each run, Pallas kernels for 8% -> 9%
where the time goes in v3:
time: 152 us; the launch traced here: 150 us
  waiting for transfers between devices  72.4 us (48%)
  starting transfers between devices  37.2 us (24%)
  Pallas kernels  25.2 us (17%)
  local copies, waits for them, and re-layouts  10.2 us (7%)
  other arithmetic  4.11 us (3%)
    all_to_all x1, waiting for transfers between devices, scatter(): return lax.all_to_all(part, 'row', 0, 0)  25.3 us
    all_to_all x1, waiting for transfers between devices, body(): line = lax.all_to_all(line, 'row', 0, 0, axis_index_groups=z_groups)  21.2 us
    all_to_all x2, waiting for transfers between devices, gather(): return lax.all_to_all(part, 'row', 0, 0, axis_index_groups=y_groups)  12.9 us
    ppermute x3, waiting for transfers between devices, body(): hops = [lax.ppermute(own, 'col', pairs(0, to)) for to in (1, 3, 2)]  11.9 us
    all_to_all x1, starting transfers between devices, scatter(): return lax.all_to_all(part, 'row', 0, 0)  11.7 us
    all_to_all x2, starting transfers between devices, gather(): return lax.all_to_all(part, 'row', 0, 0, axis_index_groups=y_groups)  9.85 us
    pallas_call x1, Pallas kernels, chain(): pl.pallas_call(chain_kernel, out_shape=jax.ShapeDtypeStruct((4, TILE, TIL...  9.78 us
    all_to_all x1, starting transfers between devices, body(): line = lax.all_to_all(line, 'row', 0, 0, axis_index_groups=z_groups)  6.65 us
  transfers between devices with their start and end apart: 13, of which 6 were waited for; matrix products, arithmetic and copies ran while one was open for 4% of the time, Pallas kernels for 9%

profile of v3, /device:TPU:12, one launch (start us, length us, event | category | flops | bytes accessed | tf_op | source)
XLA Modules:
  0.0 149.9 jit_solution(13251409995400492919)
XLA Ops:
  0.0 0.0 copy-start.9
  0.0 0.0 copy-start.5
  0.0 0.0 copy-start.6
  0.0 0.0 copy-start.7
  0.0 0.0 copy-start.10
  0.0 0.0 copy-start.11
  0.0 4.0 %head.1 = (bf16[2,512,640]{2,1,0:T(8,128)(2,1)}, bf16[32,16,1152]{2,1,0:T(8,128)(2,1)}) custom-call(s32[64]{0:T(128)} %row_map.3, s32[2,2]{1,0:T(2,128)} %bitcast.23, s32[2,2]{1,0:T(2,128)} %bitcast.26, bf16[2,2,512,512]{3,2,1,0:T(8,128)(2,1)} %bitcast.14, bf16[2,2,64,512]{3,2,1,0:T(8,128)(2,1)} %bitcast.17, bf16[2,2,64,512]{3,2,1,0:T(8,128)(2,1)} %bitcast.20), custom_call_target="tpu_custom_call" | custom-call | tf_op jit(solution)/shard_map/head/pallas_call | solution.py:118
  4.1 0.0 copy-done.9
  4.1 0.1 reshape.28
  4.2 0.1 reduce_sum.9
  4.3 0.6 compare_reduce_fusion
  4.9 0.0 copy-done.5
  4.9 0.0 copy-done.6
  4.9 0.0 copy-done.7
  4.9 0.0 copy-done.10
  4.9 0.0 copy-done.11
  5.5 41.4 %conditional.1 = (bf16[16,1152]{1,0:T(8,128)(2,1)S(1)}, bf16[16,2048]{1,0:T(8,128)(2,1)S(1)}, bf16[2,512,640]{2,1,0:T(8,128)(2,1)}, bf16[2,512,640]{2,1,0:T(8,128)(2,1)}) conditional(s32[]{:T(128)} %convert_element_type.3, (bf16[32,16,1152]{2,1,0:T(8,128)(2,1)}, s32[64]{0:T(128)S(1)}, bf16[2,512,640]{2,1,0:T(8,128)(2,1)}) %tuple.21, ...), branch_computations={%region_2.0_spmd, %region_3.0_spmd} | conditional | bytes 16384144 | solution.py:312
  5.5 11.7 %all-to-all-start = ((bf16[32,16,1152]{2,1,0:T(8,128)(2,1)}), bf16[32,16,1152]{2,1,0:T(8,128)(2,1)S(1)}, u32[]{:S(2)}, u32[]{:S(2)}) async-start(bf16[32,16,1152]{2,1,0:T(8,128)(2,1)} %get-tuple-element.28), calls=%async_computation | async-start | bytes 2359296 | tf_op jit(solution)/shard_map/cond/branch_0_fun/all_to_all | solution.py:296
  17.2 1.7 %collective-permute-start = (bf16[2,512,640]{2,1,0:T(8,128)(2,1)}, bf16[2,512,640]{2,1,0:T(8,128)(2,1)}, u32[]{:S(2)}, u32[]{:S(2)}) collective-permute-start(bf16[2,512,640]{2,1,0:T(8,128)(2,1)} %get-tuple-element.31), channel_id=1, source_target_pairs={{0,2},{1,3},{8,10},{9,11},{16,18},{17,19},{24,26},{25,27},{32,34},... | collective-permute-start | bytes 3932168 | tf_op jit(solution)/shard_map/cond/branch_0_fun/ppermute | solution.py:299
  19.0 1.7 %collective-permute-start.1 = (bf16[2,512,640]{2,1,0:T(8,128)(2,1)}, bf16[2,512,640]{2,1,0:T(8,128)(2,1)}, u32[]{:S(2)}, u32[]{:S(2)}) collective-permute-start(bf16[2,512,640]{2,1,0:T(8,128)(2,1)} %get-tuple-element.31), channel_id=1, source_target_pairs={{0,6},{1,7},{8,14},{9,15},{16,22},{17,23},{24,30},{25,31},{32,38},... | collective-permute-start | bytes 3932168 | tf_op jit(solution)/shard_map/cond/branch_0_fun/ppermute | solution.py:299
  20.7 25.3 %all-to-all-done.got0.got1 = bf16[32,16,1152]{2,1,0:T(8,128)(2,1)S(1)} async-done(((bf16[32,16,1152]{2,1,0:T(8,128)(2,1)}), bf16[32,16,1152]{2,1,0:T(8,128)(2,1)S(1)}, u32[]{:S(2)}, u32[]{:S(2)}) %all-to-all-start) | async-done | bytes 1179680 | tf_op jit(solution)/shard_map/cond/branch_0_fun/all_to_all | solution.py:296
  46.0 0.8 take.2
  46.9 0.0 collective-permute-done
  46.9 0.0 collective-permute-done.1
  46.9 0.7 collective-permute-start.4
  47.6 0.7 collective-permute-start.5
  48.2 1.3 collective-permute-start.6
  49.5 0.0 collective-permute-done.4.hop1
  49.5 0.0 collective-permute-done.5.hop3
  49.6 11.9 %collective-permute-done.6.hop2 = bf16[16,1152]{1,0:T(8,128)(2,1)S(1)} collective-permute-done((bf16[16,1152]{1,0:T(8,128)(2,1)S(1)}, bf16[16,1152]{1,0:T(8,128)(2,1)S(1)}, u32[]{:S(2)}, u32[]{:S(2)}) %collective-permute-start.6) | collective-permute-done | bytes 36896 | tf_op jit(solution)/shard_map/ppermute | solution.py:314
  61.4 0.9 bundle.1
  62.3 6.6 %all-to-all-start.3 = ((bf16[8,16,3200]{2,1,0:T(8,128)(2,1)}), bf16[8,16,3200]{2,1,0:T(8,128)(2,1)S(1)}, u32[]{:S(2)}, u32[]{:S(2)}) async-start(bf16[8,16,3200]{2,1,0:T(8,128)(2,1)} %bundle.1), calls=%async_computation.3 | async-start | bytes 1638400 | tf_op jit(solution)/shard_map/all_to_all | solution.py:324
  69.0 21.2 %all-to-all-done.3 = bf16[8,16,3200]{2,1,0:T(8,128)(2,1)S(1)} async-done(((bf16[8,16,3200]{2,1,0:T(8,128)(2,1)}), bf16[8,16,3200]{2,1,0:T(8,128)(2,1)S(1)}, u32[]{:S(2)}, u32[]{:S(2)}) %all-to-all-start.3) | async-done | bytes 819232 | tf_op jit(solution)/shard_map/all_to_all | solution.py:324
  90.2 1.1 broadcast_in_dim.5
  91.4 4.8 %all-to-all-start.5 = ((bf16[4,8,16,1152]{3,2,1,0:T(8,128)(2,1)}), bf16[4,8,16,1152]{3,2,1,0:T(8,128)(2,1)S(1)}, u32[]{:S(2)}, u32[]{:S(2)}) async-start(bf16[4,8,16,1152]{3,2,1,0:T(8,128)(2,1)} %broadcast_in_dim.5), calls=%async_computation.5 | async-start | bytes 2359296 | tf_op jit(solution)/shard_map/all_to_all | solution.py:328
  96.2 1.9 %add_select_fusion = bf16[2,512,640]{2,1,0:T(8,128)(2,1)S(1)} fusion(bf16[2,512,640]{2,1,0:T(8,128)(2,1)} %get-tuple-element.50, bf16[2,512,640]{2,1,0:T(8,128)(2,1)} %get-tuple-element.53, bf16[2,512,640]{2,1,0:T(8,128)(2,1)} %get-tuple-element.54, pred[]{:T(512)S(6)} %eq.15), kind=kLoop, calls=%fused_computation.1 | loop fusion | flops 1310720 | bytes 5242881 | tf_op jit(solution)/shard_map/jit(_where)/select_n | solution.py:317
  98.1 0.0 copy-start.4
  98.1 1.3 slice_bitcast_fusion.1
  99.4 0.2 copy-done.4
  99.6 1.3 collective-permute-start.8
  100.9 1.3 collective-permute-start.9
  102.2 5.8 %all-to-all-done.5.own = bf16[4,8,16,1152]{3,2,1,0:T(8,128)(2,1)S(1)} async-done(((bf16[4,8,16,1152]{3,2,1,0:T(8,128)(2,1)}), bf16[4,8,16,1152]{3,2,1,0:T(8,128)(2,1)S(1)}, u32[]{:S(2)}, u32[]{:S(2)}) %all-to-all-start.5) | async-done | bytes 1179680 | tf_op jit(solution)/shard_map/all_to_all | solution.py:328
  108.0 0.0 collective-permute-start.7
  108.0 1.6 %broadcast_in_dim.4 = bf16[4,8,16,2048]{3,2,1,0:T(8,128)(2,1)} broadcast(bf16[8,16,2048]{2,1,0:T(8,128)(2,1)S(1)} %slice.16), dimensions={1,2,3} | broadcast | bytes 2621440 | tf_op jit(solution)/shard_map/broadcast_in_dim | solution.py:327
  109.6 5.0 %all-to-all-start.4 = ((bf16[4,8,16,2048]{3,2,1,0:T(8,128)(2,1)}), bf16[4,8,16,2048]{3,2,1,0:T(8,128)(2,1)S(1)}, u32[]{:S(2)}, u32[]{:S(2)}) async-start(bf16[4,8,16,2048]{3,2,1,0:T(8,128)(2,1)} %broadcast_in_dim.4), calls=%async_computation.4 | async-start | bytes 4194304 | tf_op jit(solution)/shard_map/all_to_all | solution.py:328
  114.7 0.0 collective-permute-done.8
  114.7 1.1 collective-permute-done.9
  115.7 1.5 maximum_select_fusion.own
  117.2 0.3 collective-permute-start.10
  117.5 0.0 collective-permute-done.7.other
  117.5 9.8 %chain.1.lead = bf16[4,512,512]{2,1,0:T(8,128)(2,1)S(1)} custom-call(bf16[4,8,16,1152]{3,2,1,0:T(8,128)(2,1)S(1)} %all-to-all-done.5.own, bf16[4,8,16,1152]{3,2,1,0:T(8,128)(2,1)} %collective-permute-done.7.other), custom_call_target="tpu_custom_call" | custom-call | flops 7516192768 | bytes 5242880 | tf_op jit(solution)/shard_map/chain/pallas_call | solution.py:204
  127.3 0.0 copy-start.8
  127.3 0.0 collective-permute-done.10.other
  127.3 3.4 %mults.1.mult = bf16[2,2,512,512]{3,2,1,0:T(8,128)(2,1)S(1)} custom-call(s32[64]{0:T(128)S(1)} %copy-done.9, bf16[2,512,640]{2,1,0:T(8,128)(2,1)S(1)} %maximum_select_fusion.own, bf16[2,512,640]{2,1,0:T(8,128)(2,1)S(1)} %collective-permute-done.10.other, bf16[4,512,512]{2,1,0:T(8,128)(2,1)S(1)} %chain.1.lead), custom_call_target="tpu_custom_call" | custom-call | flops 1879048192 | bytes 7340032 | tf_op jit(solution)/shard_map/mults/pallas_call | solution.py:231
  130.7 0.0 copy-start
  130.7 1.3 copy-done
  132.0 0.0 copy-start.2
  132.0 1.3 copy-done.2
  133.4 7.1 %all-to-all-done.4.rows = bf16[4,8,16,2048]{3,2,1,0:T(8,128)(2,1)S(1)} async-done(((bf16[4,8,16,2048]{3,2,1,0:T(8,128)(2,1)}), bf16[4,8,16,2048]{3,2,1,0:T(8,128)(2,1)S(1)}, u32[]{:S(2)}, u32[]{:S(2)}) %all-to-all-start.4) | async-done | bytes 2097184 | tf_op jit(solution)/shard_map/all_to_all | solution.py:328
  140.5 0.0 copy-done.8
  140.5 0.0 copy-start.1
  140.5 1.6 %copy-done.1 = bf16[4,512,512]{2,1,0:T(8,128)(2,1)S(1)} copy-done((bf16[4,512,512]{2,1,0:T(8,128)(2,1)S(1)}, bf16[4,512,512]{2,1,0:T(8,128)(2,1)}, u32[]{:S(2)}) %copy-start.1) | copy-done | bytes 2097176
  142.1 1.6 %copy-done.3 = bf16[2,2,512,512]{3,2,1,0:T(8,128)(2,1)S(1)} copy-done((bf16[2,2,512,512]{3,2,1,0:T(8,128)(2,1)S(1)}, bf16[2,2,512,512]{3,2,1,0:T(8,128)(2,1)}, u32[]{:S(2)}) %copy-start.3) | copy-done | bytes 2097176
  143.7 6.2 %last.1 = bf16[2,2,512,512]{3,2,1,0:T(8,128)(2,1)} custom-call(s32[64]{0:T(128)S(1)} %copy-done.9, s32[2,2]{1,0:T(2,128)S(1)} %bitcast.25, s32[2,2]{1,0:T(2,128)S(1)} %bitcast.28, bf16[2,2,512,512]{3,2,1,0:T(8,128)(2,1)} %bitcast.15, bf16[2,2,64,512]{3,2,1,0:T(8,128)(2,1)S(1)} %bitcast.19, bf16[2,2,64,512]{3,2,1,0:T(8,128)(2,1)S(1)} %bitcast.22, ...), custom_call_target="tpu_custom_call" | custom-call | flops 3221225472 | bytes 10485760 | tf_op jit(solution)/shard_map/last/pallas_call | solution.py:267
  (3 shorter events, 0.1 us)
Async XLA Ops:
  0.0 4.1 %copy-start.9 = (s32[64]{0:T(128)S(1)}, s32[64]{0:T(128)}, u32[]{:S(2)}) copy-start(s32[64]{0:T(128)} %row_map.3) | copy-start | bytes 772
  0.0 4.9 %copy-start.5 = (bf16[2,2,1,512,512]{4,3,2,1,0:T(8,128)(2,1)S(1)}, bf16[2,2,1,512,512]{4,3,2,1,0:T(8,128)(2,1)}, u32[]{:S(2)}) copy-start(bf16[2,2,1,512,512]{4,3,2,1,0:T(8,128)(2,1)} %param.8) | copy-start | bytes 6291460
  0.0 4.9 %copy-start.6 = (bf16[2,2,1,64,512]{4,3,2,1,0:T(8,128)(2,1)S(1)}, bf16[2,2,1,64,512]{4,3,2,1,0:T(8,128)(2,1)}, u32[]{:S(2)}) copy-start(bf16[2,2,1,64,512]{4,3,2,1,0:T(8,128)(2,1)} %param.9) | copy-start | bytes 786436
  0.0 4.9 %copy-start.7 = (bf16[2,2,1,64,512]{4,3,2,1,0:T(8,128)(2,1)S(1)}, bf16[2,2,1,64,512]{4,3,2,1,0:T(8,128)(2,1)}, u32[]{:S(2)}) copy-start(bf16[2,2,1,64,512]{4,3,2,1,0:T(8,128)(2,1)} %param.10) | copy-start | bytes 786436
  0.0 4.9 %copy-start.10 = (s32[2,2,1]{1,2,0:T(1,128)S(1)}, s32[2,2,1]{1,2,0:T(1,128)}, u32[]{:S(2)}) copy-start(s32[2,2,1]{1,2,0:T(1,128)} %param.11) | copy-start | bytes 52
  0.0 4.9 %copy-start.11 = (s32[2,2,1]{1,2,0:T(1,128)S(1)}, s32[2,2,1]{1,2,0:T(1,128)}, u32[]{:S(2)}) copy-start(s32[2,2,1]{1,2,0:T(1,128)} %param.12) | copy-start | bytes 52
  5.5 40.5 %all-to-all-start = ((bf16[32,16,1152]{2,1,0:T(8,128)(2,1)}), bf16[32,16,1152]{2,1,0:T(8,128)(2,1)S(1)}, u32[]{:S(2)}, u32[]{:S(2)}) async-start(bf16[32,16,1152]{2,1,0:T(8,128)(2,1)} %get-tuple-element.28), calls=%async_computation | async-start | bytes 2359296 | tf_op jit(solution)/shard_map/cond/branch_0_fun/all_to_all | solution.py:296
  17.2 29.6 %collective-permute-start = (bf16[2,512,640]{2,1,0:T(8,128)(2,1)}, bf16[2,512,640]{2,1,0:T(8,128)(2,1)}, u32[]{:S(2)}, u32[]{:S(2)}) collective-permute-start(bf16[2,512,640]{2,1,0:T(8,128)(2,1)} %get-tuple-element.31), channel_id=1, source_target_pairs={{0,2},{1,3},{8,10},{9,11},{16,18},{17,19},{24,26},{25,27},{32,34},... | collective-permute-start | bytes 3932168 | tf_op jit(solution)/shard_map/cond/branch_0_fun/ppermute | solution.py:299
  19.0 27.9 %collective-permute-start.1 = (bf16[2,512,640]{2,1,0:T(8,128)(2,1)}, bf16[2,512,640]{2,1,0:T(8,128)(2,1)}, u32[]{:S(2)}, u32[]{:S(2)}) collective-permute-start(bf16[2,512,640]{2,1,0:T(8,128)(2,1)} %get-tuple-element.31), channel_id=1, source_target_pairs={{0,6},{1,7},{8,14},{9,15},{16,22},{17,23},{24,30},{25,31},{32,38},... | collective-permute-start | bytes 3932168 | tf_op jit(solution)/shard_map/cond/branch_0_fun/ppermute | solution.py:299
  46.9 2.6 %collective-permute-start.4 = (bf16[16,1152]{1,0:T(8,128)(2,1)S(1)}, bf16[16,1152]{1,0:T(8,128)(2,1)S(1)}, u32[]{:S(2)}, u32[]{:S(2)}) collective-permute-start(bf16[16,1152]{1,0:T(8,128)(2,1)S(1)} %get-tuple-element.51.own), channel_id=1, source_target_pairs={{0,2},{1,3},{8,10},{9,11},{16,18},{17,19},{24,26},{25,27},{32,34},... | collective-permute-start | bytes 110600 | tf_op jit(solution)/shard_map/ppermute | solution.py:314
  47.6 2.0 %collective-permute-start.5 = (bf16[16,1152]{1,0:T(8,128)(2,1)S(1)}, bf16[16,1152]{1,0:T(8,128)(2,1)S(1)}, u32[]{:S(2)}, u32[]{:S(2)}) collective-permute-start(bf16[16,1152]{1,0:T(8,128)(2,1)S(1)} %get-tuple-element.51.own), channel_id=1, source_target_pairs={{0,6},{1,7},{8,14},{9,15},{16,22},{17,23},{24,30},{25,31},{32,38},... | collective-permute-start | bytes 110600 | tf_op jit(solution)/shard_map/ppermute | solution.py:314
  48.2 13.2 %collective-permute-start.6 = (bf16[16,1152]{1,0:T(8,128)(2,1)S(1)}, bf16[16,1152]{1,0:T(8,128)(2,1)S(1)}, u32[]{:S(2)}, u32[]{:S(2)}) collective-permute-start(bf16[16,1152]{1,0:T(8,128)(2,1)S(1)} %get-tuple-element.51.own), channel_id=1, source_target_pairs={{0,4},{1,5},{8,12},{9,13},{16,20},{17,21},{24,28},{25,29},{32,36},... | collective-permute-start | bytes 110600 | tf_op jit(solution)/shard_map/ppermute | solution.py:314
  62.3 27.9 %all-to-all-start.3 = ((bf16[8,16,3200]{2,1,0:T(8,128)(2,1)}), bf16[8,16,3200]{2,1,0:T(8,128)(2,1)S(1)}, u32[]{:S(2)}, u32[]{:S(2)}) async-start(bf16[8,16,3200]{2,1,0:T(8,128)(2,1)} %bundle.1), calls=%async_computation.3 | async-start | bytes 1638400 | tf_op jit(solution)/shard_map/all_to_all | solution.py:324
  91.4 16.6 %all-to-all-start.5 = ((bf16[4,8,16,1152]{3,2,1,0:T(8,128)(2,1)}), bf16[4,8,16,1152]{3,2,1,0:T(8,128)(2,1)S(1)}, u32[]{:S(2)}, u32[]{:S(2)}) async-start(bf16[4,8,16,1152]{3,2,1,0:T(8,128)(2,1)} %broadcast_in_dim.5), calls=%async_computation.5 | async-start | bytes 2359296 | tf_op jit(solution)/shard_map/all_to_all | solution.py:328
  98.1 1.5 copy-start.4
  99.6 15.1 %collective-permute-start.8 = (bf16[512,640]{1,0:T(8,128)(2,1)}, bf16[512,640]{1,0:T(8,128)(2,1)}, u32[]{:S(2)}, u32[]{:S(2)}) collective-permute-start(bf16[512,640]{1,0:T(8,128)(2,1)} %get-tuple-element.55), channel_id=1, source_target_pairs={{2,4},{3,5},{10,12},{11,13},{18,20},{19,21},{26,28},{27,29},{34,36... | collective-permute-start | bytes 1966088 | tf_op jit(solution)/shard_map/ppermute | solution.py:318
  100.9 14.9 %collective-permute-start.9 = (bf16[512,640]{1,0:T(8,128)(2,1)}, bf16[512,640]{1,0:T(8,128)(2,1)}, u32[]{:S(2)}, u32[]{:S(2)}) collective-permute-start(bf16[512,640]{1,0:T(8,128)(2,1)} %get-tuple-element.56), channel_id=1, source_target_pairs={{6,4},{7,5},{14,12},{15,13},{22,20},{23,21},{30,28},{31,29},{38,36... | collective-permute-start | bytes 1966088 | tf_op jit(solution)/shard_map/ppermute | solution.py:318
  108.0 9.5 %collective-permute-start.7 = (bf16[4,8,16,1152]{3,2,1,0:T(8,128)(2,1)S(1)}, bf16[4,8,16,1152]{3,2,1,0:T(8,128)(2,1)}, u32[]{:S(2)}, u32[]{:S(2)}) collective-permute-start(bf16[4,8,16,1152]{3,2,1,0:T(8,128)(2,1)S(1)} %all-to-all-done.5.own), channel_id=1, source_target_pairs={{0,1},{1,0},{2,3},{3,2},{4,5},{5,4},{6,7},{7,6},{8,9},{9,8},{10,11... | collective-permute-start | bytes 3538952 | tf_op jit(solution)/shard_map/ppermute | solution.py:332
  109.6 30.9 %all-to-all-start.4 = ((bf16[4,8,16,2048]{3,2,1,0:T(8,128)(2,1)}), bf16[4,8,16,2048]{3,2,1,0:T(8,128)(2,1)S(1)}, u32[]{:S(2)}, u32[]{:S(2)}) async-start(bf16[4,8,16,2048]{3,2,1,0:T(8,128)(2,1)} %broadcast_in_dim.4), calls=%async_computation.4 | async-start | bytes 4194304 | tf_op jit(solution)/shard_map/all_to_all | solution.py:328
  117.2 10.1 %collective-permute-start.10 = (bf16[2,512,640]{2,1,0:T(8,128)(2,1)S(1)}, bf16[2,512,640]{2,1,0:T(8,128)(2,1)S(1)}, u32[]{:S(2)}, u32[]{:S(2)}) collective-permute-start(bf16[2,512,640]{2,1,0:T(8,128)(2,1)S(1)} %maximum_select_fusion.own), channel_id=1, source_target_pairs={{0,1},{1,0},{2,3},{3,2},{4,5},{5,4},{6,7},{7,6},{8,9},{9,8},{10,11... | collective-permute-start | bytes 3932168 | tf_op jit(solution)/shard_map/ppermute | solution.py:333
  127.3 13.2 %copy-start.8 = (bf16[2,2,1,64,512]{4,3,2,1,0:T(8,128)(2,1)S(1)}, bf16[2,2,1,64,512]{4,3,2,1,0:T(8,128)(2,1)}, u32[]{:S(2)}) copy-start(bf16[2,2,1,64,512]{4,3,2,1,0:T(8,128)(2,1)} %param.10) | copy-start | bytes 786436
  130.7 1.3 copy-start
  132.0 1.3 copy-start.2
  140.5 1.6 %copy-start.1 = (bf16[4,512,512]{2,1,0:T(8,128)(2,1)S(1)}, bf16[4,512,512]{2,1,0:T(8,128)(2,1)}, u32[]{:S(2)}) copy-start(bf16[4,512,512]{2,1,0:T(8,128)(2,1)} %copy-done) | copy-start | bytes 6291460
  142.1 1.6 %copy-start.3 = (bf16[2,2,512,512]{3,2,1,0:T(8,128)(2,1)S(1)}, bf16[2,2,512,512]{3,2,1,0:T(8,128)(2,1)}, u32[]{:S(2)}) copy-start(bf16[2,2,512,512]{3,2,1,0:T(8,128)(2,1)} %copy-done.2) | copy-start | bytes 6291460

commit v4 on v3

v4 whole, which is shorter than its diff:
```python
import math

import jax
import jax.numpy as jnp
from jax import lax
from jax.experimental import pallas as pl
from jax.experimental.pallas import tpu as pltpu
from jax.sharding import PartitionSpec as P

TILE = 512
KMAX = 64
LANES = 128
WIDE = TILE + LANES
FIRST = TILE + WIDE
BLOCKS = TILE // LANES
CHUNK = 16
PARTS = TILE // CHUNK
NROWS = 64
SHIFT = 1.1 * math.sqrt(TILE)
NY, NZ, NX = 4, 8, 4
BF = jnp.bfloat16
F32 = jnp.float32

SMEM = pl.BlockSpec(memory_space=pltpu.SMEM)
VMEM = pl.BlockSpec(memory_space=pltpu.VMEM)
ANY = pl.BlockSpec(memory_space=pl.ANY)
PARAMS = pltpu.CompilerParams(vmem_limit_bytes=40 << 20)


def dot(a, b):
    return jnp.dot(a, b, preferred_element_type=F32)


def split(a):
    high = a.astype(BF)
    return high, (a - high.astype(F32)).astype(BF)


def dot_hi(a, b):
    return dot(a[0], b[0]) + (dot(a[0], b[1]) + dot(a[1], b[0]))


def eye():
    rows = lax.broadcasted_iota(jnp.int32, (TILE, TILE), 0)
    cols = lax.broadcasted_iota(jnp.int32, (TILE, TILE), 1)
    return (rows == cols).astype(F32)


def low_rank(left, right):
    return lax.dot_general(left, right, (((0,), (0,)), ((), ())), preferred_element_type=F32)


def build(near, factors, diag):
    factors = factors.reshape(BLOCKS, 2, KMAX, LANES)
    left = jnp.concatenate([factors[k, 0] for k in range(BLOCKS)], axis=1)
    right = jnp.concatenate([factors[k, 1] for k in range(BLOCKS)], axis=1)
    tile = near.astype(F32) + low_rank(left, right)
    return tile + jnp.where(diag, SHIFT, 0.0) * eye()


def inverse(pivot):
    ident = eye()
    e = ident - pivot * (1.0 / SHIFT)
    es = split(e)
    e2 = dot_hi(es, es)
    e2s = split(e2)
    total = split(ident + e + e2 + dot_hi(es, e2s))
    e4 = dot_hi(e2s, e2s)
    whole = total[0].astype(F32) + total[1].astype(F32) + dot_hi(total, split(e4))
    return (whole * (1.0 / SHIFT)).astype(BF)


def kept_left(u, rank):
    rows = lax.broadcasted_iota(jnp.int32, (KMAX, TILE), 0)
    return jnp.where(rows < rank, u.astype(F32), 0.0).astype(BF)


def lane_blocks(left, right):
    parts = []
    for k in range(BLOCKS):
        cut = slice(k * LANES, (k + 1) * LANES)
        parts += [left[:, cut], right[:, cut]]
    return jnp.concatenate(parts, axis=0)


def find_owners(row_map):
    def step(slot, found):
        held = row_map[slot]
        return jnp.where(held == 0, slot, found[0]), jnp.where(held == 1, slot, found[1])

    return lax.fori_loop(0, NROWS, step, (0, 0), unroll=8)


def head_kernel(second, row_map, mask, ranks, near, u, v, send, near_buf, u_buf, v_buf, sems):
    row = lax.axis_index("row")
    col = lax.axis_index("col")
    owners = find_owners(row_map)
    panel = 1 if second else jnp.where(row == owners[0] >> 1, 0, 1)
    s = jnp.where(panel == 0, owners[0], owners[1]) & 1
    copies = [
        pltpu.make_async_copy(source.at[s], target, sems.at[i])
        for i, (source, target) in enumerate(((u, u_buf), (v, v_buf), (near, near_buf)))
    ]
    for copy in copies:
        copy.start()
    for copy in copies:
        copy.wait()
    for t in range(2):
        low = low_rank(kept_left(u_buf[t], ranks[s, t]), v_buf[t])
        tile = (near_buf[t].astype(F32) * mask[s, t].astype(F32) + low).astype(BF)
        start = t * WIDE
        send[:, :, start : start + TILE] = tile.reshape(PARTS, CHUNK, TILE)

    @pl.when(col == panel)
    def _():
        tile = near_buf[0] * mask[s, 0].astype(F32).astype(BF)
        factors = lane_blocks(kept_left(u_buf[0], ranks[s, 0]), v_buf[0])
        send[:, :, :TILE] = tile.reshape(PARTS, CHUNK, TILE)
        send[:, :, TILE:WIDE] = factors.reshape(PARTS, CHUNK, LANES)


def head(second, row_map, mask, ranks, near, u, v):
    def kernel(*refs):
        head_kernel(second, *refs)

    return pl.pallas_call(
        kernel,
        out_shape=jax.ShapeDtypeStruct((PARTS, CHUNK, WIDE + TILE), BF),
        in_specs=[SMEM] * 3 + [ANY] * 3,
        out_specs=VMEM,
        scratch_shapes=[
            pltpu.VMEM((2, TILE, TILE), BF),
            pltpu.VMEM((2, KMAX, TILE), BF),
            pltpu.VMEM((2, KMAX, TILE), BF),
            pltpu.SemaphoreType.DMA((3,)),
        ],
        compiler_params=PARAMS,
        name="head_again" if second else "head",
    )(row_map, mask, ranks, near, u, v)


def columns_kernel(mask, ranks, near, u, v, cols):
    for s in range(2):
        cols[s, :, :TILE] = near[s, 0] * mask[s, 0].astype(F32).astype(BF)
        cols[s, :, TILE:] = lane_blocks(kept_left(u[s, 0], ranks[s, 0]), v[s, 0])


def columns(mask, ranks, near, u, v):
    def tiles(height):
        return pl.BlockSpec((2, 1, height, TILE), lambda i: (0, 0, 0, 0))

    return pl.pallas_call(
        columns_kernel,
        grid=(1,),
        out_shape=jax.ShapeDtypeStruct((2, TILE, WIDE), BF),
        in_specs=[SMEM] * 2 + [tiles(TILE), tiles(KMAX), tiles(KMAX)],
        out_specs=pl.BlockSpec((2, TILE, WIDE), lambda i: (0, 0, 0)),
        compiler_params=PARAMS,
        name="columns",
    )(mask, ranks, near, u, v)


def take_kernel(row_map, got0, got1, out, chunk, sems):
    copies = []
    for k, (got, owner) in enumerate(zip((got0, got1), find_owners(row_map))):
        copies.append(pltpu.make_async_copy(got.at[owner >> 1], chunk.at[k], sems.at[k]))
        copies[-1].start()
    for copy in copies:
        copy.wait()
    core = lax.axis_index("col") & 1
    parts = [chunk[0, :, :TILE], chunk[1, :, :TILE], chunk[core, :, TILE:WIDE]]
    parts += [chunk[0, :, WIDE:], chunk[1, :, WIDE:]]
    whole = jnp.concatenate(parts, axis=1)
    for z in range(NZ):
        out[z] = whole


def take(row_map, got0, got1):
    return pl.pallas_call(
        take_kernel,
        out_shape=jax.ShapeDtypeStruct((NZ, CHUNK, FIRST + 2 * TILE), BF),
        in_specs=[SMEM, ANY, ANY],
        out_specs=VMEM,
        scratch_shapes=[pltpu.VMEM((2, CHUNK, WIDE + TILE), BF), pltpu.SemaphoreType.DMA((2,))],
        compiler_params=PARAMS,
        name="take",
    )(row_map, got0, got1)


def fan_kernel(line, pivots, rows0, rows1):
    pivots[...] = line[:, :, :FIRST]
    for y in range(NY):
        rows0[y] = line[:, :, : 2 * TILE]
        rows1[y] = line[:, :, FIRST:]


def fan(line):
    rows = jax.ShapeDtypeStruct((NY, NZ, CHUNK, 2 * TILE), BF)
    return pl.pallas_call(
        fan_kernel,
        out_shape=(jax.ShapeDtypeStruct((NZ, CHUNK, FIRST), BF), rows, rows),
        in_specs=[VMEM],
        out_specs=(VMEM,) * 3,
        compiler_params=PARAMS,
        name="fan",
    )(line)


def fan_pivots_kernel(own, hop1, hop3, hop2, out):
    x = lax.axis_index("col") >> 1

    @pl.when(x == 0)
    def _():
        for y in range(NY):
            out[y] = own[...]

    @pl.when(x != 0)
    def _():
        pivots = hop1[...] + hop3[...] + hop2[...]
        for y in range(NY):
            out[y] = pivots


def fan_pivots(own, hops):
    return pl.pallas_call(
        fan_pivots_kernel,
        out_shape=jax.ShapeDtypeStruct((NY, NZ, CHUNK, FIRST), BF),
        in_specs=[VMEM] * 4,
        out_specs=VMEM,
        compiler_params=PARAMS,
        name="fan_pivots",
    )(own, *hops)


def chain_kernel(own, other, out, piv):
    core = lax.axis_index("col") & 1
    piv[core] = own[...].reshape(TILE, FIRST)
    piv[1 - core] = other[...].reshape(TILE, FIRST)
    inv0 = inverse(build(piv[0, :, :TILE], piv[0, :, 2 * TILE :], True))
    row1 = piv[1, :, :TILE]
    mult_p1 = dot(piv[0, :, TILE : 2 * TILE], inv0).astype(BF)
    out[0] = inv0
    out[1] = row1
    out[2] = mult_p1
    pivot = build(piv[1, :, TILE : 2 * TILE], piv[1, :, 2 * TILE :], True)
    out[3] = inverse(pivot - dot(mult_p1, row1))


def chain(own, other):
    return pl.pallas_call(
        chain_kernel,
        out_shape=jax.ShapeDtypeStruct((4, TILE, TILE), BF),
        in_specs=[VMEM] * 2,
        out_specs=VMEM,
        scratch_shapes=[pltpu.VMEM((2, TILE, FIRST), BF)],
        compiler_params=PARAMS,
        cost_estimate=pl.CostEstimate(flops=28 * 2 * TILE**3, bytes_accessed=5 << 20, transcendentals=0),
        name="chain",
    )(own, other)


def mults_kernel(row_map, own, other, lead, out, cols):
    core = lax.axis_index("col") & 1
    row = lax.axis_index("row")
    cols[core] = own[...]
    cols[1 - core] = other[...]
    for s in range(2):
        held = row_map[2 * row + s]
        first = build(cols[0, s, :, :TILE], cols[0, s, :, TILE:], held == 0).astype(BF)
        first = dot(first, lead[0]).astype(BF)
        second = build(cols[1, s, :, :TILE], cols[1, s, :, TILE:], held == 1)
        second = jnp.where(held > 0, second - dot(first, lead[1]), second)
        out[s, 0] = first
        out[s, 1] = dot(second.astype(BF), lead[3]).astype(BF)


def mults(row_map, own, other, lead):
    return pl.pallas_call(
        mults_kernel,
        out_shape=jax.ShapeDtypeStruct((2, 2, TILE, TILE), BF),
        in_specs=[SMEM] + [VMEM] * 3,
        out_specs=VMEM,
        scratch_shapes=[pltpu.VMEM((2, 2, TILE, WIDE), BF)],
        compiler_params=PARAMS,
        cost_estimate=pl.CostEstimate(flops=7 * 2 * TILE**3, bytes_accessed=7 << 20, transcendentals=0),
        name="mults",
    )(row_map, own, other, lead)


def last_kernel(
    row_map, mask, ranks, near, u, v, rows0, rows1, lead, mult, out,
    near_buf, u_buf, v_buf, rows_buf, lead_buf, mult_buf, out_buf, sems, out_sems,
):
    row = lax.axis_index("row")
    col = lax.axis_index("col")
    moves = {
        "lead": (lead.at[pl.ds(1, 2)], lead_buf),
        "rows1": (rows1, rows_buf.at[1]),
        "u": (u, u_buf),
        "v": (v, v_buf),
        "near1": (near.at[:, 1], near_buf.at[1]),
        "mult": (mult, mult_buf),
        "rows0": (rows0, rows_buf.at[0]),
        "near0": (near.at[:, 0], near_buf.at[0]),
    }
    copies = {}
    for i, (name, (source, target)) in enumerate(moves.items()):
        copies[name] = pltpu.make_async_copy(source, target, sems.at[i])
        copies[name].start()
    stores = []
    for t in (1, 0):
        j = t * 2 * NX + col
        if t == 1:
            copies["lead"].wait()
        copies[f"rows{t}"].wait()
        row0 = rows_buf[t, :, :, :, :TILE].reshape(TILE, TILE)
        if t == 0:
            row0 = jnp.where(j == 1, lead_buf[0].astype(F32), row0.astype(F32)).astype(BF)
        row1 = rows_buf[t, :, :, :, TILE:].reshape(TILE, TILE).astype(F32)
        row1 = (row1 - dot(lead_buf[1], row0)).astype(BF)
        for name in ("u", "v", "near1", "mult") if t == 1 else ("near0",):
            copies[name].wait()
        for s in range(2):
            held = row_map[2 * row + s]
            tile = near_buf[t, s].astype(F32) * mask[s, t].astype(F32)
            tile = tile + low_rank(kept_left(u_buf[s, t], ranks[s, t]), v_buf[s, t])
            tile = tile + jnp.where(held == j, SHIFT, 0.0) * eye()
            for k, pivot_row in enumerate((row0, row1)):
                live = (held > k) & (j > k)
                tile = jnp.where(live, tile - dot(mult_buf[s, k], pivot_row), tile)
            out_buf[s, t] = tile.astype(BF)
            store = pltpu.make_async_copy(out_buf.at[s, t], out.at[s, t], out_sems.at[s, t])
            store.start()
            stores.append(store)
    for store in stores:
        store.wait()


def last(row_map, mask, ranks, near, u, v, rows0, rows1, lead, mult):
    return pl.pallas_call(
        last_kernel,
        out_shape=jax.ShapeDtypeStruct((2, 2, TILE, TILE), BF),
        in_specs=[SMEM] * 3 + [ANY] * 7,
        out_specs=ANY,
        scratch_shapes=[
            pltpu.VMEM((2, 2, TILE, TILE), BF),
            pltpu.VMEM((2, 2, KMAX, TILE), BF),
            pltpu.VMEM((2, 2, KMAX, TILE), BF),
            pltpu.VMEM((2, NY, NZ, CHUNK, 2 * TILE), BF),
            pltpu.VMEM((2, TILE, TILE), BF),
            pltpu.VMEM((2, 2, TILE, TILE), BF),
            pltpu.VMEM((2, 2, TILE, TILE), BF),
            pltpu.SemaphoreType.DMA((8,)),
            pltpu.SemaphoreType.DMA((2, 2)),
        ],
        compiler_params=pltpu.CompilerParams(vmem_limit_bytes=56 << 20),
        cost_estimate=pl.CostEstimate(flops=12 * 2 * TILE**3, bytes_accessed=10 << 20, transcendentals=0),
        name="last",
    )(row_map, mask, ranks, near, u, v, rows0, rows1, lead, mult)


def pairs(source, target):
    return [(source * 2 + core, target * 2 + core) for core in range(2)]


def body(near_tiles, basis_u, basis_v, near_mask, ranks, row_map):
    near = near_tiles.reshape(2, 2, TILE, TILE)
    u = basis_u.reshape(2, 2, KMAX, TILE)
    v = basis_v.reshape(2, 2, KMAX, TILE)
    mask = near_mask.reshape(2, 2)
    ranks = ranks.reshape(2, 2)
    x = lax.axis_index("col") >> 1

    send = head(False, row_map, mask, ranks, near, u, v)

    def scatter(part):
        return lax.all_to_all(part, "row", 0, 0)

    def first_hop():
        cols = columns(mask, ranks, near, u, v)
        return [cols] + [lax.ppermute(cols, "col", pairs(0, to)) for to in (1, 3)]

    def apart():
        again = head(True, row_map, mask, ranks, near, u, v)
        got = [scatter(send), scatter(again)]
        return take(row_map, *got), first_hop()

    def merged():
        got = scatter(send)
        return take(row_map, got, got), first_hop()

    one_device = jnp.any(row_map.reshape(-1, 2).sum(axis=1) == 1)
    line, hop = lax.cond(one_device, apart, merged)

    cols = jnp.where(x == 0, hop[0], hop[1] + hop[2])
    hop = [lax.ppermute(cols[s], "col", pairs(source, 2)) for s, source in enumerate((1, 3))]
    cols = jnp.where(x == 2, jnp.stack(hop), cols)
    swap = [(c, c ^ 1) for c in range(2 * NX)]

    z_groups = [[y * NZ + z for z in range(NZ)] for y in range(NY)]
    y_groups = [[y * NZ + z for y in range(NY)] for z in range(NZ)]
    line = lax.all_to_all(line, "row", 0, 0, axis_index_groups=z_groups)

    def gather(part):
        return lax.all_to_all(part, "row", 0, 0, axis_index_groups=y_groups)

    pivots, rows0, rows1 = fan(line)
    rows1 = gather(rows1)
    hops = [lax.ppermute(pivots, "col", pairs(0, to)) for to in (1, 3, 2)]
    piv = gather(fan_pivots(pivots, hops))
    rows0, piv = lax.optimization_barrier((rows0, piv))
    rows0 = gather(rows0)
    lead = chain(piv, lax.ppermute(piv, "col", swap))
    mult = mults(row_map, cols, lax.ppermute(cols, "col", swap), lead)
    out = last(row_map, mask, ranks, near, u, v, rows0, rows1, lead, mult)
    return out.reshape(2, 2, 1, TILE, TILE)


def solution(mesh):
    return jax.shard_map(
        body,
        mesh=mesh,
        in_specs=(
            P("row", None, "col", None, None),
            P("row", None, "col", None, None),
            P("row", None, "col", None, None),
            P("row", None, "col"),
            P("row", None, "col"),
            P(),
        ),
        out_specs=P("row", None, "col", None, None),
        check_vma=False,
    )
```

time: 152 us -> 164 us (1.079)
  blocking collectives: 0 us -> 22.5 us
  waiting for transfers between devices: 72.4 us -> 60.9 us
  Pallas kernels: 25.2 us -> 30.3 us
  local copies, waits for them, and re-layouts: 10.2 us -> 6.34 us
    all_to_all x0 -> x1, blocking collectives: none -> 22.5 us  [body(): line = lax.all_to_all(line, 'row', 0, 0, axis_index_groups=z_groups)]
    all_to_all x1 -> x0, waiting for transfers between devices: 21.2 us -> none  [body(): line = lax.all_to_all(line, 'row', 0, 0, axis_index_groups=z_groups)]
    all_to_all x1 -> x0, starting transfers between devices: 6.65 us -> none  [body(): line = lax.all_to_all(line, 'row', 0, 0, axis_index_groups=z_groups)]
    all_to_all x2 -> x3, starting transfers between devices: 9.85 us -> 16.2 us  [gather(): return lax.all_to_all(part, 'row', 0, 0, axis_index_groups=y_groups)]
    ppermute x5, waiting for transfers between devices: 11.9 us -> 17.8 us  [the longest x3 17.8 us: body(): hops = [lax.ppermute(pivots, 'col', pairs(0, to)) for to in (1, 3, 2)]]
    all_to_all x2 -> x3, waiting for transfers between devices: 12.9 us -> 18.5 us  [gather(): return lax.all_to_all(part, 'row', 0, 0, axis_index_groups=y_groups)]
    pallas_call x4 -> x6, Pallas kernels: 12 us -> 16.3 us  [the longest x1 7.78 us: last(): pl.pallas_call(last_kernel, out_shape=jax.ShapeDtypeStruct((2, 2, TILE, T...]
    broadcast_in_dim x2 -> x0, local copies, waits for them, and re-layouts: 2.71 us -> none  [gather(): part = jnp.broadcast_to(part[None], (NY, *part.shape))]
  transfers between devices with their start and end apart: 13 -> 13, of which waited for: 6 -> 5; matrix products, arithmetic and copies ran while one was open for 4% -> 2% of each run, Pallas kernels for 9% -> 10%
where the time goes in v4:
time: 164 us; the launch traced here: 163 us
  waiting for transfers between devices  60.9 us (37%)
  starting transfers between devices  36.8 us (22%)
  Pallas kernels  30.3 us (18%)
  blocking collectives  22.5 us (14%)
  local copies, waits for them, and re-layouts  6.34 us (4%)
  other arithmetic  5.14 us (3%)
    all_to_all x1, waiting for transfers between devices, scatter(): return lax.all_to_all(part, 'row', 0, 0)  23.1 us
    all_to_all x1, blocking collectives, body(): line = lax.all_to_all(line, 'row', 0, 0, axis_index_groups=z_groups)  22.5 us
    all_to_all x3, waiting for transfers between devices, gather(): return lax.all_to_all(part, 'row', 0, 0, axis_index_groups=y_groups)  18.5 us
    ppermute x3, waiting for transfers between devices, body(): hops = [lax.ppermute(pivots, 'col', pairs(0, to)) for to in (1, 3, 2)]  17.8 us
    all_to_all x3, starting transfers between devices, gather(): return lax.all_to_all(part, 'row', 0, 0, axis_index_groups=y_groups)  16.2 us
    all_to_all x1, starting transfers between devices, scatter(): return lax.all_to_all(part, 'row', 0, 0)  11.8 us
    pallas_call x1, Pallas kernels, chain(): pl.pallas_call(chain_kernel, out_shape=jax.ShapeDtypeStruct((4, TILE, TIL...  9.78 us
    pallas_call x1, Pallas kernels, last(): pl.pallas_call(last_kernel, out_shape=jax.ShapeDtypeStruct((2, 2, TILE, T...  7.78 us
  transfers between devices with their start and end apart: 13, of which 5 were waited for; matrix products, arithmetic and copies ran while one was open for 2% of the time, Pallas kernels for 10%

profile of v4, /device:TPU:12, one launch (start us, length us, event | category | flops | bytes accessed | tf_op | source)
XLA Modules:
  0.0 163.0 jit_solution(14476649110207058002)
XLA Ops:
  0.0 0.7 reshape.26
  0.8 0.0 copy-start.2
  0.8 0.0 copy-start.7
  0.8 2.9 %head.1 = bf16[32,16,1152]{2,1,0:T(8,128)(2,1)S(1)} custom-call(s32[64]{0:T(128)} %row_map.3, s32[2,2]{1,0:T(2,128)} %bitcast.27, s32[2,2]{1,0:T(2,128)} %bitcast.31, bf16[2,2,512,512]{3,2,1,0:T(8,128)(2,1)} %bitcast.14, bf16[2,2,64,512]{3,2,1,0:T(8,128)(2,1)} %bitcast.18, bf16[2,2,64,512]{3,2,1,0:T(8,128)(2,1)} %bitcast.22), custom_call_target="tpu_custom_call" | custom-call | tf_op jit(solution)/shard_map/head/pallas_call | solution.py:126
  3.6 0.6 reduce_sum.9
  4.3 1.3 compare_reduce_fusion
  5.6 0.0 copy-done.2
  5.6 0.0 copy-done.7
  6.3 42.5 %conditional.1 = (bf16[8,16,2176]{2,1,0:T(8,128)(2,1)S(1)}, bf16[2,512,640]{2,1,0:T(8,128)(2,1)}, bf16[2,512,640]{2,1,0:T(8,128)(2,1)}, bf16[2,512,640]{2,1,0:T(8,128)(2,1)}) conditional(s32[]{:T(128)} %convert_element_type.3, (bf16[32,16,1152]{2,1,0:T(8,128)(2,1)S(1)}, s32[64]{0:T(128)}, s32[2,2]{1,0:T(2,128)}, s32[2,2]{1,0:T(2,128)}, ...), branch_computations={%region_2.0_spmd, %region_3.0_spmd} | conditional | bytes 30541240 | solution.py:393
  6.3 0.0 copy-start.5
  6.3 1.0 copy-done.5
  7.3 11.8 %all-to-all-start = ((bf16[32,16,1152]{2,1,0:T(8,128)(2,1)}), bf16[32,16,1152]{2,1,0:T(8,128)(2,1)S(1)}, u32[]{:S(2)}, u32[]{:S(2)}) async-start(bf16[32,16,1152]{2,1,0:T(8,128)(2,1)} %copy-done.5), calls=%async_computation | async-start | bytes 2359296 | tf_op jit(solution)/shard_map/cond/branch_0_fun/all_to_all | solution.py:377
  19.1 0.0 copy-done.12
  19.1 0.0 copy-done.15
  19.2 0.0 copy-start.18
  19.2 2.2 %columns.2 = bf16[2,512,640]{2,1,0:T(8,128)(2,1)} custom-call(s32[2,2]{1,0:T(2,128)S(1)} %copy-done.12, s32[2,2]{1,0:T(2,128)S(1)} %copy-done.15, bf16[2,2,512,512]{3,2,1,0:T(8,128)(2,1)S(1)} %get-tuple-element.37.near, bf16[2,2,64,512]{3,2,1,0:T(8,128)(2,1)S(1)} %get-tuple-element.38.u, bf16[2,2,64,512]{3,2,1,0:T(8,128)(2,1)} %get-tuple-element.39.v), custom_call_target="tpu_custom_call" | custom-call | tf_op jit(solution)/shard_map/cond/branch_0_fun/columns/pallas_call | solution.py:152
  21.3 1.7 %collective-permute-start = (bf16[2,512,640]{2,1,0:T(8,128)(2,1)}, bf16[2,512,640]{2,1,0:T(8,128)(2,1)}, u32[]{:S(2)}, u32[]{:S(2)}) collective-permute-start(bf16[2,512,640]{2,1,0:T(8,128)(2,1)} %columns.2), channel_id=1, source_target_pairs={{0,2},{1,3},{8,10},{9,11},{16,18},{17,19},{24,26},{25,27},{32,34},... | collective-permute-start | bytes 3932168 | tf_op jit(solution)/shard_map/cond/branch_0_fun/ppermute | solution.py:381
  23.1 1.7 %collective-permute-start.1 = (bf16[2,512,640]{2,1,0:T(8,128)(2,1)}, bf16[2,512,640]{2,1,0:T(8,128)(2,1)}, u32[]{:S(2)}, u32[]{:S(2)}) collective-permute-start(bf16[2,512,640]{2,1,0:T(8,128)(2,1)} %columns.2), channel_id=1, source_target_pairs={{0,6},{1,7},{8,14},{9,15},{16,22},{17,23},{24,30},{25,31},{32,38},... | collective-permute-start | bytes 3932168 | tf_op jit(solution)/shard_map/cond/branch_0_fun/ppermute | solution.py:381
  24.8 23.1 %all-to-all-done.got0.got1 = bf16[32,16,1152]{2,1,0:T(8,128)(2,1)S(1)} async-done(((bf16[32,16,1152]{2,1,0:T(8,128)(2,1)}), bf16[32,16,1152]{2,1,0:T(8,128)(2,1)S(1)}, u32[]{:S(2)}, u32[]{:S(2)}) %all-to-all-start) | async-done | bytes 1179680 | tf_op jit(solution)/shard_map/cond/branch_0_fun/all_to_all | solution.py:377
  47.9 0.0 copy-done.18
  47.9 0.8 take.2
  48.8 0.0 collective-permute-done
  48.8 0.0 collective-permute-done.1
  48.8 0.0 copy-start.10
  48.8 0.8 copy-done.10
  49.6 22.5 %all_to_all.33.line = bf16[8,16,2176]{2,1,0:T(8,128)(2,1)S(1)} all-to-all(bf16[8,16,2176]{2,1,0:T(8,128)(2,1)} %copy-done.10), channel_id=1, replica_groups={{0,8,16,24,32,40,48,56},{64,72,80,88,96,104,112,120},{128,136,144,152,1..., dimensions={0} | all-to-all | bytes 1114112 | tf_op jit(solution)/shard_map/all_to_all | solution.py:402
  72.1 1.5 fan.1
  73.6 0.7 collective-permute-start.4
  74.3 0.7 collective-permute-start.5
  75.0 1.3 collective-permute-start.6
  76.3 0.0 collective-permute-done.4.hop1
  76.3 0.0 collective-permute-done.5.hop3
  76.3 17.7 %collective-permute-done.6.hop2 = bf16[8,16,1152]{2,1,0:T(8,128)(2,1)S(1)} collective-permute-done((bf16[8,16,1152]{2,1,0:T(8,128)(2,1)S(1)}, bf16[8,16,1152]{2,1,0:T(8,128)(2,1)S(1)}, u32[]{:S(2)}, u32[]{:S(2)}) %collective-permute-start.6) | collective-permute-done | bytes 294944 | tf_op jit(solution)/shard_map/ppermute | solution.py:409
  94.0 1.1 fan_pivots.1
  95.2 4.8 %all-to-all-start.4 = ((bf16[4,8,16,1152]{3,2,1,0:T(8,128)(2,1)}), bf16[4,8,16,1152]{3,2,1,0:T(8,128)(2,1)S(1)}, u32[]{:S(2)}, u32[]{:S(2)}) async-start(bf16[4,8,16,1152]{3,2,1,0:T(8,128)(2,1)} %fan_pivots.1), calls=%async_computation.4 | async-start | bytes 2359296 | tf_op jit(solution)/shard_map/all_to_all | solution.py:405
  100.0 1.9 %add_select_fusion = bf16[2,512,640]{2,1,0:T(8,128)(2,1)S(1)} fusion(bf16[2,512,640]{2,1,0:T(8,128)(2,1)} %get-tuple-element.62, bf16[2,512,640]{2,1,0:T(8,128)(2,1)} %get-tuple-element.63, bf16[2,512,640]{2,1,0:T(8,128)(2,1)} %get-tuple-element.64, pred[]{:T(512)S(6)} %eq.15), kind=kLoop, calls=%fused_computation.1 | loop fusion | flops 1310720 | bytes 5242881 | tf_op jit(solution)/shard_map/jit(_where)/select_n | solution.py:395
  101.9 0.0 copy-start.4
  101.9 0.1 slice_bitcast_fusion.1
  102.0 0.9 copy-done.4
  102.9 1.3 collective-permute-start.8
  104.2 1.3 collective-permute-start.9
  105.5 6.6 %all-to-all-done.4.own = bf16[4,8,16,1152]{3,2,1,0:T(8,128)(2,1)S(1)} async-done(((bf16[4,8,16,1152]{3,2,1,0:T(8,128)(2,1)}), bf16[4,8,16,1152]{3,2,1,0:T(8,128)(2,1)S(1)}, u32[]{:S(2)}, u32[]{:S(2)}) %all-to-all-start.4) | async-done | bytes 1179680 | tf_op jit(solution)/shard_map/all_to_all | solution.py:405
  112.2 0.0 collective-permute-start.7
  112.2 5.7 %all-to-all-start.6 = ((bf16[4,8,16,1024]{3,2,1,0:T(8,128)(2,1)}), bf16[4,8,16,1024]{3,2,1,0:T(8,128)(2,1)}, u32[]{:S(2)}, u32[]{:S(2)}) async-start(bf16[4,8,16,1024]{3,2,1,0:T(8,128)(2,1)} %get-tuple-element.60), calls=%async_computation.6 | async-start | bytes 2097152 | tf_op jit(solution)/shard_map/all_to_all | solution.py:405
  117.8 0.0 collective-permute-done.8
  117.9 1.4 collective-permute-done.9
  119.3 1.3 maximum_select_fusion.own
  120.6 0.1 collective-permute-start.10
  120.7 11.9 %all-to-all-done.6.rows1 = bf16[4,8,16,1024]{3,2,1,0:T(8,128)(2,1)} async-done(((bf16[4,8,16,1024]{3,2,1,0:T(8,128)(2,1)}), bf16[4,8,16,1024]{3,2,1,0:T(8,128)(2,1)}, u32[]{:S(2)}, u32[]{:S(2)}) %all-to-all-start.6) | async-done | bytes 1048608 | tf_op jit(solution)/shard_map/all_to_all | solution.py:405
  132.5 5.7 %all-to-all-start.5 = ((bf16[4,8,16,1024]{3,2,1,0:T(8,128)(2,1)}), bf16[4,8,16,1024]{3,2,1,0:T(8,128)(2,1)}, u32[]{:S(2)}, u32[]{:S(2)}) async-start(bf16[4,8,16,1024]{3,2,1,0:T(8,128)(2,1)} %get-tuple-element.59), calls=%async_computation.5 | async-start | bytes 2097152 | tf_op jit(solution)/shard_map/all_to_all | solution.py:405
  138.2 0.0 collective-permute-done.7.other
  138.2 9.8 %chain.1.lead = bf16[4,512,512]{2,1,0:T(8,128)(2,1)S(1)} custom-call(bf16[4,8,16,1152]{3,2,1,0:T(8,128)(2,1)S(1)} %all-to-all-done.4.own, bf16[4,8,16,1152]{3,2,1,0:T(8,128)(2,1)} %collective-permute-done.7.other), custom_call_target="tpu_custom_call" | custom-call | flops 7516192768 | bytes 5242880 | tf_op jit(solution)/shard_map/chain/pallas_call | solution.py:250
  148.0 0.0 copy-start.8
  148.0 0.0 copy-start.11
  148.0 0.0 copy-start.14
  148.1 0.0 collective-permute-done.10.other
  148.1 4.2 %mults.1.mult = bf16[2,2,512,512]{3,2,1,0:T(8,128)(2,1)S(1)} custom-call(s32[64]{0:T(128)S(1)} %copy-done.17, bf16[2,512,640]{2,1,0:T(8,128)(2,1)S(1)} %maximum_select_fusion.own, bf16[2,512,640]{2,1,0:T(8,128)(2,1)} %collective-permute-done.10.other, bf16[4,512,512]{2,1,0:T(8,128)(2,1)S(1)} %chain.1.lead), custom_call_target="tpu_custom_call" | custom-call | flops 1879048192 | bytes 7340032 | tf_op jit(solution)/shard_map/mults/pallas_call | solution.py:278
  152.3 0.0 copy-start
  152.3 1.3 copy-done
  153.7 1.3 copy-done.1
  155.0 0.0 all-to-all-done.5.rows0
  155.0 0.0 copy-done.11
  155.0 0.0 copy-done.14
  155.0 7.8 %last.1 = bf16[2,2,512,512]{3,2,1,0:T(8,128)(2,1)} custom-call(s32[64]{0:T(128)S(1)} %copy-done.17, s32[2,2]{1,0:T(2,128)S(1)} %bitcast.30, s32[2,2]{1,0:T(2,128)S(1)} %bitcast.34, bf16[2,2,512,512]{3,2,1,0:T(8,128)(2,1)} %bitcast.15, bf16[2,2,64,512]{3,2,1,0:T(8,128)(2,1)S(1)} %bitcast.21, bf16[2,2,64,512]{3,2,1,0:T(8,128)(2,1)S(1)} %bitcast.25, ...), custom_call_target="tpu_custom_call" | custom-call | flops 3221225472 | bytes 10485760 | tf_op jit(solution)/shard_map/last/pallas_call | solution.py:340
  (6 shorter events, 0.0 us)
Async XLA Ops:
  0.8 4.9 %copy-start.2 = (bf16[2,2,1,512,512]{4,3,2,1,0:T(8,128)(2,1)S(1)}, bf16[2,2,1,512,512]{4,3,2,1,0:T(8,128)(2,1)}, u32[]{:S(2)}) copy-start(bf16[2,2,1,512,512]{4,3,2,1,0:T(8,128)(2,1)} %param.8) | copy-start | bytes 6291460
  0.8 4.9 %copy-start.7 = (bf16[2,2,1,64,512]{4,3,2,1,0:T(8,128)(2,1)S(1)}, bf16[2,2,1,64,512]{4,3,2,1,0:T(8,128)(2,1)}, u32[]{:S(2)}) copy-start(bf16[2,2,1,64,512]{4,3,2,1,0:T(8,128)(2,1)} %param.9) | copy-start | bytes 786436
  6.3 1.0 copy-start.5
  7.3 11.9 %copy-start.12 = (s32[2,2]{1,0:T(2,128)S(1)}, s32[2,2]{1,0:T(2,128)}, u32[]{:S(2)}) copy-start(s32[2,2]{1,0:T(2,128)} %get-tuple-element.35.mask) | copy-start | bytes 52 | tf_op jit(solution)/shard_map/cond
  7.3 11.9 %copy-start.15 = (s32[2,2]{1,0:T(2,128)S(1)}, s32[2,2]{1,0:T(2,128)}, u32[]{:S(2)}) copy-start(s32[2,2]{1,0:T(2,128)} %get-tuple-element.36.ranks) | copy-start | bytes 52 | tf_op jit(solution)/shard_map/cond
  7.3 40.6 %all-to-all-start = ((bf16[32,16,1152]{2,1,0:T(8,128)(2,1)}), bf16[32,16,1152]{2,1,0:T(8,128)(2,1)S(1)}, u32[]{:S(2)}, u32[]{:S(2)}) async-start(bf16[32,16,1152]{2,1,0:T(8,128)(2,1)} %copy-done.5), calls=%async_computation | async-start | bytes 2359296 | tf_op jit(solution)/shard_map/cond/branch_0_fun/all_to_all | solution.py:377
  19.2 28.8 %copy-start.18 = (s32[64]{0:T(128)S(1)}, s32[64]{0:T(128)}, u32[]{:S(2)}) copy-start(s32[64]{0:T(128)} %get-tuple-element.33.row_map) | copy-start | bytes 772 | tf_op jit(solution)/shard_map/cond
  21.3 27.4 %collective-permute-start = (bf16[2,512,640]{2,1,0:T(8,128)(2,1)}, bf16[2,512,640]{2,1,0:T(8,128)(2,1)}, u32[]{:S(2)}, u32[]{:S(2)}) collective-permute-start(bf16[2,512,640]{2,1,0:T(8,128)(2,1)} %columns.2), channel_id=1, source_target_pairs={{0,2},{1,3},{8,10},{9,11},{16,18},{17,19},{24,26},{25,27},{32,34},... | collective-permute-start | bytes 3932168 | tf_op jit(solution)/shard_map/cond/branch_0_fun/ppermute | solution.py:381
  23.1 25.7 %collective-permute-start.1 = (bf16[2,512,640]{2,1,0:T(8,128)(2,1)}, bf16[2,512,640]{2,1,0:T(8,128)(2,1)}, u32[]{:S(2)}, u32[]{:S(2)}) collective-permute-start(bf16[2,512,640]{2,1,0:T(8,128)(2,1)} %columns.2), channel_id=1, source_target_pairs={{0,6},{1,7},{8,14},{9,15},{16,22},{17,23},{24,30},{25,31},{32,38},... | collective-permute-start | bytes 3932168 | tf_op jit(solution)/shard_map/cond/branch_0_fun/ppermute | solution.py:381
  48.8 0.8 copy-start.10
  73.6 2.7 %collective-permute-start.4 = (bf16[8,16,1152]{2,1,0:T(8,128)(2,1)S(1)}, bf16[8,16,1152]{2,1,0:T(8,128)(2,1)S(1)}, u32[]{:S(2)}, u32[]{:S(2)}) collective-permute-start(bf16[8,16,1152]{2,1,0:T(8,128)(2,1)S(1)} %get-tuple-element.58.own), channel_id=1, source_target_pairs={{0,2},{1,3},{8,10},{9,11},{16,18},{17,19},{24,26},{25,27},{32,34},... | collective-permute-start | bytes 884744 | tf_op jit(solution)/shard_map/ppermute | solution.py:409
  74.3 2.0 %collective-permute-start.5 = (bf16[8,16,1152]{2,1,0:T(8,128)(2,1)S(1)}, bf16[8,16,1152]{2,1,0:T(8,128)(2,1)S(1)}, u32[]{:S(2)}, u32[]{:S(2)}) collective-permute-start(bf16[8,16,1152]{2,1,0:T(8,128)(2,1)S(1)} %get-tuple-element.58.own), channel_id=1, source_target_pairs={{0,6},{1,7},{8,14},{9,15},{16,22},{17,23},{24,30},{25,31},{32,38},... | collective-permute-start | bytes 884744 | tf_op jit(solution)/shard_map/ppermute | solution.py:409
  75.0 19.1 %collective-permute-start.6 = (bf16[8,16,1152]{2,1,0:T(8,128)(2,1)S(1)}, bf16[8,16,1152]{2,1,0:T(8,128)(2,1)S(1)}, u32[]{:S(2)}, u32[]{:S(2)}) collective-permute-start(bf16[8,16,1152]{2,1,0:T(8,128)(2,1)S(1)} %get-tuple-element.58.own), channel_id=1, source_target_pairs={{0,4},{1,5},{8,12},{9,13},{16,20},{17,21},{24,28},{25,29},{32,36},... | collective-permute-start | bytes 884744 | tf_op jit(solution)/shard_map/ppermute | solution.py:409
  95.2 17.0 %all-to-all-start.4 = ((bf16[4,8,16,1152]{3,2,1,0:T(8,128)(2,1)}), bf16[4,8,16,1152]{3,2,1,0:T(8,128)(2,1)S(1)}, u32[]{:S(2)}, u32[]{:S(2)}) async-start(bf16[4,8,16,1152]{3,2,1,0:T(8,128)(2,1)} %fan_pivots.1), calls=%async_computation.4 | async-start | bytes 2359296 | tf_op jit(solution)/shard_map/all_to_all | solution.py:405
  101.9 1.1 copy-start.4
  102.9 14.9 %collective-permute-start.8 = (bf16[512,640]{1,0:T(8,128)(2,1)S(1)}, bf16[512,640]{1,0:T(8,128)(2,1)S(1)}, u32[]{:S(2)}, u32[]{:S(2)}) collective-permute-start(bf16[512,640]{1,0:T(8,128)(2,1)S(1)} %get-tuple-element.65), channel_id=1, source_target_pairs={{2,4},{3,5},{10,12},{11,13},{18,20},{19,21},{26,28},{27,29},{34,36... | collective-permute-start | bytes 1966088 | tf_op jit(solution)/shard_map/ppermute | solution.py:396
  104.2 15.1 %collective-permute-start.9 = (bf16[512,640]{1,0:T(8,128)(2,1)S(1)}, bf16[512,640]{1,0:T(8,128)(2,1)}, u32[]{:S(2)}, u32[]{:S(2)}) collective-permute-start(bf16[512,640]{1,0:T(8,128)(2,1)S(1)} %get-tuple-element.66), channel_id=1, source_target_pairs={{6,4},{7,5},{14,12},{15,13},{22,20},{23,21},{30,28},{31,29},{38,36... | collective-permute-start | bytes 1966088 | tf_op jit(solution)/shard_map/ppermute | solution.py:396
  112.2 26.1 %collective-permute-start.7 = (bf16[4,8,16,1152]{3,2,1,0:T(8,128)(2,1)S(1)}, bf16[4,8,16,1152]{3,2,1,0:T(8,128)(2,1)}, u32[]{:S(2)}, u32[]{:S(2)}) collective-permute-start(bf16[4,8,16,1152]{3,2,1,0:T(8,128)(2,1)S(1)} %all-to-all-done.4.own), channel_id=1, source_target_pairs={{0,1},{1,0},{2,3},{3,2},{4,5},{5,4},{6,7},{7,6},{8,9},{9,8},{10,11... | collective-permute-start | bytes 3538952 | tf_op jit(solution)/shard_map/ppermute | solution.py:413
  112.2 20.4 %all-to-all-start.6 = ((bf16[4,8,16,1024]{3,2,1,0:T(8,128)(2,1)}), bf16[4,8,16,1024]{3,2,1,0:T(8,128)(2,1)}, u32[]{:S(2)}, u32[]{:S(2)}) async-start(bf16[4,8,16,1024]{3,2,1,0:T(8,128)(2,1)} %get-tuple-element.60), calls=%async_computation.6 | async-start | bytes 2097152 | tf_op jit(solution)/shard_map/all_to_all | solution.py:405
  120.6 27.5 %collective-permute-start.10 = (bf16[2,512,640]{2,1,0:T(8,128)(2,1)S(1)}, bf16[2,512,640]{2,1,0:T(8,128)(2,1)}, u32[]{:S(2)}, u32[]{:S(2)}) collective-permute-start(bf16[2,512,640]{2,1,0:T(8,128)(2,1)S(1)} %maximum_select_fusion.own), channel_id=1, source_target_pairs={{0,1},{1,0},{2,3},{3,2},{4,5},{5,4},{6,7},{7,6},{8,9},{9,8},{10,11... | collective-permute-start | bytes 3932168 | tf_op jit(solution)/shard_map/ppermute | solution.py:414
  132.5 22.5 %all-to-all-start.5 = ((bf16[4,8,16,1024]{3,2,1,0:T(8,128)(2,1)}), bf16[4,8,16,1024]{3,2,1,0:T(8,128)(2,1)}, u32[]{:S(2)}, u32[]{:S(2)}) async-start(bf16[4,8,16,1024]{3,2,1,0:T(8,128)(2,1)} %get-tuple-element.59), calls=%async_computation.5 | async-start | bytes 2097152 | tf_op jit(solution)/shard_map/all_to_all | solution.py:405
  138.2 9.8 %copy-start.17 = (s32[64]{0:T(128)S(1)}, s32[64]{0:T(128)}, u32[]{:S(2)}) copy-start(s32[64]{0:T(128)} %row_map.3) | copy-start | bytes 772
  148.0 7.0 %copy-start.8 = (bf16[2,2,1,64,512]{4,3,2,1,0:T(8,128)(2,1)S(1)}, bf16[2,2,1,64,512]{4,3,2,1,0:T(8,128)(2,1)}, u32[]{:S(2)}) copy-start(bf16[2,2,1,64,512]{4,3,2,1,0:T(8,128)(2,1)} %param.10) | copy-start | bytes 786436
  148.0 7.0 %copy-start.11 = (s32[2,2,1]{1,2,0:T(1,128)S(1)}, s32[2,2,1]{1,2,0:T(1,128)}, u32[]{:S(2)}) copy-start(s32[2,2,1]{1,2,0:T(1,128)} %param.11) | copy-start | bytes 52
  148.0 7.0 %copy-start.14 = (s32[2,2,1]{1,2,0:T(1,128)S(1)}, s32[2,2,1]{1,2,0:T(1,128)}, u32[]{:S(2)}) copy-start(s32[2,2,1]{1,2,0:T(1,128)} %param.12) | copy-start | bytes 52
  152.3 1.4 copy-start
  153.7 1.3 copy-start.1

commit v5 on v4

--- a/solution.py
+++ b/solution.py
@@ -24,7 +24,8 @@
 SMEM = pl.BlockSpec(memory_space=pltpu.SMEM)
 VMEM = pl.BlockSpec(memory_space=pltpu.VMEM)
 ANY = pl.BlockSpec(memory_space=pl.ANY)
-PARAMS = pltpu.CompilerParams(vmem_limit_bytes=40 << 20)
+PARAMS = pltpu.CompilerParams(vmem_limit_bytes=32 << 20)
+SMALL = pltpu.CompilerParams(vmem_limit_bytes=28 << 20)
 
 
 def dot(a, b):
@@ -259,104 +260,129 @@
     )(own, other)
 
 
-def mults_kernel(row_map, own, other, lead, out, cols):
+def own_kernel(row_map, mask, ranks, near, u, v, out):
+    row = lax.axis_index("row")
+    col = lax.axis_index("col")
+    t = pl.program_id(1)
+    s = pl.program_id(0)
+    tile = near[0, 0].astype(F32) * mask[s, t].astype(F32)
+    out[0, 0] = tile + low_rank(kept_left(u[0, 0], ranks[s, t]), v[0, 0])
+
+    @pl.when(row_map[2 * row + s] == t * 2 * NX + col)
+    def _():
+        out[0, 0] += SHIFT * eye()
+
+
+def own_tiles(row_map, mask, ranks, near, u, v):
+    def tiles(height):
+        return pl.BlockSpec((1, 1, height, TILE), lambda s, t: (s, t, 0, 0))
+
+    return pl.pallas_call(
+        own_kernel,
+        grid=(2, 2),
+        out_shape=jax.ShapeDtypeStruct((2, 2, TILE, TILE), F32),
+        in_specs=[SMEM] * 3 + [tiles(TILE), tiles(KMAX), tiles(KMAX)],
+        out_specs=tiles(TILE),
+        compiler_params=SMALL,
+        cost_estimate=pl.CostEstimate(flops=4 * 2 * TILE**3, bytes_accessed=7 << 20, transcendentals=0),
+        name="own_tiles",
+    )(row_map, mask, ranks, near, u, v)
+
+
+def columns_built_kernel(row_map, own, other, first, second, cols):
     core = lax.axis_index("col") & 1
     row = lax.axis_index("row")
     cols[core] = own[...]
     cols[1 - core] = other[...]
     for s in range(2):
         held = row_map[2 * row + s]
-        first = build(cols[0, s, :, :TILE], cols[0, s, :, TILE:], held == 0).astype(BF)
-        first = dot(first, lead[0]).astype(BF)
-        second = build(cols[1, s, :, :TILE], cols[1, s, :, TILE:], held == 1)
-        second = jnp.where(held > 0, second - dot(first, lead[1]), second)
-        out[s, 0] = first
-        out[s, 1] = dot(second.astype(BF), lead[3]).astype(BF)
-
-
-def mults(row_map, own, other, lead):
+        first[s] = build(cols[0, s, :, :TILE], cols[0, s, :, TILE:], held == 0).astype(BF)
+        second[s] = build(cols[1, s, :, :TILE], cols[1, s, :, TILE:], held == 1)
+
+
+def columns_built(row_map, own, other):
+    return pl.pallas_call(
+        columns_built_kernel,
+        out_shape=(
+            jax.ShapeDtypeStruct((2, TILE, TILE), BF),
+            jax.ShapeDtypeStruct((2, TILE, TILE), F32),
+        ),
+        in_specs=[SMEM] + [VMEM] * 2,
+        out_specs=(VMEM, VMEM),
+        scratch_shapes=[pltpu.VMEM((2, 2, TILE, WIDE), BF)],
+        compiler_params=SMALL,
+        cost_estimate=pl.CostEstimate(flops=4 * 2 * TILE**3, bytes_accessed=6 << 20, transcendentals=0),
+        name="columns_built",
+    )(row_map, own, other)
+
+
+def mults_kernel(row_map, first, second, lead, out):
+    row = lax.axis_index("row")
+    for s in range(2):
+        held = row_map[2 * row + s]
+        mult = jnp.where(held > 0, dot(first[s], lead[0]), 0.0).astype(BF)
+        out[s, :, :TILE] = mult
+        tile = second[s] - dot(mult, lead[1])
+        out[s, :, TILE:] = jnp.where(held > 1, dot(tile.astype(BF), lead[3]), 0.0).astype(BF)
+
+
+def mults(row_map, first, second, lead):
     return pl.pallas_call(
         mults_kernel,
-        out_shape=jax.ShapeDtypeStruct((2, 2, TILE, TILE), BF),
+        out_shape=jax.ShapeDtypeStruct((2, TILE, 2 * TILE), BF),
         in_specs=[SMEM] + [VMEM] * 3,
         out_specs=VMEM,
-        scratch_shapes=[pltpu.VMEM((2, 2, TILE, WIDE), BF)],
-        compiler_params=PARAMS,
-        cost_estimate=pl.CostEstimate(flops=7 * 2 * TILE**3, bytes_accessed=7 << 20, transcendentals=0),
+        compiler_params=SMALL,
+        cost_estimate=pl.CostEstimate(flops=6 * 2 * TILE**3, bytes_accessed=7 << 20, transcendentals=0),
         name="mults",
-    )(row_map, own, other, lead)
-
-
-def last_kernel(
-    row_map, mask, ranks, near, u, v, rows0, rows1, lead, mult, out,
-    near_buf, u_buf, v_buf, rows_buf, lead_buf, mult_buf, out_buf, sems, out_sems,
-):
-    row = lax.axis_index("row")
+    )(row_map, first, second, lead)
+
+
+def last_kernel(rows0, rows1, own, lead, mult, out, rows_buf, pivot_rows, out_buf, sems, out_sems):
     col = lax.axis_index("col")
-    moves = {
-        "lead": (lead.at[pl.ds(1, 2)], lead_buf),
-        "rows1": (rows1, rows_buf.at[1]),
-        "u": (u, u_buf),
-        "v": (v, v_buf),
-        "near1": (near.at[:, 1], near_buf.at[1]),
-        "mult": (mult, mult_buf),
-        "rows0": (rows0, rows_buf.at[0]),
-        "near0": (near.at[:, 0], near_buf.at[0]),
+    copies = {
+        t: pltpu.make_async_copy(source, rows_buf.at[t], sems.at[t]) for t, source in ((1, rows1), (0, rows0))
     }
-    copies = {}
-    for i, (name, (source, target)) in enumerate(moves.items()):
-        copies[name] = pltpu.make_async_copy(source, target, sems.at[i])
-        copies[name].start()
+    for copy in copies.values():
+        copy.start()
     stores = []
     for t in (1, 0):
         j = t * 2 * NX + col
-        if t == 1:
-            copies["lead"].wait()
-        copies[f"rows{t}"].wait()
+        copies[t].wait()
         row0 = rows_buf[t, :, :, :, :TILE].reshape(TILE, TILE)
         if t == 0:
-            row0 = jnp.where(j == 1, lead_buf[0].astype(F32), row0.astype(F32)).astype(BF)
-        row1 = rows_buf[t, :, :, :, TILE:].reshape(TILE, TILE).astype(F32)
-        row1 = (row1 - dot(lead_buf[1], row0)).astype(BF)
-        for name in ("u", "v", "near1", "mult") if t == 1 else ("near0",):
-            copies[name].wait()
+            row0 = jnp.where(j == 1, lead[1].astype(F32), row0.astype(F32))
+            row0 = jnp.where(j > 0, row0, 0.0).astype(BF)
+        row1 = rows_buf[t, :, :, :, TILE:].reshape(TILE, TILE).astype(F32) - dot(lead[2], row0)
+        if t == 0:
+            row1 = jnp.where(j > 1, row1, 0.0)
+        pivot_rows[t, :TILE] = row0
+        pivot_rows[t, TILE:] = row1.astype(BF)
         for s in range(2):
-            held = row_map[2 * row + s]
-            tile = near_buf[t, s].astype(F32) * mask[s, t].astype(F32)
-            tile = tile + low_rank(kept_left(u_buf[s, t], ranks[s, t]), v_buf[s, t])
-            tile = tile + jnp.where(held == j, SHIFT, 0.0) * eye()
-            for k, pivot_row in enumerate((row0, row1)):
-                live = (held > k) & (j > k)
-                tile = jnp.where(live, tile - dot(mult_buf[s, k], pivot_row), tile)
-            out_buf[s, t] = tile.astype(BF)
-            store = pltpu.make_async_copy(out_buf.at[s, t], out.at[s, t], out_sems.at[s, t])
-            store.start()
-            stores.append(store)
+            out_buf[s, t] = (own[s, t] - dot(mult[s], pivot_rows[t])).astype(BF)
+            stores.append(pltpu.make_async_copy(out_buf.at[s, t], out.at[s, t], out_sems.at[s, t]))
+            stores[-1].start()
     for store in stores:
         store.wait()
 
 
-def last(row_map, mask, ranks, near, u, v, rows0, rows1, lead, mult):
+def last(rows0, rows1, own, lead, mult):
     return pl.pallas_call(
         last_kernel,
         out_shape=jax.ShapeDtypeStruct((2, 2, TILE, TILE), BF),
-        in_specs=[SMEM] * 3 + [ANY] * 7,
+        in_specs=[ANY] * 2 + [VMEM] * 3,
         out_specs=ANY,
         scratch_shapes=[
+            pltpu.VMEM((2, NY, NZ, CHUNK, 2 * TILE), BF),
+            pltpu.VMEM((2, 2 * TILE, TILE), BF),
             pltpu.VMEM((2, 2, TILE, TILE), BF),
-            pltpu.VMEM((2, 2, KMAX, TILE), BF),
-            pltpu.VMEM((2, 2, KMAX, TILE), BF),
-            pltpu.VMEM((2, NY, NZ, CHUNK, 2 * TILE), BF),
-            pltpu.VMEM((2, TILE, TILE), BF),
-            pltpu.VMEM((2, 2, TILE, TILE), BF),
-            pltpu.VMEM((2, 2, TILE, TILE), BF),
-            pltpu.SemaphoreType.DMA((8,)),
+            pltpu.SemaphoreType.DMA((2,)),
             pltpu.SemaphoreType.DMA((2, 2)),
         ],
-        compiler_params=pltpu.CompilerParams(vmem_limit_bytes=56 << 20),
+        compiler_params=SMALL,
         cost_estimate=pl.CostEstimate(flops=12 * 2 * TILE**3, bytes_accessed=10 << 20, transcendentals=0),
         name="last",
-    )(row_map, mask, ranks, near, u, v, rows0, rows1, lead, mult)
+    )(rows0, rows1, own, lead, mult)
 
 
 def pairs(source, target):
@@ -389,7 +415,9 @@
         got = scatter(send)
         return take(row_map, got, got), first_hop()
 
-    one_device = jnp.any(row_map.reshape(-1, 2).sum(axis=1) == 1)
+    device = jnp.arange(NROWS, dtype=jnp.int32) >> 1
+    apart_by = jnp.sum(jnp.where(row_map == 0, device, 0) - jnp.where(row_map == 1, device, 0))
+    one_device = apart_by == 0
     line, hop = lax.cond(one_device, apart, merged)
 
     cols = jnp.where(x == 0, hop[0], hop[1] + hop[2])
@@ -399,7 +427,9 @@
 
     z_groups = [[y * NZ + z for z in range(NZ)] for y in range(NY)]
     y_groups = [[y * NZ + z for y in range(NY)] for z in range(NZ)]
+    line, near, u, v = lax.optimization_barrier((line, near, u, v))
     line = lax.all_to_all(line, "row", 0, 0, axis_index_groups=z_groups)
+    own = own_tiles(row_map, mask, ranks, near, u, v)
 
     def gather(part):
         return lax.all_to_all(part, "row", 0, 0, axis_index_groups=y_groups)
@@ -407,12 +437,14 @@
     pivots, rows0, rows1 = fan(line)
     rows1 = gather(rows1)
     hops = [lax.ppermute(pivots, "col", pairs(0, to)) for to in (1, 3, 2)]
+    hops, rows1 = lax.optimization_barrier((hops, rows1))
     piv = gather(fan_pivots(pivots, hops))
     rows0, piv = lax.optimization_barrier((rows0, piv))
     rows0 = gather(rows0)
     lead = chain(piv, lax.ppermute(piv, "col", swap))
-    mult = mults(row_map, cols, lax.ppermute(cols, "col", swap), lead)
-    out = last(row_map, mask, ranks, near, u, v, rows0, rows1, lead, mult)
+    first, second = columns_built(row_map, cols, lax.ppermute(cols, "col", swap))
+    mult = mults(row_map, first, second, lead)
+    out = last(rows0, rows1, own, lead, mult)
     return out.reshape(2, 2, 1, TILE, TILE)
 
 

time: 164 us -> 160 us (0.976)
  the two profiles are of different devices: /device:TPU:12 before, /device:TPU:3 now
where the time goes in v5:
time: 160 us; the launch traced here: 159 us
  waiting for transfers between devices  61.4 us (38%)
  starting transfers between devices  46.7 us (29%)
  Pallas kernels  30.8 us (19%)
  local copies, waits for them, and re-layouts  13.6 us (8%)
  other arithmetic  5.05 us (3%)
    all_to_all x1, waiting for transfers between devices, scatter(): return lax.all_to_all(part, 'row', 0, 0)  22.3 us
    all_to_all x1, waiting for transfers between devices, body(): line = lax.all_to_all(line, 'row', 0, 0, axis_index_groups=z_groups)  16 us
    all_to_all x3, starting transfers between devices, gather(): return lax.all_to_all(part, 'row', 0, 0, axis_index_groups=y_groups)  12.7 us
    unnamed x34, local copies, waits for them, and re-layouts  12.5 us
    all_to_all x1, starting transfers between devices, scatter(): return lax.all_to_all(part, 'row', 0, 0)  11.2 us
    pallas_call x1, Pallas kernels, chain(): pl.pallas_call(chain_kernel, out_shape=jax.ShapeDtypeStruct((4, TILE, TIL...  9.95 us
    ppermute x2, waiting for transfers between devices, first_hop(): return [cols] + [lax.ppermute(cols, 'col', pairs(0, to)) for to in (1, 3)]  8.97 us
    all_to_all x1, starting transfers between devices, body(): line = lax.all_to_all(line, 'row', 0, 0, axis_index_groups=z_groups)  6.12 us
  transfers between devices with their start and end apart: 14, of which 6 were waited for; matrix products, arithmetic and copies ran while one was open for 2% of the time, Pallas kernels for 14%

profile of v5, /device:TPU:3, one launch (start us, length us, event | category | flops | bytes accessed | tf_op | source)
XLA Modules:
  0.0 158.7 jit_solution(15424063389163629457)
XLA Ops:
  0.0 1.3 fusion.1
  1.9 0.0 copy-start.10
  2.0 0.0 copy-start.15
  2.0 0.0 copy-start.18
  2.0 0.0 copy-start.19
  2.0 0.0 copy-start.20
  2.0 2.9 %head.1 = bf16[32,16,1152]{2,1,0:T(8,128)(2,1)S(1)} custom-call(s32[64]{0:T(128)} %row_map.5, s32[2,2]{1,0:T(2,128)} %bitcast.26, s32[2,2]{1,0:T(2,128)} %bitcast.30, bf16[2,2,512,512]{3,2,1,0:T(8,128)(2,1)} %bitcast.14, bf16[2,2,64,512]{3,2,1,0:T(8,128)(2,1)} %bitcast.18, bf16[2,2,64,512]{3,2,1,0:T(8,128)(2,1)} %bitcast.22), custom_call_target="tpu_custom_call" | custom-call | tf_op jit(solution)/shard_map/head/pallas_call | solution.py:127
  4.9 0.0 copy-done.10
  4.9 0.0 copy-done.15
  4.9 49.6 %conditional.1 = (bf16[8,16,2176]{2,1,0:T(8,128)(2,1)S(1)}, bf16[2,512,640]{2,1,0:T(8,128)(2,1)}, bf16[2,512,640]{2,1,0:T(8,128)(2,1)}, bf16[2,512,640]{2,1,0:T(8,128)(2,1)}) conditional(s32[]{:T(128)} %convert_element_type.3, (bf16[32,16,1152]{2,1,0:T(8,128)(2,1)S(1)}, s32[64]{0:T(128)S(1)}, s32[2,2]{1,0:T(2,128)S(1)}, s32[2,2]{1,0:T(2,128)S(1)}, ...), branch_computations={%region_1.2_spmd, %region_2.3_spmd} | conditional | bytes 31719684 | solution.py:421
  4.9 0.0 copy-start.13
  5.0 1.0 copy-done.13
  6.0 11.2 %all-to-all-start = ((bf16[32,16,1152]{2,1,0:T(8,128)(2,1)}), bf16[32,16,1152]{2,1,0:T(8,128)(2,1)S(1)}, u32[]{:S(2)}, u32[]{:S(2)}) async-start(bf16[32,16,1152]{2,1,0:T(8,128)(2,1)} %copy-done.13), calls=%async_computation | async-start | bytes 2359296 | tf_op jit(solution)/shard_map/cond/branch_0_fun/all_to_all | solution.py:403
  17.2 2.2 %columns.2 = bf16[2,512,640]{2,1,0:T(8,128)(2,1)} custom-call(s32[2,2]{1,0:T(2,128)S(1)} %get-tuple-element.35.mask, s32[2,2]{1,0:T(2,128)S(1)} %get-tuple-element.36.ranks, bf16[2,2,512,512]{3,2,1,0:T(8,128)(2,1)S(1)} %get-tuple-element.37.near, bf16[2,2,64,512]{3,2,1,0:T(8,128)(2,1)S(1)} %get-tuple-element.38.u, bf16[2,2,64,512]{3,2,1,0:T(8,128)(2,1)} %get-tuple-element.39.v), custom_call_target="tpu_custom_call" | custom-call | tf_op jit(solution)/shard_map/cond/branch_0_fun/columns/pallas_call | solution.py:153
  19.4 1.7 %collective-permute-start.1 = (bf16[2,512,640]{2,1,0:T(8,128)(2,1)}, bf16[2,512,640]{2,1,0:T(8,128)(2,1)}, u32[]{:S(2)}, u32[]{:S(2)}) collective-permute-start(bf16[2,512,640]{2,1,0:T(8,128)(2,1)} %columns.2), channel_id=1, source_target_pairs={{0,6},{1,7},{8,14},{9,15},{16,22},{17,23},{24,30},{25,31},{32,38},... | collective-permute-start | bytes 3932168 | tf_op jit(solution)/shard_map/cond/branch_0_fun/ppermute | solution.py:407
  21.1 1.3 collective-permute-start
  22.4 22.3 %all-to-all-done.got0.got1 = bf16[32,16,1152]{2,1,0:T(8,128)(2,1)S(1)} async-done(((bf16[32,16,1152]{2,1,0:T(8,128)(2,1)}), bf16[32,16,1152]{2,1,0:T(8,128)(2,1)S(1)}, u32[]{:S(2)}, u32[]{:S(2)}) %all-to-all-start) | async-done | bytes 1179680 | tf_op jit(solution)/shard_map/cond/branch_0_fun/all_to_all | solution.py:403
  44.7 0.8 take.2
  45.5 0.0 collective-permute-done.1
  45.6 9.0 %collective-permute-done = bf16[2,512,640]{2,1,0:T(8,128)(2,1)} collective-permute-done((bf16[2,512,640]{2,1,0:T(8,128)(2,1)}, bf16[2,512,640]{2,1,0:T(8,128)(2,1)}, u32[]{:S(2)}, u32[]{:S(2)}) %collective-permute-start) | collective-permute-done | bytes 1310752 | tf_op jit(solution)/shard_map/cond/branch_0_fun/ppermute | solution.py:407
  54.5 0.8 copy-done.17
  55.3 6.1 %all-to-all-start.3 = ((bf16[8,16,2176]{2,1,0:T(8,128)(2,1)}), bf16[8,16,2176]{2,1,0:T(8,128)(2,1)S(1)}, u32[]{:S(2)}, u32[]{:S(2)}) async-start(bf16[8,16,2176]{2,1,0:T(8,128)(2,1)} %copy-done.17), calls=%async_computation.3 | async-start | bytes 1114112 | tf_op jit(solution)/shard_map/all_to_all | solution.py:431
  61.5 16.0 %all-to-all-done.3.line = bf16[8,16,2176]{2,1,0:T(8,128)(2,1)S(1)} async-done(((bf16[8,16,2176]{2,1,0:T(8,128)(2,1)}), bf16[8,16,2176]{2,1,0:T(8,128)(2,1)S(1)}, u32[]{:S(2)}, u32[]{:S(2)}) %all-to-all-start.3) | async-done | bytes 557088 | tf_op jit(solution)/shard_map/all_to_all | solution.py:431
  77.5 1.6 %fan.1 = (bf16[8,16,1152]{2,1,0:T(8,128)(2,1)S(1)}, bf16[4,8,16,1024]{3,2,1,0:T(8,128)(2,1)}, bf16[4,8,16,1024]{3,2,1,0:T(8,128)(2,1)}) custom-call(bf16[8,16,2176]{2,1,0:T(8,128)(2,1)S(1)} %all-to-all-done.3.line), custom_call_target="tpu_custom_call" | custom-call | tf_op jit(solution)/shard_map/fan/pallas_call | solution.py:200
  79.1 4.0 %all-to-all-start.4 = ((bf16[4,8,16,1024]{3,2,1,0:T(8,128)(2,1)}), bf16[4,8,16,1024]{3,2,1,0:T(8,128)(2,1)S(1)}, u32[]{:S(2)}, u32[]{:S(2)}) async-start(bf16[4,8,16,1024]{3,2,1,0:T(8,128)(2,1)} %get-tuple-element.70), calls=%async_computation.4 | async-start | bytes 2097152 | tf_op jit(solution)/shard_map/all_to_all | solution.py:435
  83.0 1.9 %add_select_fusion = bf16[2,512,640]{2,1,0:T(8,128)(2,1)S(1)} fusion(bf16[2,512,640]{2,1,0:T(8,128)(2,1)} %get-tuple-element.80, bf16[2,512,640]{2,1,0:T(8,128)(2,1)} %get-tuple-element.81, bf16[2,512,640]{2,1,0:T(8,128)(2,1)} %get-tuple-element.82, pred[]{:T(512)S(6)} %eq.23), kind=kLoop, calls=%fused_computation.1 | loop fusion | flops 1310720 | bytes 5242881 | tf_op jit(solution)/shard_map/jit(_where)/select_n | solution.py:423
  84.9 0.0 copy-start.12
  85.0 0.7 collective-permute-start.6
  85.6 0.7 collective-permute-start.5
  86.3 1.3 collective-permute-start.4
  87.6 0.1 slice_bitcast_fusion.1
  87.8 2.1 %collective-permute-start.8 = (bf16[512,640]{1,0:T(8,128)(2,1)S(1)}, bf16[512,640]{1,0:T(8,128)(2,1)}, u32[]{:S(2)}, u32[]{:S(2)}) collective-permute-start(bf16[512,640]{1,0:T(8,128)(2,1)S(1)} %get-tuple-element.85), channel_id=1, source_target_pairs={{2,4},{3,5},{10,12},{11,13},{18,20},{19,21},{26,28},{27,29},{34,36... | collective-permute-start | bytes 1966088 | tf_op jit(solution)/shard_map/ppermute | solution.py:424
  89.9 1.5 collective-permute-start.9
  91.4 0.0 collective-permute-done.6.hop2
  91.4 0.0 collective-permute-done.5.hop3
  91.4 5.8 %collective-permute-done.4.hop1 = bf16[8,16,1152]{2,1,0:T(8,128)(2,1)S(1)} collective-permute-done((bf16[8,16,1152]{2,1,0:T(8,128)(2,1)S(1)}, bf16[8,16,1152]{2,1,0:T(8,128)(2,1)S(1)}, u32[]{:S(2)}, u32[]{:S(2)}) %collective-permute-start.4) | collective-permute-done | bytes 294944 | tf_op jit(solution)/shard_map/ppermute | solution.py:439
  97.2 0.0 all-to-all-done.4.rows1
  97.3 1.1 fan_pivots.1
  98.4 4.3 %all-to-all-start.5 = ((bf16[4,8,16,1152]{3,2,1,0:T(8,128)(2,1)}), bf16[4,8,16,1152]{3,2,1,0:T(8,128)(2,1)}, u32[]{:S(2)}, u32[]{:S(2)}) async-start(bf16[4,8,16,1152]{3,2,1,0:T(8,128)(2,1)} %fan_pivots.1), calls=%async_computation.5 | async-start | bytes 2359296 | tf_op jit(solution)/shard_map/all_to_all | solution.py:435
  102.7 2.2 %collective-permute-done.8 = bf16[512,640]{1,0:T(8,128)(2,1)} collective-permute-done((bf16[512,640]{1,0:T(8,128)(2,1)S(1)}, bf16[512,640]{1,0:T(8,128)(2,1)}, u32[]{:S(2)}, u32[]{:S(2)}) %collective-permute-start.8) | collective-permute-done | bytes 655392 | tf_op jit(solution)/shard_map/ppermute | solution.py:424
  104.9 0.0 collective-permute-done.9
  104.9 1.9 %maximum_select_fusion.own = bf16[2,512,640]{2,1,0:T(8,128)(2,1)S(1)} fusion(bf16[2,512,640]{2,1,0:T(8,128)(2,1)} %copy-done.12, bf16[1,512,640]{2,1,0:T(8,128)(2,1)} %bitcast.8, bf16[1,512,640]{2,1,0:T(8,128)(2,1)} %bitcast.6, pred[]{:T(512)S(6)} %eq.22), kind=kLoop, calls=%fused_computation | loop fusion | flops 1310720 | bytes 3932161 | tf_op jit(solution)/shard_map/jit(_where)/select_n | solution.py:425
  106.7 2.3 %collective-permute-start.10 = (bf16[2,512,640]{2,1,0:T(8,128)(2,1)S(1)}, bf16[2,512,640]{2,1,0:T(8,128)(2,1)}, u32[]{:S(2)}, u32[]{:S(2)}) collective-permute-start(bf16[2,512,640]{2,1,0:T(8,128)(2,1)S(1)} %maximum_select_fusion.own), channel_id=1, source_target_pairs={{0,1},{1,0},{2,3},{3,2},{4,5},{5,4},{6,7},{7,6},{8,9},{9,8},{10,11... | collective-permute-start | bytes 3932168 | tf_op jit(solution)/shard_map/ppermute | solution.py:445
  109.1 6.0 %all-to-all-done.5.own = bf16[4,8,16,1152]{3,2,1,0:T(8,128)(2,1)} async-done(((bf16[4,8,16,1152]{3,2,1,0:T(8,128)(2,1)}), bf16[4,8,16,1152]{3,2,1,0:T(8,128)(2,1)}, u32[]{:S(2)}, u32[]{:S(2)}) %all-to-all-start.5) | async-done | bytes 1179680 | tf_op jit(solution)/shard_map/all_to_all | solution.py:435
  115.1 5.1 %collective-permute-start.7 = (bf16[4,8,16,1152]{3,2,1,0:T(8,128)(2,1)}, bf16[4,8,16,1152]{3,2,1,0:T(8,128)(2,1)S(1)}, u32[]{:S(2)}, u32[]{:S(2)}) collective-permute-start(bf16[4,8,16,1152]{3,2,1,0:T(8,128)(2,1)} %all-to-all-done.5.own), channel_id=1, source_target_pairs={{0,1},{1,0},{2,3},{3,2},{4,5},{5,4},{6,7},{7,6},{8,9},{9,8},{10,11... | collective-permute-start | bytes 3538952 | tf_op jit(solution)/shard_map/ppermute | solution.py:444
  120.2 3.3 %own_tiles.1.own = f32[2,2,512,512]{3,2,1,0:T(8,128)S(1)} custom-call(s32[64]{0:T(128)S(1)} %copy-done.20, s32[2,2]{1,0:T(2,128)S(1)} %bitcast.29, s32[2,2]{1,0:T(2,128)S(1)} %bitcast.33, bf16[2,2,512,512]{3,2,1,0:T(8,128)(2,1)} %bitcast.15, bf16[2,2,64,512]{3,2,1,0:T(8,128)(2,1)} %bitcast.19, bf16[2,2,64,512]{3,2,1,0:T(8,128)(2,1)} %bitcast.25), custom_call_target="tpu_custom_call" | custom-call | flops 1073741824 | bytes 7340032 | tf_op jit(solution)/shard_map/own_tiles/pallas_call | solution.py:280
  123.5 1.9 %copy-done = f32[2,2,512,512]{3,2,1,0:T(8,128)} copy-done((f32[2,2,512,512]{3,2,1,0:T(8,128)}, f32[2,2,512,512]{3,2,1,0:T(8,128)S(1)}, u32[]{:S(2)}) %copy-start) | copy-done | bytes 4194328
  125.5 0.0 collective-permute-done.10.other
  125.5 2.5 %columns_built.1 = (bf16[2,512,512]{2,1,0:T(8,128)(2,1)S(1)}, f32[2,512,512]{2,1,0:T(8,128)S(1)}) custom-call(s32[64]{0:T(128)S(1)} %copy-done.20, bf16[2,512,640]{2,1,0:T(8,128)(2,1)S(1)} %maximum_select_fusion.own, bf16[2,512,640]{2,1,0:T(8,128)(2,1)} %collective-permute-done.10.other), custom_call_target="tpu_custom_call" | custom-call | flops 1073741824 | bytes 6291456 | tf_op jit(solution)/shard_map/columns_built/pallas_call | solution.py:304
  128.0 0.0 copy-start.4
  128.0 1.3 copy-done.4
  129.3 1.0 copy-done.6
  130.3 4.5 %all-to-all-start.6 = ((bf16[4,8,16,1024]{3,2,1,0:T(8,128)(2,1)}), bf16[4,8,16,1024]{3,2,1,0:T(8,128)(2,1)}, u32[]{:S(2)}, u32[]{:S(2)}) async-start(bf16[4,8,16,1024]{3,2,1,0:T(8,128)(2,1)} %get-tuple-element.74), calls=%async_computation.6 | async-start | bytes 2097152 | tf_op jit(solution)/shard_map/all_to_all | solution.py:435
  134.7 0.0 collective-permute-done.7.other
  134.8 1.0 copy-done.8
  135.8 1.3 copy-done.9
  137.1 9.9 %chain.1.lead = bf16[4,512,512]{2,1,0:T(8,128)(2,1)S(1)} custom-call(bf16[4,8,16,1152]{3,2,1,0:T(8,128)(2,1)} %all-to-all-done.5.own, bf16[4,8,16,1152]{3,2,1,0:T(8,128)(2,1)S(1)} %copy-done.9), custom_call_target="tpu_custom_call" | custom-call | flops 7516192768 | bytes 5242880 | tf_op jit(solution)/shard_map/chain/pallas_call | solution.py:251
  147.0 2.3 %mults.1.mult = bf16[2,512,1024]{2,1,0:T(8,128)(2,1)S(1)} custom-call(s32[64]{0:T(128)S(1)} %copy-done.20, bf16[2,512,512]{2,1,0:T(8,128)(2,1)S(1)} %copy-done.7, f32[2,512,512]{2,1,0:T(8,128)S(1)} %copy-done.5, bf16[4,512,512]{2,1,0:T(8,128)(2,1)S(1)} %chain.1.lead), custom_call_target="tpu_custom_call" | custom-call | flops 1610612736 | bytes 7340032 | tf_op jit(solution)/shard_map/mults/pallas_call | solution.py:330
  149.4 0.0 copy-start.2
  149.4 1.3 copy-done.2
  150.7 0.0 all-to-all-done.6.rows0
  150.7 2.2 %copy-done.1 = f32[2,2,512,512]{3,2,1,0:T(8,128)S(1)} copy-done((f32[2,2,512,512]{3,2,1,0:T(8,128)S(1)}, f32[2,2,512,512]{3,2,1,0:T(8,128)}, u32[]{:S(2)}) %copy-start.1) | copy-done | bytes 4194328
  152.9 1.6 %copy-done.3 = bf16[2,512,1024]{2,1,0:T(8,128)(2,1)S(1)} copy-done((bf16[2,512,1024]{2,1,0:T(8,128)(2,1)S(1)}, bf16[2,512,1024]{2,1,0:T(8,128)(2,1)}, u32[]{:S(2)}) %copy-start.3) | copy-done | bytes 2097176
  154.5 4.0 %last.1 = bf16[2,2,512,512]{3,2,1,0:T(8,128)(2,1)} custom-call(bf16[4,8,16,1024]{3,2,1,0:T(8,128)(2,1)} %all-to-all-done.6.rows0, bf16[4,8,16,1024]{3,2,1,0:T(8,128)(2,1)S(1)} %all-to-all-done.4.rows1, f32[2,2,512,512]{3,2,1,0:T(8,128)S(1)} %copy-done.1, bf16[4,512,512]{2,1,0:T(8,128)(2,1)S(1)} %chain.1.lead, bf16[2,512,1024]{2,1,0:T(8,128)(2,1)S(1)} %copy-done.3), custom_call_target="tpu_custom_call" | custom-call | flops 3221225472 | bytes 10485760 | tf_op jit(solution)/shard_map/last/pallas_call | solution.py:370
  (15 shorter events, 0.0 us)
Async XLA Ops:
  1.9 2.9 %copy-start.10 = (bf16[2,2,1,512,512]{4,3,2,1,0:T(8,128)(2,1)S(1)}, bf16[2,2,1,512,512]{4,3,2,1,0:T(8,128)(2,1)}, u32[]{:S(2)}) copy-start(bf16[2,2,1,512,512]{4,3,2,1,0:T(8,128)(2,1)} %param.8) | copy-start | bytes 6291460
  2.0 2.9 %copy-start.15 = (bf16[2,2,1,64,512]{4,3,2,1,0:T(8,128)(2,1)S(1)}, bf16[2,2,1,64,512]{4,3,2,1,0:T(8,128)(2,1)}, u32[]{:S(2)}) copy-start(bf16[2,2,1,64,512]{4,3,2,1,0:T(8,128)(2,1)} %param.9) | copy-start | bytes 786436
  2.0 2.9 %copy-start.18 = (s32[2,2,1]{1,2,0:T(1,128)S(1)}, s32[2,2,1]{1,2,0:T(1,128)}, u32[]{:S(2)}) copy-start(s32[2,2,1]{1,2,0:T(1,128)} %param.11) | copy-start | bytes 52
  2.0 2.9 %copy-start.19 = (s32[2,2,1]{1,2,0:T(1,128)S(1)}, s32[2,2,1]{1,2,0:T(1,128)}, u32[]{:S(2)}) copy-start(s32[2,2,1]{1,2,0:T(1,128)} %param.12) | copy-start | bytes 52
  2.0 2.9 %copy-start.20 = (s32[64]{0:T(128)S(1)}, s32[64]{0:T(128)}, u32[]{:S(2)}) copy-start(s32[64]{0:T(128)} %row_map.5) | copy-start | bytes 772
  4.9 1.0 copy-start.13
  6.0 38.7 %all-to-all-start = ((bf16[32,16,1152]{2,1,0:T(8,128)(2,1)}), bf16[32,16,1152]{2,1,0:T(8,128)(2,1)S(1)}, u32[]{:S(2)}, u32[]{:S(2)}) async-start(bf16[32,16,1152]{2,1,0:T(8,128)(2,1)} %copy-done.13), calls=%async_computation | async-start | bytes 2359296 | tf_op jit(solution)/shard_map/cond/branch_0_fun/all_to_all | solution.py:403
  19.4 26.2 %collective-permute-start.1 = (bf16[2,512,640]{2,1,0:T(8,128)(2,1)}, bf16[2,512,640]{2,1,0:T(8,128)(2,1)}, u32[]{:S(2)}, u32[]{:S(2)}) collective-permute-start(bf16[2,512,640]{2,1,0:T(8,128)(2,1)} %columns.2), channel_id=1, source_target_pairs={{0,6},{1,7},{8,14},{9,15},{16,22},{17,23},{24,30},{25,31},{32,38},... | collective-permute-start | bytes 3932168 | tf_op jit(solution)/shard_map/cond/branch_0_fun/ppermute | solution.py:407
  21.1 33.4 %collective-permute-start = (bf16[2,512,640]{2,1,0:T(8,128)(2,1)}, bf16[2,512,640]{2,1,0:T(8,128)(2,1)}, u32[]{:S(2)}, u32[]{:S(2)}) collective-permute-start(bf16[2,512,640]{2,1,0:T(8,128)(2,1)} %columns.2), channel_id=1, source_target_pairs={{0,2},{1,3},{8,10},{9,11},{16,18},{17,19},{24,26},{25,27},{32,34},... | collective-permute-start | bytes 3932168 | tf_op jit(solution)/shard_map/cond/branch_0_fun/ppermute | solution.py:407
  54.5 0.8 copy-start.17
  55.3 22.1 %all-to-all-start.3 = ((bf16[8,16,2176]{2,1,0:T(8,128)(2,1)}), bf16[8,16,2176]{2,1,0:T(8,128)(2,1)S(1)}, u32[]{:S(2)}, u32[]{:S(2)}) async-start(bf16[8,16,2176]{2,1,0:T(8,128)(2,1)} %copy-done.17), calls=%async_computation.3 | async-start | bytes 1114112 | tf_op jit(solution)/shard_map/all_to_all | solution.py:431
  79.1 18.2 %all-to-all-start.4 = ((bf16[4,8,16,1024]{3,2,1,0:T(8,128)(2,1)}), bf16[4,8,16,1024]{3,2,1,0:T(8,128)(2,1)S(1)}, u32[]{:S(2)}, u32[]{:S(2)}) async-start(bf16[4,8,16,1024]{3,2,1,0:T(8,128)(2,1)} %get-tuple-element.70), calls=%async_computation.4 | async-start | bytes 2097152 | tf_op jit(solution)/shard_map/all_to_all | solution.py:435
  84.9 2.8 %copy-start.12 = (bf16[2,512,640]{2,1,0:T(8,128)(2,1)}, bf16[2,512,640]{2,1,0:T(8,128)(2,1)S(1)}, u32[]{:S(2)}) copy-start(bf16[2,512,640]{2,1,0:T(8,128)(2,1)S(1)} %add_select_fusion) | copy-start | bytes 3932164
  85.0 6.4 %collective-permute-start.6 = (bf16[8,16,1152]{2,1,0:T(8,128)(2,1)S(1)}, bf16[8,16,1152]{2,1,0:T(8,128)(2,1)S(1)}, u32[]{:S(2)}, u32[]{:S(2)}) collective-permute-start(bf16[8,16,1152]{2,1,0:T(8,128)(2,1)S(1)} %get-tuple-element.69.own), channel_id=1, source_target_pairs={{0,4},{1,5},{8,12},{9,13},{16,20},{17,21},{24,28},{25,29},{32,36},... | collective-permute-start | bytes 884744 | tf_op jit(solution)/shard_map/ppermute | solution.py:439
  85.6 5.8 %collective-permute-start.5 = (bf16[8,16,1152]{2,1,0:T(8,128)(2,1)S(1)}, bf16[8,16,1152]{2,1,0:T(8,128)(2,1)S(1)}, u32[]{:S(2)}, u32[]{:S(2)}) collective-permute-start(bf16[8,16,1152]{2,1,0:T(8,128)(2,1)S(1)} %get-tuple-element.69.own), channel_id=1, source_target_pairs={{0,6},{1,7},{8,14},{9,15},{16,22},{17,23},{24,30},{25,31},{32,38},... | collective-permute-start | bytes 884744 | tf_op jit(solution)/shard_map/ppermute | solution.py:439
  86.3 10.9 %collective-permute-start.4 = (bf16[8,16,1152]{2,1,0:T(8,128)(2,1)S(1)}, bf16[8,16,1152]{2,1,0:T(8,128)(2,1)S(1)}, u32[]{:S(2)}, u32[]{:S(2)}) collective-permute-start(bf16[8,16,1152]{2,1,0:T(8,128)(2,1)S(1)} %get-tuple-element.69.own), channel_id=1, source_target_pairs={{0,2},{1,3},{8,10},{9,11},{16,18},{17,19},{24,26},{25,27},{32,34},... | collective-permute-start | bytes 884744 | tf_op jit(solution)/shard_map/ppermute | solution.py:439
  87.8 17.1 %collective-permute-start.8 = (bf16[512,640]{1,0:T(8,128)(2,1)S(1)}, bf16[512,640]{1,0:T(8,128)(2,1)}, u32[]{:S(2)}, u32[]{:S(2)}) collective-permute-start(bf16[512,640]{1,0:T(8,128)(2,1)S(1)} %get-tuple-element.85), channel_id=1, source_target_pairs={{2,4},{3,5},{10,12},{11,13},{18,20},{19,21},{26,28},{27,29},{34,36... | collective-permute-start | bytes 1966088 | tf_op jit(solution)/shard_map/ppermute | solution.py:424
  89.9 15.0 %collective-permute-start.9 = (bf16[512,640]{1,0:T(8,128)(2,1)S(1)}, bf16[512,640]{1,0:T(8,128)(2,1)}, u32[]{:S(2)}, u32[]{:S(2)}) collective-permute-start(bf16[512,640]{1,0:T(8,128)(2,1)S(1)} %get-tuple-element.86), channel_id=1, source_target_pairs={{6,4},{7,5},{14,12},{15,13},{22,20},{23,21},{30,28},{31,29},{38,36... | collective-permute-start | bytes 1966088 | tf_op jit(solution)/shard_map/ppermute | solution.py:424
  98.4 16.8 %all-to-all-start.5 = ((bf16[4,8,16,1152]{3,2,1,0:T(8,128)(2,1)}), bf16[4,8,16,1152]{3,2,1,0:T(8,128)(2,1)}, u32[]{:S(2)}, u32[]{:S(2)}) async-start(bf16[4,8,16,1152]{3,2,1,0:T(8,128)(2,1)} %fan_pivots.1), calls=%async_computation.5 | async-start | bytes 2359296 | tf_op jit(solution)/shard_map/all_to_all | solution.py:435
  106.7 18.7 %collective-permute-start.10 = (bf16[2,512,640]{2,1,0:T(8,128)(2,1)S(1)}, bf16[2,512,640]{2,1,0:T(8,128)(2,1)}, u32[]{:S(2)}, u32[]{:S(2)}) collective-permute-start(bf16[2,512,640]{2,1,0:T(8,128)(2,1)S(1)} %maximum_select_fusion.own), channel_id=1, source_target_pairs={{0,1},{1,0},{2,3},{3,2},{4,5},{5,4},{6,7},{7,6},{8,9},{9,8},{10,11... | collective-permute-start | bytes 3932168 | tf_op jit(solution)/shard_map/ppermute | solution.py:445
  115.1 19.6 %collective-permute-start.7 = (bf16[4,8,16,1152]{3,2,1,0:T(8,128)(2,1)}, bf16[4,8,16,1152]{3,2,1,0:T(8,128)(2,1)S(1)}, u32[]{:S(2)}, u32[]{:S(2)}) collective-permute-start(bf16[4,8,16,1152]{3,2,1,0:T(8,128)(2,1)} %all-to-all-done.5.own), channel_id=1, source_target_pairs={{0,1},{1,0},{2,3},{3,2},{4,5},{5,4},{6,7},{7,6},{8,9},{9,8},{10,11... | collective-permute-start | bytes 3538952 | tf_op jit(solution)/shard_map/ppermute | solution.py:444
  123.5 2.0 %copy-start = (f32[2,2,512,512]{3,2,1,0:T(8,128)}, f32[2,2,512,512]{3,2,1,0:T(8,128)S(1)}, u32[]{:S(2)}) copy-start(f32[2,2,512,512]{3,2,1,0:T(8,128)S(1)} %own_tiles.1.own) | copy-start | bytes 12582916
  128.0 1.3 copy-start.4
  129.3 1.0 copy-start.6
  130.3 20.4 %all-to-all-start.6 = ((bf16[4,8,16,1024]{3,2,1,0:T(8,128)(2,1)}), bf16[4,8,16,1024]{3,2,1,0:T(8,128)(2,1)}, u32[]{:S(2)}, u32[]{:S(2)}) async-start(bf16[4,8,16,1024]{3,2,1,0:T(8,128)(2,1)} %get-tuple-element.74), calls=%async_computation.6 | async-start | bytes 2097152 | tf_op jit(solution)/shard_map/all_to_all | solution.py:435
  134.7 12.3 %copy-start.7 = (bf16[2,512,512]{2,1,0:T(8,128)(2,1)S(1)}, bf16[2,512,512]{2,1,0:T(8,128)(2,1)}, u32[]{:S(2)}) copy-start(bf16[2,512,512]{2,1,0:T(8,128)(2,1)} %copy-done.6) | copy-start | bytes 3145732
  134.8 1.0 copy-start.8
  135.8 1.3 copy-start.9
  137.1 10.0 %copy-start.5 = (f32[2,512,512]{2,1,0:T(8,128)S(1)}, f32[2,512,512]{2,1,0:T(8,128)}, u32[]{:S(2)}) copy-start(f32[2,512,512]{2,1,0:T(8,128)} %copy-done.4) | copy-start | bytes 6291460
  149.4 1.3 copy-start.2
  150.7 2.2 %copy-start.1 = (f32[2,2,512,512]{3,2,1,0:T(8,128)S(1)}, f32[2,2,512,512]{3,2,1,0:T(8,128)}, u32[]{:S(2)}) copy-start(f32[2,2,512,512]{3,2,1,0:T(8,128)} %copy-done) | copy-start | bytes 12582916
  152.9 1.6 %copy-start.3 = (bf16[2,512,1024]{2,1,0:T(8,128)(2,1)S(1)}, bf16[2,512,1024]{2,1,0:T(8,128)(2,1)}, u32[]{:S(2)}) copy-start(bf16[2,512,1024]{2,1,0:T(8,128)(2,1)} %copy-done.2) | copy-start | bytes 6291460

commit v6 on v5

--- a/solution.py
+++ b/solution.py
@@ -140,25 +140,29 @@
     )(row_map, mask, ranks, near, u, v)
 
 
-def columns_kernel(mask, ranks, near, u, v, cols):
+def columns_kernel(row_map, mask, ranks, near, u, v, cols):
+    row = lax.axis_index("row")
+    col = lax.axis_index("col")
     for s in range(2):
-        cols[s, :, :TILE] = near[s, 0] * mask[s, 0].astype(F32).astype(BF)
-        cols[s, :, TILE:] = lane_blocks(kept_left(u[s, 0], ranks[s, 0]), v[s, 0])
-
-
-def columns(mask, ranks, near, u, v):
+        tile = near[s, 0].astype(F32) * mask[s, 0].astype(F32)
+        tile = tile + low_rank(kept_left(u[s, 0], ranks[s, 0]), v[s, 0])
+        tile = tile + jnp.where(row_map[2 * row + s] == col, SHIFT, 0.0) * eye()
+        cols[s] = tile.astype(BF)
+
+
+def columns(row_map, mask, ranks, near, u, v):
     def tiles(height):
         return pl.BlockSpec((2, 1, height, TILE), lambda i: (0, 0, 0, 0))
 
     return pl.pallas_call(
         columns_kernel,
         grid=(1,),
-        out_shape=jax.ShapeDtypeStruct((2, TILE, WIDE), BF),
-        in_specs=[SMEM] * 2 + [tiles(TILE), tiles(KMAX), tiles(KMAX)],
-        out_specs=pl.BlockSpec((2, TILE, WIDE), lambda i: (0, 0, 0)),
+        out_shape=jax.ShapeDtypeStruct((2, TILE, TILE), BF),
+        in_specs=[SMEM] * 3 + [tiles(TILE), tiles(KMAX), tiles(KMAX)],
+        out_specs=pl.BlockSpec((2, TILE, TILE), lambda i: (0, 0, 0)),
         compiler_params=PARAMS,
         name="columns",
-    )(mask, ranks, near, u, v)
+    )(row_map, mask, ranks, near, u, v)
 
 
 def take_kernel(row_map, got0, got1, out, chunk, sems):
@@ -231,33 +235,6 @@
         compiler_params=PARAMS,
         name="fan_pivots",
     )(own, *hops)
-
-
-def chain_kernel(own, other, out, piv):
-    core = lax.axis_index("col") & 1
-    piv[core] = own[...].reshape(TILE, FIRST)
-    piv[1 - core] = other[...].reshape(TILE, FIRST)
-    inv0 = inverse(build(piv[0, :, :TILE], piv[0, :, 2 * TILE :], True))
-    row1 = piv[1, :, :TILE]
-    mult_p1 = dot(piv[0, :, TILE : 2 * TILE], inv0).astype(BF)
-    out[0] = inv0
-    out[1] = row1
-    out[2] = mult_p1
-    pivot = build(piv[1, :, TILE : 2 * TILE], piv[1, :, 2 * TILE :], True)
-    out[3] = inverse(pivot - dot(mult_p1, row1))
-
-
-def chain(own, other):
-    return pl.pallas_call(
-        chain_kernel,
-        out_shape=jax.ShapeDtypeStruct((4, TILE, TILE), BF),
-        in_specs=[VMEM] * 2,
-        out_specs=VMEM,
-        scratch_shapes=[pltpu.VMEM((2, TILE, FIRST), BF)],
-        compiler_params=PARAMS,
-        cost_estimate=pl.CostEstimate(flops=28 * 2 * TILE**3, bytes_accessed=5 << 20, transcendentals=0),
-        name="chain",
-    )(own, other)
 
 
 def own_kernel(row_map, mask, ranks, near, u, v, out):
@@ -289,100 +266,128 @@
     )(row_map, mask, ranks, near, u, v)
 
 
-def columns_built_kernel(row_map, own, other, first, second, cols):
+def panel_kernel(
+    row_map, piv_own, piv_other, cols_own, cols_other, rows1, own, lead, mult, out,
+    piv, cols, rows, tiles, pivot_rows, out_buf, sems, out_sems,
+):
     core = lax.axis_index("col") & 1
     row = lax.axis_index("row")
-    cols[core] = own[...]
-    cols[1 - core] = other[...]
+    moves = (
+        (piv_own, piv.at[core]),
+        (piv_other, piv.at[1 - core]),
+        (cols_own, cols.at[core]),
+        (cols_other, cols.at[1 - core]),
+        (rows1, rows),
+        (own.at[:, 1], tiles),
+    )
+    copies = [pltpu.make_async_copy(*move, sems.at[i]) for i, move in enumerate(moves)]
+    for copy in copies:
+        copy.start()
+    copies[0].wait()
+    copies[1].wait()
+
+    def part(j, lanes):
+        return piv[j, :, :, :, lanes].reshape(TILE, -1)
+
+    firsts = slice(0, TILE)
+    seconds = slice(TILE, 2 * TILE)
+    factors = slice(2 * TILE, FIRST)
+    inv0 = inverse(build(part(0, firsts), part(0, factors), True))
+    row1 = part(1, firsts)
+    lead[0] = row1
+    mult_p1 = dot(part(0, seconds), inv0).astype(BF)
+    lead[1] = mult_p1
+    inv1 = inverse(build(part(1, seconds), part(1, factors), True) - dot(mult_p1, row1))
+    copies[2].wait()
+    copies[3].wait()
     for s in range(2):
         held = row_map[2 * row + s]
-        first[s] = build(cols[0, s, :, :TILE], cols[0, s, :, TILE:], held == 0).astype(BF)
-        second[s] = build(cols[1, s, :, :TILE], cols[1, s, :, TILE:], held == 1)
-
-
-def columns_built(row_map, own, other):
-    return pl.pallas_call(
-        columns_built_kernel,
+        first = jnp.where(held > 0, dot(cols[0, s], inv0), 0.0).astype(BF)
+        second = cols[1, s].astype(F32) - dot(first, row1)
+        mult[s, :, :TILE] = first
+        mult[s, :, TILE:] = jnp.where(held > 1, dot(second.astype(BF), inv1), 0.0).astype(BF)
+    copies[4].wait()
+    copies[5].wait()
+    update(rows[..., :TILE].reshape(TILE, TILE), rows, lead, mult, tiles, pivot_rows, out, out_buf, out_sems, 1)
+
+
+def update(row0, rows, lead, mult, tiles, pivot_rows, out, out_buf, out_sems, t):
+    row1 = rows[..., TILE:].reshape(TILE, TILE).astype(F32) - dot(lead[1], row0)
+    if t == 0:
+        row1 = jnp.where(lax.axis_index("col") > 1, row1, 0.0)
+    pivot_rows[:TILE] = row0
+    pivot_rows[TILE:] = row1.astype(BF)
+    stores = []
+    for s in range(2):
+        out_buf[s] = (tiles[s] - dot(mult[s], pivot_rows[...])).astype(BF)
+        stores.append(pltpu.make_async_copy(out_buf.at[s], out.at[s, t], out_sems.at[s]))
+        stores[-1].start()
+    for store in stores:
+        store.wait()
+
+
+def panel(row_map, piv_own, piv_other, cols_own, cols_other, rows1, own):
+    return pl.pallas_call(
+        panel_kernel,
         out_shape=(
             jax.ShapeDtypeStruct((2, TILE, TILE), BF),
-            jax.ShapeDtypeStruct((2, TILE, TILE), F32),
+            jax.ShapeDtypeStruct((2, TILE, 2 * TILE), BF),
+            jax.ShapeDtypeStruct((2, 2, TILE, TILE), BF),
         ),
-        in_specs=[SMEM] + [VMEM] * 2,
-        out_specs=(VMEM, VMEM),
-        scratch_shapes=[pltpu.VMEM((2, 2, TILE, WIDE), BF)],
-        compiler_params=SMALL,
-        cost_estimate=pl.CostEstimate(flops=4 * 2 * TILE**3, bytes_accessed=6 << 20, transcendentals=0),
-        name="columns_built",
-    )(row_map, own, other)
-
-
-def mults_kernel(row_map, first, second, lead, out):
-    row = lax.axis_index("row")
-    for s in range(2):
-        held = row_map[2 * row + s]
-        mult = jnp.where(held > 0, dot(first[s], lead[0]), 0.0).astype(BF)
-        out[s, :, :TILE] = mult
-        tile = second[s] - dot(mult, lead[1])
-        out[s, :, TILE:] = jnp.where(held > 1, dot(tile.astype(BF), lead[3]), 0.0).astype(BF)
-
-
-def mults(row_map, first, second, lead):
-    return pl.pallas_call(
-        mults_kernel,
-        out_shape=jax.ShapeDtypeStruct((2, TILE, 2 * TILE), BF),
-        in_specs=[SMEM] + [VMEM] * 3,
-        out_specs=VMEM,
-        compiler_params=SMALL,
-        cost_estimate=pl.CostEstimate(flops=6 * 2 * TILE**3, bytes_accessed=7 << 20, transcendentals=0),
-        name="mults",
-    )(row_map, first, second, lead)
-
-
-def last_kernel(rows0, rows1, own, lead, mult, out, rows_buf, pivot_rows, out_buf, sems, out_sems):
+        in_specs=[SMEM] + [ANY] * 6,
+        out_specs=(VMEM, VMEM, ANY),
+        scratch_shapes=[
+            pltpu.VMEM((2, NY, NZ, CHUNK, FIRST), BF),
+            pltpu.VMEM((2, 2, TILE, TILE), BF),
+            pltpu.VMEM((NY, NZ, CHUNK, 2 * TILE), BF),
+            pltpu.VMEM((2, TILE, TILE), F32),
+            pltpu.VMEM((2 * TILE, TILE), BF),
+            pltpu.VMEM((2, TILE, TILE), BF),
+            pltpu.SemaphoreType.DMA((6,)),
+            pltpu.SemaphoreType.DMA((2,)),
+        ],
+        compiler_params=PARAMS,
+        cost_estimate=pl.CostEstimate(flops=38 * 2 * TILE**3, bytes_accessed=5 << 20, transcendentals=0),
+        name="panel",
+    )(row_map, piv_own, piv_other, cols_own, cols_other, rows1, own)
+
+
+def last_kernel(rows0, own, lead, mult, begun, out, rows, tiles, pivot_rows, out_buf, sems, out_sems):
+    del begun
     col = lax.axis_index("col")
-    copies = {
-        t: pltpu.make_async_copy(source, rows_buf.at[t], sems.at[t]) for t, source in ((1, rows1), (0, rows0))
-    }
-    for copy in copies.values():
+    copies = [
+        pltpu.make_async_copy(rows0, rows, sems.at[0]),
+        pltpu.make_async_copy(own.at[:, 0], tiles, sems.at[1]),
+    ]
+    for copy in copies:
         copy.start()
-    stores = []
-    for t in (1, 0):
-        j = t * 2 * NX + col
-        copies[t].wait()
-        row0 = rows_buf[t, :, :, :, :TILE].reshape(TILE, TILE)
-        if t == 0:
-            row0 = jnp.where(j == 1, lead[1].astype(F32), row0.astype(F32))
-            row0 = jnp.where(j > 0, row0, 0.0).astype(BF)
-        row1 = rows_buf[t, :, :, :, TILE:].reshape(TILE, TILE).astype(F32) - dot(lead[2], row0)
-        if t == 0:
-            row1 = jnp.where(j > 1, row1, 0.0)
-        pivot_rows[t, :TILE] = row0
-        pivot_rows[t, TILE:] = row1.astype(BF)
-        for s in range(2):
-            out_buf[s, t] = (own[s, t] - dot(mult[s], pivot_rows[t])).astype(BF)
-            stores.append(pltpu.make_async_copy(out_buf.at[s, t], out.at[s, t], out_sems.at[s, t]))
-            stores[-1].start()
-    for store in stores:
-        store.wait()
-
-
-def last(rows0, rows1, own, lead, mult):
+    for copy in copies:
+        copy.wait()
+    row0 = rows[..., :TILE].reshape(TILE, TILE).astype(F32)
+    row0 = jnp.where(col == 1, lead[0].astype(F32), row0)
+    row0 = jnp.where(col > 0, row0, 0.0).astype(BF)
+    update(row0, rows, lead, mult, tiles, pivot_rows, out, out_buf, out_sems, 0)
+
+
+def last(rows0, own, lead, mult, begun):
     return pl.pallas_call(
         last_kernel,
         out_shape=jax.ShapeDtypeStruct((2, 2, TILE, TILE), BF),
-        in_specs=[ANY] * 2 + [VMEM] * 3,
+        in_specs=[ANY] * 2 + [VMEM] * 2 + [ANY],
         out_specs=ANY,
+        input_output_aliases={4: 0},
         scratch_shapes=[
-            pltpu.VMEM((2, NY, NZ, CHUNK, 2 * TILE), BF),
-            pltpu.VMEM((2, 2 * TILE, TILE), BF),
-            pltpu.VMEM((2, 2, TILE, TILE), BF),
+            pltpu.VMEM((NY, NZ, CHUNK, 2 * TILE), BF),
+            pltpu.VMEM((2, TILE, TILE), F32),
+            pltpu.VMEM((2 * TILE, TILE), BF),
+            pltpu.VMEM((2, TILE, TILE), BF),
             pltpu.SemaphoreType.DMA((2,)),
-            pltpu.SemaphoreType.DMA((2, 2)),
+            pltpu.SemaphoreType.DMA((2,)),
         ],
         compiler_params=SMALL,
-        cost_estimate=pl.CostEstimate(flops=12 * 2 * TILE**3, bytes_accessed=10 << 20, transcendentals=0),
+        cost_estimate=pl.CostEstimate(flops=6 * 2 * TILE**3, bytes_accessed=6 << 20, transcendentals=0),
         name="last",
-    )(rows0, rows1, own, lead, mult)
+    )(rows0, own, lead, mult, begun)
 
 
 def pairs(source, target):
@@ -402,34 +407,33 @@
     def scatter(part):
         return lax.all_to_all(part, "row", 0, 0)
 
-    def first_hop():
-        cols = columns(mask, ranks, near, u, v)
-        return [cols] + [lax.ppermute(cols, "col", pairs(0, to)) for to in (1, 3)]
+    def beside():
+        cols = columns(row_map, mask, ranks, near, u, v)
+        hop = [lax.ppermute(cols, "col", pairs(0, to)) for to in (1, 3)]
+        return cols, hop, own_tiles(row_map, mask, ranks, near, u, v)
 
     def apart():
         again = head(True, row_map, mask, ranks, near, u, v)
         got = [scatter(send), scatter(again)]
-        return take(row_map, *got), first_hop()
+        return take(row_map, *got), beside()
 
     def merged():
         got = scatter(send)
-        return take(row_map, got, got), first_hop()
+        return take(row_map, got, got), beside()
 
     device = jnp.arange(NROWS, dtype=jnp.int32) >> 1
     apart_by = jnp.sum(jnp.where(row_map == 0, device, 0) - jnp.where(row_map == 1, device, 0))
     one_device = apart_by == 0
-    line, hop = lax.cond(one_device, apart, merged)
-
-    cols = jnp.where(x == 0, hop[0], hop[1] + hop[2])
+    line, (cols, hop, own) = lax.cond(one_device, apart, merged)
+
+    cols = jnp.where(x == 0, cols, hop[0] + hop[1])
     hop = [lax.ppermute(cols[s], "col", pairs(source, 2)) for s, source in enumerate((1, 3))]
     cols = jnp.where(x == 2, jnp.stack(hop), cols)
     swap = [(c, c ^ 1) for c in range(2 * NX)]
 
     z_groups = [[y * NZ + z for z in range(NZ)] for y in range(NY)]
     y_groups = [[y * NZ + z for y in range(NY)] for z in range(NZ)]
-    line, near, u, v = lax.optimization_barrier((line, near, u, v))
     line = lax.all_to_all(line, "row", 0, 0, axis_index_groups=z_groups)
-    own = own_tiles(row_map, mask, ranks, near, u, v)
 
     def gather(part):
         return lax.all_to_all(part, "row", 0, 0, axis_index_groups=y_groups)
@@ -441,10 +445,10 @@
     piv = gather(fan_pivots(pivots, hops))
     rows0, piv = lax.optimization_barrier((rows0, piv))
     rows0 = gather(rows0)
-    lead = chain(piv, lax.ppermute(piv, "col", swap))
-    first, second = columns_built(row_map, cols, lax.ppermute(cols, "col", swap))
-    mult = mults(row_map, first, second, lead)
-    out = last(rows0, rows1, own, lead, mult)
+    piv_other = lax.ppermute(piv, "col", swap)
+    cols_other = lax.ppermute(cols, "col", swap)
+    lead, mult, begun = panel(row_map, piv, piv_other, cols, cols_other, rows1, own)
+    out = last(rows0, own, lead, mult, begun)
     return out.reshape(2, 2, 1, TILE, TILE)
 
 

time: 160 us -> 146 us (0.912)
  the two profiles are of different devices: /device:TPU:3 before, /device:TPU:12 now
where the time goes in v6:
time: 146 us; the launch traced here: 145 us
  waiting for transfers between devices  43.1 us (30%)
  starting transfers between devices  34.5 us (24%)
  Pallas kernels  32.1 us (22%)
  blocking collectives  22.5 us (15%)
  local copies, waits for them, and re-layouts  7.81 us (5%)
  other arithmetic  4.33 us (3%)
    all_to_all x1, blocking collectives, body(): line = lax.all_to_all(line, 'row', 0, 0, axis_index_groups=z_groups)  22.5 us
    all_to_all x1, waiting for transfers between devices, scatter(): return lax.all_to_all(part, 'row', 0, 0)  19.4 us
    pallas_call x1, Pallas kernels, panel(): pl.pallas_call(panel_kernel, out_shape=(jax.ShapeDtypeStruct((2, TILE, TI...  14.5 us
    all_to_all x3, starting transfers between devices, gather(): return lax.all_to_all(part, 'row', 0, 0, axis_index_groups=y_groups)  14.2 us
    ppermute x3, waiting for transfers between devices, body(): hops = [lax.ppermute(pivots, 'col', pairs(0, to)) for to in (1, 3, 2)]  12.7 us
    all_to_all x1, starting transfers between devices, scatter(): return lax.all_to_all(part, 'row', 0, 0)  11.7 us
    all_to_all x3, waiting for transfers between devices, gather(): return lax.all_to_all(part, 'row', 0, 0, axis_index_groups=y_groups)  7.12 us
    unnamed x30, local copies, waits for them, and re-layouts  6.94 us
  transfers between devices with their start and end apart: 13, of which 5 were waited for; matrix products, arithmetic and copies ran while one was open for 3% of the time, Pallas kernels for 15%

profile of v6, /device:TPU:12, one launch (start us, length us, event | category | flops | bytes accessed | tf_op | source)
XLA Modules:
  0.0 145.5 jit_solution(15608527765087565545)
XLA Ops:
  0.0 1.3 fusion.1
  1.3 0.0 copy-start.8
  1.3 0.0 copy-start.11
  1.3 0.0 copy-start.17
  1.3 3.9 %head.1 = bf16[32,16,1152]{2,1,0:T(8,128)(2,1)} custom-call(s32[64]{0:T(128)} %row_map.1, s32[2,2]{1,0:T(2,128)} %bitcast.24, s32[2,2]{1,0:T(2,128)} %bitcast.27, bf16[2,2,512,512]{3,2,1,0:T(8,128)(2,1)} %bitcast.14, bf16[2,2,64,512]{3,2,1,0:T(8,128)(2,1)} %bitcast.17, bf16[2,2,64,512]{3,2,1,0:T(8,128)(2,1)} %bitcast.20), custom_call_target="tpu_custom_call" | custom-call | tf_op jit(solution)/shard_map/head/pallas_call | solution.py:127
  5.9 0.0 copy-done.8
  5.9 0.0 copy-done.11
  5.9 0.0 copy-done.16
  5.9 0.0 copy-done.17
  5.9 0.0 copy-done.18
  6.0 41.4 %conditional.1 = (bf16[8,16,2176]{2,1,0:T(8,128)(2,1)S(1)}, bf16[2,512,512]{2,1,0:T(8,128)(2,1)}, bf16[2,512,512]{2,1,0:T(8,128)(2,1)}, bf16[2,512,512]{2,1,0:T(8,128)(2,1)}, f32[2,2,512,512]{3,2,1,0:T(8,128)}) conditional(s32[]{:T(128)} %convert_element_type.3, (bf16[32,16,1152]{2,1,0:T(8,128)(2,1)}, s32[64]{0:T(128)S(1)}, s32[2,2]{1,0:T(2,128)S(1)}, ...), branch_computations={%region_1.2_spmd, %region_2.3_spmd} | conditional | flops 1073741824 | bytes 39452908 | solution.py:427
  6.0 11.7 %all-to-all-start = ((bf16[32,16,1152]{2,1,0:T(8,128)(2,1)}), bf16[32,16,1152]{2,1,0:T(8,128)(2,1)S(1)}, u32[]{:S(2)}, u32[]{:S(2)}) async-start(bf16[32,16,1152]{2,1,0:T(8,128)(2,1)} %get-tuple-element.34), calls=%async_computation | async-start | bytes 2359296 | tf_op jit(solution)/shard_map/cond/branch_0_fun/all_to_all | solution.py:408
  17.7 0.0 copy-start.12
  17.7 2.5 %columns.2 = bf16[2,512,512]{2,1,0:T(8,128)(2,1)} custom-call(s32[64]{0:T(128)S(1)} %get-tuple-element.33.row_map, s32[2,2]{1,0:T(2,128)S(1)} %get-tuple-element.35.mask, s32[2,2]{1,0:T(2,128)S(1)} %get-tuple-element.36.ranks, bf16[2,2,512,512]{3,2,1,0:T(8,128)(2,1)S(1)} %get-tuple-element.37.near, bf16[2,2,64,512]{3,2,1,0:T(8,128)(2,1)S(1)} %get-tuple-element.38.u, ...), custom_call_target="tpu_custom_call" | custom-call | tf_op jit(solution)/shard_map/cond/branch_0_fun/columns/pallas_call | solution.py:157
  20.2 1.7 %collective-permute-start = (bf16[2,512,512]{2,1,0:T(8,128)(2,1)}, bf16[2,512,512]{2,1,0:T(8,128)(2,1)}, u32[]{:S(2)}, u32[]{:S(2)}) collective-permute-start(bf16[2,512,512]{2,1,0:T(8,128)(2,1)} %columns.2), channel_id=1, source_target_pairs={{0,2},{1,3},{8,10},{9,11},{16,18},{17,19},{24,26},{25,27},{32,34},... | collective-permute-start | bytes 3145736 | tf_op jit(solution)/shard_map/cond/branch_0_fun/ppermute | solution.py:412
  21.9 1.6 %collective-permute-start.1 = (bf16[2,512,512]{2,1,0:T(8,128)(2,1)}, bf16[2,512,512]{2,1,0:T(8,128)(2,1)}, u32[]{:S(2)}, u32[]{:S(2)}) collective-permute-start(bf16[2,512,512]{2,1,0:T(8,128)(2,1)} %columns.2), channel_id=1, source_target_pairs={{0,6},{1,7},{8,14},{9,15},{16,22},{17,23},{24,30},{25,31},{32,38},... | collective-permute-start | bytes 3145736 | tf_op jit(solution)/shard_map/cond/branch_0_fun/ppermute | solution.py:412
  23.5 0.0 copy-done.12
  23.5 3.6 %own_tiles.2 = f32[2,2,512,512]{3,2,1,0:T(8,128)} custom-call(s32[64]{0:T(128)S(1)} %get-tuple-element.33.row_map, s32[2,2]{1,0:T(2,128)S(1)} %get-tuple-element.35.mask, s32[2,2]{1,0:T(2,128)S(1)} %get-tuple-element.36.ranks, bf16[2,2,512,512]{3,2,1,0:T(8,128)(2,1)S(1)} %get-tuple-element.37.near, bf16[2,2,64,512]{3,2,1,0:T(8,128)(2,1)S(1)} %get-tuple-element.38.u, ...), custom_call_target="tpu_custom_call" | custom-call | flops 1073741824 | bytes 7340032 | tf_op jit(solution)/shard_map/cond/branch_0_fun/own_tiles/pallas_call | solution.py:257
  27.1 19.4 %all-to-all-done.got0.got1 = bf16[32,16,1152]{2,1,0:T(8,128)(2,1)S(1)} async-done(((bf16[32,16,1152]{2,1,0:T(8,128)(2,1)}), bf16[32,16,1152]{2,1,0:T(8,128)(2,1)S(1)}, u32[]{:S(2)}, u32[]{:S(2)}) %all-to-all-start) | async-done | bytes 1179680 | tf_op jit(solution)/shard_map/cond/branch_0_fun/all_to_all | solution.py:408
  46.5 0.8 take.2
  47.3 0.0 collective-permute-done
  47.3 0.0 collective-permute-done.1
  47.4 0.0 copy-start.14
  47.4 0.8 copy-done.14
  48.2 22.5 %all_to_all.33.line = bf16[8,16,2176]{2,1,0:T(8,128)(2,1)S(1)} all-to-all(bf16[8,16,2176]{2,1,0:T(8,128)(2,1)} %copy-done.14), channel_id=1, replica_groups={{0,8,16,24,32,40,48,56},{64,72,80,88,96,104,112,120},{128,136,144,152,1..., dimensions={0} | all-to-all | bytes 1114112 | tf_op jit(solution)/shard_map/all_to_all | solution.py:436
  70.7 1.5 %fan.1 = (bf16[8,16,1152]{2,1,0:T(8,128)(2,1)S(1)}, bf16[4,8,16,1024]{3,2,1,0:T(8,128)(2,1)}, bf16[4,8,16,1024]{3,2,1,0:T(8,128)(2,1)}) custom-call(bf16[8,16,2176]{2,1,0:T(8,128)(2,1)S(1)} %all_to_all.33.line), custom_call_target="tpu_custom_call" | custom-call | tf_op jit(solution)/shard_map/fan/pallas_call | solution.py:204
  72.1 4.6 %all-to-all-start.4 = ((bf16[4,8,16,1024]{3,2,1,0:T(8,128)(2,1)}), bf16[4,8,16,1024]{3,2,1,0:T(8,128)(2,1)S(1)}, u32[]{:S(2)}, u32[]{:S(2)}) async-start(bf16[4,8,16,1024]{3,2,1,0:T(8,128)(2,1)} %get-tuple-element.67), calls=%async_computation.4 | async-start | bytes 2097152 | tf_op jit(solution)/shard_map/all_to_all | solution.py:439
  76.7 0.7 collective-permute-start.4
  77.4 0.7 collective-permute-start.5
  78.1 1.3 collective-permute-start.6
  79.4 0.0 collective-permute-done.4.hop1
  79.4 0.0 collective-permute-done.5.hop3
  79.4 12.7 %collective-permute-done.6.hop2 = bf16[8,16,1152]{2,1,0:T(8,128)(2,1)S(1)} collective-permute-done((bf16[8,16,1152]{2,1,0:T(8,128)(2,1)S(1)}, bf16[8,16,1152]{2,1,0:T(8,128)(2,1)S(1)}, u32[]{:S(2)}, u32[]{:S(2)}) %collective-permute-start.6) | collective-permute-done | bytes 294944 | tf_op jit(solution)/shard_map/ppermute | solution.py:443
  92.1 0.0 all-to-all-done.4.rows1
  92.1 1.2 fan_pivots.1
  93.3 0.2 copy-done.4
  93.5 4.8 %all-to-all-start.5 = ((bf16[4,8,16,1152]{3,2,1,0:T(8,128)(2,1)}), bf16[4,8,16,1152]{3,2,1,0:T(8,128)(2,1)S(1)}, u32[]{:S(2)}, u32[]{:S(2)}) async-start(bf16[4,8,16,1152]{3,2,1,0:T(8,128)(2,1)} %fan_pivots.1), calls=%async_computation.5 | async-start | bytes 2359296 | tf_op jit(solution)/shard_map/all_to_all | solution.py:439
  98.3 1.7 %add_select_fusion = bf16[2,512,512]{2,1,0:T(8,128)(2,1)S(1)} fusion(bf16[2,512,512]{2,1,0:T(8,128)(2,1)} %get-tuple-element.74, bf16[2,512,512]{2,1,0:T(8,128)(2,1)} %get-tuple-element.75, bf16[2,512,512]{2,1,0:T(8,128)(2,1)} %get-tuple-element.76, pred[]{:T(512)S(6)} %eq.23), kind=kLoop, calls=%fused_computation.1 | loop fusion | flops 1048576 | bytes 4194305 | tf_op jit(solution)/shard_map/jit(_where)/select_n | solution.py:429
  100.0 0.9 slice_bitcast_fusion.1
  100.9 1.3 collective-permute-start.8
  102.2 1.3 collective-permute-start.9
  103.5 7.1 %all-to-all-done.5.piv_own = bf16[4,8,16,1152]{3,2,1,0:T(8,128)(2,1)S(1)} async-done(((bf16[4,8,16,1152]{3,2,1,0:T(8,128)(2,1)}), bf16[4,8,16,1152]{3,2,1,0:T(8,128)(2,1)S(1)}, u32[]{:S(2)}, u32[]{:S(2)}) %all-to-all-start.5) | async-done | bytes 1179680 | tf_op jit(solution)/shard_map/all_to_all | solution.py:439
  110.6 0.0 collective-permute-start.7
  110.6 2.7 %collective-permute-done.8 = bf16[512,512]{1,0:T(8,128)(2,1)S(1)} collective-permute-done((bf16[512,512]{1,0:T(8,128)(2,1)}, bf16[512,512]{1,0:T(8,128)(2,1)S(1)}, u32[]{:S(2)}, u32[]{:S(2)}) %collective-permute-start.8) | collective-permute-done | bytes 524320 | tf_op jit(solution)/shard_map/ppermute | solution.py:430
  113.3 1.2 collective-permute-done.9
  114.5 0.0 copy-done.15
  114.5 1.3 maximum_select_fusion.cols_own
  115.9 0.0 copy-done
  115.9 0.0 copy-start.6
  115.9 0.1 collective-permute-start.10
  116.0 4.8 %all-to-all-start.6 = ((bf16[4,8,16,1024]{3,2,1,0:T(8,128)(2,1)}), bf16[4,8,16,1024]{3,2,1,0:T(8,128)(2,1)S(1)}, u32[]{:S(2)}, u32[]{:S(2)}) async-start(bf16[4,8,16,1024]{3,2,1,0:T(8,128)(2,1)} %get-tuple-element.71), calls=%async_computation.6 | async-start | bytes 2097152 | tf_op jit(solution)/shard_map/all_to_all | solution.py:439
  120.8 0.0 collective-permute-done.10.cols_other
  120.8 0.0 collective-permute-done.7.piv_other
  120.8 0.0 copy-done.6
  120.8 0.0 copy-start.1
  120.8 1.3 copy-done.1
  122.1 1.2 copy-done.5
  123.3 1.2 copy-done.7
  124.5 14.5 %panel.1 = (bf16[2,512,512]{2,1,0:T(8,128)(2,1)S(1)}, bf16[2,512,1024]{2,1,0:T(8,128)(2,1)S(1)}, bf16[2,2,512,512]{3,2,1,0:T(8,128)(2,1)}) custom-call(s32[64]{0:T(128)S(1)} %copy-done.18, bf16[4,8,16,1152]{3,2,1,0:T(8,128)(2,1)S(1)} %copy-done.1, bf16[4,8,16,1152]{3,2,1,0:T(8,128)(2,1)} %collective-permute-done.7.piv_other, ...), custom_call_target="tpu_custom_call" | custom-call | flops 10200547328 | bytes 5242880 | tf_op jit(solution)/shard_map/panel/pallas_call | solution.py:330
  139.0 0.0 copy-start.2
  139.1 1.0 copy-done.2
  140.0 0.0 all-to-all-done.6.rows0
  140.0 1.2 copy-done.3
  141.3 4.0 %last.1 = bf16[2,2,512,512]{3,2,1,0:T(8,128)(2,1)} custom-call(bf16[4,8,16,1024]{3,2,1,0:T(8,128)(2,1)S(1)} %all-to-all-done.6.rows0, f32[2,2,512,512]{3,2,1,0:T(8,128)} %get-tuple-element.72.own, bf16[2,512,512]{2,1,0:T(8,128)(2,1)S(1)} %copy-done.3, bf16[2,512,1024]{2,1,0:T(8,128)(2,1)S(1)} %get-tuple-element.79.mult, ...), custom_call_target="tpu_custom_call", output_to_operand_aliasing={{}: (4, {})} | custom-call | flops 1610612736 | bytes 6291456 | tf_op jit(solution)/shard_map/last/pallas_call | solution.py:373
  (8 shorter events, 0.0 us)
Async XLA Ops:
  1.3 4.6 %copy-start.8 = (bf16[2,2,1,512,512]{4,3,2,1,0:T(8,128)(2,1)S(1)}, bf16[2,2,1,512,512]{4,3,2,1,0:T(8,128)(2,1)}, u32[]{:S(2)}) copy-start(bf16[2,2,1,512,512]{4,3,2,1,0:T(8,128)(2,1)} %param.8) | copy-start | bytes 6291460
  1.3 4.6 %copy-start.11 = (bf16[2,2,1,64,512]{4,3,2,1,0:T(8,128)(2,1)S(1)}, bf16[2,2,1,64,512]{4,3,2,1,0:T(8,128)(2,1)}, u32[]{:S(2)}) copy-start(bf16[2,2,1,64,512]{4,3,2,1,0:T(8,128)(2,1)} %param.9) | copy-start | bytes 786436
  1.3 4.6 %copy-start.16 = (s32[2,2,1]{1,2,0:T(1,128)S(1)}, s32[2,2,1]{1,2,0:T(1,128)}, u32[]{:S(2)}) copy-start(s32[2,2,1]{1,2,0:T(1,128)} %param.11) | copy-start | bytes 52
  1.3 4.6 %copy-start.17 = (s32[2,2,1]{1,2,0:T(1,128)S(1)}, s32[2,2,1]{1,2,0:T(1,128)}, u32[]{:S(2)}) copy-start(s32[2,2,1]{1,2,0:T(1,128)} %param.12) | copy-start | bytes 52
  1.3 4.6 %copy-start.18 = (s32[64]{0:T(128)S(1)}, s32[64]{0:T(128)}, u32[]{:S(2)}) copy-start(s32[64]{0:T(128)} %row_map.1) | copy-start | bytes 772
  6.0 40.5 %all-to-all-start = ((bf16[32,16,1152]{2,1,0:T(8,128)(2,1)}), bf16[32,16,1152]{2,1,0:T(8,128)(2,1)S(1)}, u32[]{:S(2)}, u32[]{:S(2)}) async-start(bf16[32,16,1152]{2,1,0:T(8,128)(2,1)} %get-tuple-element.34), calls=%async_computation | async-start | bytes 2359296 | tf_op jit(solution)/shard_map/cond/branch_0_fun/all_to_all | solution.py:408
  17.7 5.8 %copy-start.12 = (bf16[2,2,64,512]{3,2,1,0:T(8,128)(2,1)S(1)}, bf16[2,2,64,512]{3,2,1,0:T(8,128)(2,1)}, u32[]{:S(2)}) copy-start(bf16[2,2,64,512]{3,2,1,0:T(8,128)(2,1)} %get-tuple-element.39.v) | copy-start | bytes 786436 | tf_op jit(solution)/shard_map/cond
  20.2 27.1 %collective-permute-start = (bf16[2,512,512]{2,1,0:T(8,128)(2,1)}, bf16[2,512,512]{2,1,0:T(8,128)(2,1)}, u32[]{:S(2)}, u32[]{:S(2)}) collective-permute-start(bf16[2,512,512]{2,1,0:T(8,128)(2,1)} %columns.2), channel_id=1, source_target_pairs={{0,2},{1,3},{8,10},{9,11},{16,18},{17,19},{24,26},{25,27},{32,34},... | collective-permute-start | bytes 3145736 | tf_op jit(solution)/shard_map/cond/branch_0_fun/ppermute | solution.py:412
  21.9 25.5 %collective-permute-start.1 = (bf16[2,512,512]{2,1,0:T(8,128)(2,1)}, bf16[2,512,512]{2,1,0:T(8,128)(2,1)}, u32[]{:S(2)}, u32[]{:S(2)}) collective-permute-start(bf16[2,512,512]{2,1,0:T(8,128)(2,1)} %columns.2), channel_id=1, source_target_pairs={{0,6},{1,7},{8,14},{9,15},{16,22},{17,23},{24,30},{25,31},{32,38},... | collective-permute-start | bytes 3145736 | tf_op jit(solution)/shard_map/cond/branch_0_fun/ppermute | solution.py:412
  47.4 0.8 copy-start.14
  72.1 20.0 %all-to-all-start.4 = ((bf16[4,8,16,1024]{3,2,1,0:T(8,128)(2,1)}), bf16[4,8,16,1024]{3,2,1,0:T(8,128)(2,1)S(1)}, u32[]{:S(2)}, u32[]{:S(2)}) async-start(bf16[4,8,16,1024]{3,2,1,0:T(8,128)(2,1)} %get-tuple-element.67), calls=%async_computation.4 | async-start | bytes 2097152 | tf_op jit(solution)/shard_map/all_to_all | solution.py:439
  76.7 2.7 %collective-permute-start.4 = (bf16[8,16,1152]{2,1,0:T(8,128)(2,1)S(1)}, bf16[8,16,1152]{2,1,0:T(8,128)(2,1)S(1)}, u32[]{:S(2)}, u32[]{:S(2)}) collective-permute-start(bf16[8,16,1152]{2,1,0:T(8,128)(2,1)S(1)} %get-tuple-element.66.own), channel_id=1, source_target_pairs={{0,2},{1,3},{8,10},{9,11},{16,18},{17,19},{24,26},{25,27},{32,34},... | collective-permute-start | bytes 884744 | tf_op jit(solution)/shard_map/ppermute | solution.py:443
  77.4 2.0 %collective-permute-start.5 = (bf16[8,16,1152]{2,1,0:T(8,128)(2,1)S(1)}, bf16[8,16,1152]{2,1,0:T(8,128)(2,1)S(1)}, u32[]{:S(2)}, u32[]{:S(2)}) collective-permute-start(bf16[8,16,1152]{2,1,0:T(8,128)(2,1)S(1)} %get-tuple-element.66.own), channel_id=1, source_target_pairs={{0,6},{1,7},{8,14},{9,15},{16,22},{17,23},{24,30},{25,31},{32,38},... | collective-permute-start | bytes 884744 | tf_op jit(solution)/shard_map/ppermute | solution.py:443
  78.1 14.0 %collective-permute-start.6 = (bf16[8,16,1152]{2,1,0:T(8,128)(2,1)S(1)}, bf16[8,16,1152]{2,1,0:T(8,128)(2,1)S(1)}, u32[]{:S(2)}, u32[]{:S(2)}) collective-permute-start(bf16[8,16,1152]{2,1,0:T(8,128)(2,1)S(1)} %get-tuple-element.66.own), channel_id=1, source_target_pairs={{0,4},{1,5},{8,12},{9,13},{16,20},{17,21},{24,28},{25,29},{32,36},... | collective-permute-start | bytes 884744 | tf_op jit(solution)/shard_map/ppermute | solution.py:443
  92.1 1.4 copy-start.4
  93.5 17.1 %all-to-all-start.5 = ((bf16[4,8,16,1152]{3,2,1,0:T(8,128)(2,1)}), bf16[4,8,16,1152]{3,2,1,0:T(8,128)(2,1)S(1)}, u32[]{:S(2)}, u32[]{:S(2)}) async-start(bf16[4,8,16,1152]{3,2,1,0:T(8,128)(2,1)} %fan_pivots.1), calls=%async_computation.5 | async-start | bytes 2359296 | tf_op jit(solution)/shard_map/all_to_all | solution.py:439
  100.9 12.4 %collective-permute-start.8 = (bf16[512,512]{1,0:T(8,128)(2,1)}, bf16[512,512]{1,0:T(8,128)(2,1)S(1)}, u32[]{:S(2)}, u32[]{:S(2)}) collective-permute-start(bf16[512,512]{1,0:T(8,128)(2,1)} %get-tuple-element.81), channel_id=1, source_target_pairs={{2,4},{3,5},{10,12},{11,13},{18,20},{19,21},{26,28},{27,29},{34,36... | collective-permute-start | bytes 1572872 | tf_op jit(solution)/shard_map/ppermute | solution.py:430
  102.2 12.3 %collective-permute-start.9 = (bf16[512,512]{1,0:T(8,128)(2,1)S(1)}, bf16[512,512]{1,0:T(8,128)(2,1)}, u32[]{:S(2)}, u32[]{:S(2)}) collective-permute-start(bf16[512,512]{1,0:T(8,128)(2,1)S(1)} %get-tuple-element.82), channel_id=1, source_target_pairs={{6,4},{7,5},{14,12},{15,13},{22,20},{23,21},{30,28},{31,29},{38,36... | collective-permute-start | bytes 1572872 | tf_op jit(solution)/shard_map/ppermute | solution.py:430
  110.6 5.3 %copy-start = (bf16[4,8,16,1152]{3,2,1,0:T(8,128)(2,1)}, bf16[4,8,16,1152]{3,2,1,0:T(8,128)(2,1)S(1)}, u32[]{:S(2)}) copy-start(bf16[4,8,16,1152]{3,2,1,0:T(8,128)(2,1)S(1)} %all-to-all-done.5.piv_own) | copy-start | bytes 3538948
  110.6 10.2 %collective-permute-start.7 = (bf16[4,8,16,1152]{3,2,1,0:T(8,128)(2,1)S(1)}, bf16[4,8,16,1152]{3,2,1,0:T(8,128)(2,1)}, u32[]{:S(2)}, u32[]{:S(2)}) collective-permute-start(bf16[4,8,16,1152]{3,2,1,0:T(8,128)(2,1)S(1)} %all-to-all-done.5.piv_own), channel_id=1, source_target_pairs={{0,1},{1,0},{2,3},{3,2},{4,5},{5,4},{6,7},{7,6},{8,9},{9,8},{10,11... | collective-permute-start | bytes 3538952 | tf_op jit(solution)/shard_map/ppermute | solution.py:448
  113.3 1.2 copy-start.15
  115.9 4.9 %copy-start.6 = (bf16[2,512,512]{2,1,0:T(8,128)(2,1)}, bf16[2,512,512]{2,1,0:T(8,128)(2,1)S(1)}, u32[]{:S(2)}) copy-start(bf16[2,512,512]{2,1,0:T(8,128)(2,1)S(1)} %maximum_select_fusion.cols_own) | copy-start | bytes 3145732
  115.9 4.9 %collective-permute-start.10 = (bf16[2,512,512]{2,1,0:T(8,128)(2,1)S(1)}, bf16[2,512,512]{2,1,0:T(8,128)(2,1)}, u32[]{:S(2)}, u32[]{:S(2)}) collective-permute-start(bf16[2,512,512]{2,1,0:T(8,128)(2,1)S(1)} %maximum_select_fusion.cols_own), channel_id=1, source_target_pairs={{0,1},{1,0},{2,3},{3,2},{4,5},{5,4},{6,7},{7,6},{8,9},{9,8},{10,11... | collective-permute-start | bytes 3145736 | tf_op jit(solution)/shard_map/ppermute | solution.py:449
  116.0 24.1 %all-to-all-start.6 = ((bf16[4,8,16,1024]{3,2,1,0:T(8,128)(2,1)}), bf16[4,8,16,1024]{3,2,1,0:T(8,128)(2,1)S(1)}, u32[]{:S(2)}, u32[]{:S(2)}) async-start(bf16[4,8,16,1024]{3,2,1,0:T(8,128)(2,1)} %get-tuple-element.71), calls=%async_computation.6 | async-start | bytes 2097152 | tf_op jit(solution)/shard_map/all_to_all | solution.py:439
  120.8 1.3 copy-start.1
  122.1 1.2 copy-start.5
  123.3 1.2 copy-start.7
  139.0 1.0 copy-start.2
  140.0 1.2 copy-start.3

commit v7 on v6

--- a/solution.py
+++ b/solution.py
@@ -24,8 +24,18 @@
 SMEM = pl.BlockSpec(memory_space=pltpu.SMEM)
 VMEM = pl.BlockSpec(memory_space=pltpu.VMEM)
 ANY = pl.BlockSpec(memory_space=pl.ANY)
-PARAMS = pltpu.CompilerParams(vmem_limit_bytes=32 << 20)
-SMALL = pltpu.CompilerParams(vmem_limit_bytes=28 << 20)
+
+
+def grant(mib):
+    return pltpu.CompilerParams(vmem_limit_bytes=mib << 20)
+
+
+def in_hbm(shape, dtype=BF):
+    return pltpu.HBM(shape, dtype)
+
+
+def pin(space, *arrays):
+    return [pltpu.with_memory_space_constraint(array, space) for array in arrays]
 
 
 def dot(a, b):
@@ -38,7 +48,8 @@
 
 
 def dot_hi(a, b):
-    return dot(a[0], b[0]) + (dot(a[0], b[1]) + dot(a[1], b[0]))
+    left = jnp.concatenate([a[0], a[0], a[1]], axis=1)
+    return dot(left, jnp.concatenate([b[0], b[1], b[0]], axis=0))
 
 
 def eye():
@@ -126,7 +137,7 @@
 
     return pl.pallas_call(
         kernel,
-        out_shape=jax.ShapeDtypeStruct((PARTS, CHUNK, WIDE + TILE), BF),
+        out_shape=in_hbm((PARTS, CHUNK, WIDE + TILE)),
         in_specs=[SMEM] * 3 + [ANY] * 3,
         out_specs=VMEM,
         scratch_shapes=[
@@ -135,7 +146,7 @@
             pltpu.VMEM((2, KMAX, TILE), BF),
             pltpu.SemaphoreType.DMA((3,)),
         ],
-        compiler_params=PARAMS,
+        compiler_params=grant(12),
         name="head_again" if second else "head",
     )(row_map, mask, ranks, near, u, v)
 
@@ -157,10 +168,10 @@
     return pl.pallas_call(
         columns_kernel,
         grid=(1,),
-        out_shape=jax.ShapeDtypeStruct((2, TILE, TILE), BF),
+        out_shape=in_hbm((2, TILE, TILE)),
         in_specs=[SMEM] * 3 + [tiles(TILE), tiles(KMAX), tiles(KMAX)],
         out_specs=pl.BlockSpec((2, TILE, TILE), lambda i: (0, 0, 0)),
-        compiler_params=PARAMS,
+        compiler_params=grant(10),
         name="columns",
     )(row_map, mask, ranks, near, u, v)
 
@@ -183,11 +194,11 @@
 def take(row_map, got0, got1):
     return pl.pallas_call(
         take_kernel,
-        out_shape=jax.ShapeDtypeStruct((NZ, CHUNK, FIRST + 2 * TILE), BF),
+        out_shape=in_hbm((NZ, CHUNK, FIRST + 2 * TILE)),
         in_specs=[SMEM, ANY, ANY],
         out_specs=VMEM,
         scratch_shapes=[pltpu.VMEM((2, CHUNK, WIDE + TILE), BF), pltpu.SemaphoreType.DMA((2,))],
-        compiler_params=PARAMS,
+        compiler_params=grant(8),
         name="take",
     )(row_map, got0, got1)
 
@@ -200,13 +211,13 @@
 
 
 def fan(line):
-    rows = jax.ShapeDtypeStruct((NY, NZ, CHUNK, 2 * TILE), BF)
+    rows = in_hbm((NY, NZ, CHUNK, 2 * TILE))
     return pl.pallas_call(
         fan_kernel,
         out_shape=(jax.ShapeDtypeStruct((NZ, CHUNK, FIRST), BF), rows, rows),
         in_specs=[VMEM],
         out_specs=(VMEM,) * 3,
-        compiler_params=PARAMS,
+        compiler_params=grant(8),
         name="fan",
     )(line)
 
@@ -229,10 +240,10 @@
 def fan_pivots(own, hops):
     return pl.pallas_call(
         fan_pivots_kernel,
-        out_shape=jax.ShapeDtypeStruct((NY, NZ, CHUNK, FIRST), BF),
+        out_shape=in_hbm((NY, NZ, CHUNK, FIRST)),
         in_specs=[VMEM] * 4,
         out_specs=VMEM,
-        compiler_params=PARAMS,
+        compiler_params=grant(8),
         name="fan_pivots",
     )(own, *hops)
 
@@ -257,18 +268,34 @@
     return pl.pallas_call(
         own_kernel,
         grid=(2, 2),
-        out_shape=jax.ShapeDtypeStruct((2, 2, TILE, TILE), F32),
+        out_shape=in_hbm((2, 2, TILE, TILE), F32),
         in_specs=[SMEM] * 3 + [tiles(TILE), tiles(KMAX), tiles(KMAX)],
         out_specs=tiles(TILE),
-        compiler_params=SMALL,
+        compiler_params=grant(10),
         cost_estimate=pl.CostEstimate(flops=4 * 2 * TILE**3, bytes_accessed=7 << 20, transcendentals=0),
         name="own_tiles",
     )(row_map, mask, ranks, near, u, v)
 
 
+def second_hop_kernel(cols, hop1, hop3, out):
+    out[0] = cols[0] + hop1[...]
+    out[1] = cols[1] + hop3[...]
+
+
+def second_hop(cols, hops):
+    return pl.pallas_call(
+        second_hop_kernel,
+        out_shape=jax.ShapeDtypeStruct((2, TILE, TILE), BF),
+        in_specs=[VMEM] * 3,
+        out_specs=VMEM,
+        compiler_params=grant(8),
+        name="second_hop",
+    )(cols, *hops)
+
+
 def panel_kernel(
-    row_map, piv_own, piv_other, cols_own, cols_other, rows1, own, lead, mult, out,
-    piv, cols, rows, tiles, pivot_rows, out_buf, sems, out_sems,
+    row_map, piv_own, piv_other, cols_own, cols_other, rows1, own, mult, lead_out, out,
+    lead, piv, cols, rows, tiles, pivot_rows, out_buf, sems, out_sems,
 ):
     core = lax.axis_index("col") & 1
     row = lax.axis_index("row")
@@ -294,9 +321,10 @@
     factors = slice(2 * TILE, FIRST)
     inv0 = inverse(build(part(0, firsts), part(0, factors), True))
     row1 = part(1, firsts)
-    lead[0] = row1
     mult_p1 = dot(part(0, seconds), inv0).astype(BF)
-    lead[1] = mult_p1
+    lead[...] = mult_p1
+    store = pltpu.make_async_copy(lead, lead_out, out_sems.at[2])
+    store.start()
     inv1 = inverse(build(part(1, seconds), part(1, factors), True) - dot(mult_p1, row1))
     copies[2].wait()
     copies[3].wait()
@@ -309,14 +337,17 @@
     copies[4].wait()
     copies[5].wait()
     update(rows[..., :TILE].reshape(TILE, TILE), rows, lead, mult, tiles, pivot_rows, out, out_buf, out_sems, 1)
-
-
-def update(row0, rows, lead, mult, tiles, pivot_rows, out, out_buf, out_sems, t):
-    row1 = rows[..., TILE:].reshape(TILE, TILE).astype(F32) - dot(lead[1], row0)
+    store.wait()
+
+
+def update(row0, rows, lead, mult, tiles, pivot_rows, out, out_buf, out_sems, t, ready=()):
+    row1 = rows[..., TILE:].reshape(TILE, TILE).astype(F32) - dot(lead[...], row0)
     if t == 0:
         row1 = jnp.where(lax.axis_index("col") > 1, row1, 0.0)
     pivot_rows[:TILE] = row0
     pivot_rows[TILE:] = row1.astype(BF)
+    for copy in ready:
+        copy.wait()
     stores = []
     for s in range(2):
         out_buf[s] = (tiles[s] - dot(mult[s], pivot_rows[...])).astype(BF)
@@ -330,13 +361,14 @@
     return pl.pallas_call(
         panel_kernel,
         out_shape=(
-            jax.ShapeDtypeStruct((2, TILE, TILE), BF),
-            jax.ShapeDtypeStruct((2, TILE, 2 * TILE), BF),
-            jax.ShapeDtypeStruct((2, 2, TILE, TILE), BF),
+            pltpu.VMEM((2, TILE, 2 * TILE), BF),
+            in_hbm((TILE, TILE)),
+            in_hbm((2, 2, TILE, TILE)),
         ),
         in_specs=[SMEM] + [ANY] * 6,
-        out_specs=(VMEM, VMEM, ANY),
+        out_specs=(VMEM, ANY, ANY),
         scratch_shapes=[
+            pltpu.VMEM((TILE, TILE), BF),
             pltpu.VMEM((2, NY, NZ, CHUNK, FIRST), BF),
             pltpu.VMEM((2, 2, TILE, TILE), BF),
             pltpu.VMEM((NY, NZ, CHUNK, 2 * TILE), BF),
@@ -344,50 +376,48 @@
             pltpu.VMEM((2 * TILE, TILE), BF),
             pltpu.VMEM((2, TILE, TILE), BF),
             pltpu.SemaphoreType.DMA((6,)),
-            pltpu.SemaphoreType.DMA((2,)),
+            pltpu.SemaphoreType.DMA((3,)),
         ],
-        compiler_params=PARAMS,
+        compiler_params=grant(32),
         cost_estimate=pl.CostEstimate(flops=38 * 2 * TILE**3, bytes_accessed=5 << 20, transcendentals=0),
         name="panel",
-    )(row_map, piv_own, piv_other, cols_own, cols_other, rows1, own)
-
-
-def last_kernel(rows0, own, lead, mult, begun, out, rows, tiles, pivot_rows, out_buf, sems, out_sems):
+    )(row_map, *pin(pltpu.HBM, piv_own, piv_other, cols_own, cols_other, rows1, own))
+
+
+def last_kernel(rows, own, lead_in, mult, begun, out, lead, tiles, pivot_rows, out_buf, sems, out_sems):
     del begun
     col = lax.axis_index("col")
     copies = [
-        pltpu.make_async_copy(rows0, rows, sems.at[0]),
+        pltpu.make_async_copy(lead_in, lead, sems.at[0]),
         pltpu.make_async_copy(own.at[:, 0], tiles, sems.at[1]),
     ]
     for copy in copies:
         copy.start()
-    for copy in copies:
-        copy.wait()
     row0 = rows[..., :TILE].reshape(TILE, TILE).astype(F32)
-    row0 = jnp.where(col == 1, lead[0].astype(F32), row0)
     row0 = jnp.where(col > 0, row0, 0.0).astype(BF)
-    update(row0, rows, lead, mult, tiles, pivot_rows, out, out_buf, out_sems, 0)
+    copies[0].wait()
+    update(row0, rows, lead, mult, tiles, pivot_rows, out, out_buf, out_sems, 0, copies[1:])
 
 
 def last(rows0, own, lead, mult, begun):
     return pl.pallas_call(
         last_kernel,
-        out_shape=jax.ShapeDtypeStruct((2, 2, TILE, TILE), BF),
-        in_specs=[ANY] * 2 + [VMEM] * 2 + [ANY],
+        out_shape=in_hbm((2, 2, TILE, TILE)),
+        in_specs=[VMEM, ANY, ANY, VMEM, ANY],
         out_specs=ANY,
         input_output_aliases={4: 0},
         scratch_shapes=[
-            pltpu.VMEM((NY, NZ, CHUNK, 2 * TILE), BF),
+            pltpu.VMEM((TILE, TILE), BF),
             pltpu.VMEM((2, TILE, TILE), F32),
             pltpu.VMEM((2 * TILE, TILE), BF),
             pltpu.VMEM((2, TILE, TILE), BF),
             pltpu.SemaphoreType.DMA((2,)),
             pltpu.SemaphoreType.DMA((2,)),
         ],
-        compiler_params=SMALL,
+        compiler_params=grant(28),
         cost_estimate=pl.CostEstimate(flops=6 * 2 * TILE**3, bytes_accessed=6 << 20, transcendentals=0),
         name="last",
-    )(rows0, own, lead, mult, begun)
+    )(*pin(pltpu.VMEM, rows0), *pin(pltpu.HBM, own, lead), *pin(pltpu.VMEM, mult), *pin(pltpu.HBM, begun))
 
 
 def pairs(source, target):
@@ -426,11 +456,6 @@
     one_device = apart_by == 0
     line, (cols, hop, own) = lax.cond(one_device, apart, merged)
 
-    cols = jnp.where(x == 0, cols, hop[0] + hop[1])
-    hop = [lax.ppermute(cols[s], "col", pairs(source, 2)) for s, source in enumerate((1, 3))]
-    cols = jnp.where(x == 2, jnp.stack(hop), cols)
-    swap = [(c, c ^ 1) for c in range(2 * NX)]
-
     z_groups = [[y * NZ + z for z in range(NZ)] for y in range(NY)]
     y_groups = [[y * NZ + z for y in range(NY)] for z in range(NZ)]
     line = lax.all_to_all(line, "row", 0, 0, axis_index_groups=z_groups)
@@ -441,13 +466,17 @@
     pivots, rows0, rows1 = fan(line)
     rows1 = gather(rows1)
     hops = [lax.ppermute(pivots, "col", pairs(0, to)) for to in (1, 3, 2)]
-    hops, rows1 = lax.optimization_barrier((hops, rows1))
+    cols = jnp.where(x == 0, cols, hop[0] + hop[1])
+    hops, rows1, cols = lax.optimization_barrier((hops, rows1, cols))
+    hop = [lax.ppermute(cols[s], "col", pairs(source, 2)) for s, source in enumerate((1, 3))]
     piv = gather(fan_pivots(pivots, hops))
-    rows0, piv = lax.optimization_barrier((rows0, piv))
+    cols = second_hop(cols, hop)
+    swap = [(c, c ^ 1) for c in range(2 * NX)]
+    rows0, piv, cols = lax.optimization_barrier((rows0, piv, cols))
     rows0 = gather(rows0)
     piv_other = lax.ppermute(piv, "col", swap)
     cols_other = lax.ppermute(cols, "col", swap)
-    lead, mult, begun = panel(row_map, piv, piv_other, cols, cols_other, rows1, own)
+    mult, lead, begun = panel(row_map, piv, piv_other, cols, cols_other, rows1, own)
     out = last(rows0, own, lead, mult, begun)
     return out.reshape(2, 2, 1, TILE, TILE)
 

time: 146 us -> 137 us (0.938)
  local copies, waits for them, and re-layouts: 7.81 us -> 1.23 us
  waiting for transfers between devices: 43.1 us -> 41.2 us
    ppermute x2, waiting for transfers between devices: 3.91 us -> 11.3 us  [body(): lax.ppermute(cols[s], 'col', pairs(source, 2))]
    all_to_all x3, waiting for transfers between devices: 7.12 us -> 0.01 us  [gather(): return lax.all_to_all(part, 'row', 0, 0, axis_index_groups=y_groups)]
    unnamed x30 -> x16, local copies, waits for them, and re-layouts: 6.94 us -> 1.16 us
    ppermute x3, waiting for transfers between devices: 12.7 us -> 10.5 us  [body(): hops = [lax.ppermute(pivots, 'col', pairs(0, to)) for to in (1, 3, 2)]]
    pallas_call x7 -> x8, Pallas kernels: 30.7 us -> 31.3 us  [the longest x1 14.6 us: panel(): pl.pallas_call(panel_kernel, out_shape=(pltpu.VMEM((2, TILE, 2 * TILE), B...]
  transfers between devices with their start and end apart: 13 -> 13, of which waited for: 5 -> 4; matrix products, arithmetic and copies ran while one was open for 3% -> 1% of each run, Pallas kernels for 15% -> 16%
where the time goes in v7:
time: 137 us
  waiting for transfers between devices  41.2 us (30%)
  starting transfers between devices  35 us (26%)
  Pallas kernels  32.8 us (24%)
  blocking collectives  22.5 us (16%)
  other arithmetic  3 us (2%)
    all_to_all x1, blocking collectives, body(): line = lax.all_to_all(line, 'row', 0, 0, axis_index_groups=z_groups)  22.5 us
    all_to_all x1, waiting for transfers between devices, scatter(): return lax.all_to_all(part, 'row', 0, 0)  19.4 us
    pallas_call x1, Pallas kernels, panel(): pl.pallas_call(panel_kernel, out_shape=(pltpu.VMEM((2, TILE, 2 * TILE), B...  14.6 us
    all_to_all x3, starting transfers between devices, gather(): return lax.all_to_all(part, 'row', 0, 0, axis_index_groups=y_groups)  14.2 us
    all_to_all x1, starting transfers between devices, scatter(): return lax.all_to_all(part, 'row', 0, 0)  11.7 us
    ppermute x2, waiting for transfers between devices, body(): lax.ppermute(cols[s], 'col', pairs(source, 2))  11.3 us
    ppermute x3, waiting for transfers between devices, body(): hops = [lax.ppermute(pivots, 'col', pairs(0, to)) for to in (1, 3, 2)]  10.5 us
    pallas_call x1, Pallas kernels, head(): pl.pallas_call(kernel, out_shape=in_hbm((PARTS, CHUNK, WIDE + TILE)), in_...  3.9 us
  transfers between devices with their start and end apart: 13, of which 4 were waited for; matrix products, arithmetic and copies ran while one was open for 1% of the time, Pallas kernels for 16%

profile of v7, /device:TPU:12, one launch (start us, length us, event | category | flops | bytes accessed | tf_op | source)
XLA Modules:
  0.0 136.8 jit_solution(375239927065394584)
XLA Ops:
  0.0 1.3 fusion.1
  1.3 0.0 copy-start.1
  1.3 0.0 copy-start.4
  1.3 0.0 copy-start.8
  1.3 0.0 copy-start.9
  1.3 0.0 copy-start.10
  1.3 3.9 %head.1 = bf16[32,16,1152]{2,1,0:T(8,128)(2,1)} custom-call(s32[64]{0:T(128)} %row_map.1, s32[2,2]{1,0:T(2,128)} %bitcast.21, s32[2,2]{1,0:T(2,128)} %bitcast.24, bf16[2,2,512,512]{3,2,1,0:T(8,128)(2,1)} %bitcast.12, bf16[2,2,64,512]{3,2,1,0:T(8,128)(2,1)} %bitcast.15, bf16[2,2,64,512]{3,2,1,0:T(8,128)(2,1)} %bitcast.18), custom_call_target="tpu_custom_call" | custom-call | tf_op jit(solution)/shard_map/head/pallas_call | solution.py:138
  5.9 0.0 copy-done.1
  5.9 0.0 copy-done.4
  5.9 0.0 copy-done.8
  5.9 0.0 copy-done.9
  5.9 0.0 copy-done.10
  5.9 42.2 %conditional.1 = (bf16[8,16,2176]{2,1,0:T(8,128)(2,1)}, bf16[2,512,512]{2,1,0:T(8,128)(2,1)}, bf16[2,512,512]{2,1,0:T(8,128)(2,1)}, bf16[2,512,512]{2,1,0:T(8,128)(2,1)}, f32[2,2,512,512]{3,2,1,0:T(8,128)}) conditional(s32[]{:T(128)} %convert_element_type.3, (bf16[32,16,1152]{2,1,0:T(8,128)(2,1)}, s32[64]{0:T(128)S(1)}, s32[2,2]{1,0:T(2,128)S(1)}, ...), branch_computations={%region_1.2_spmd, %region_2.3_spmd} | conditional | flops 1073741824 | bytes 39452908 | solution.py:457
  5.9 11.7 %all-to-all-start = ((bf16[32,16,1152]{2,1,0:T(8,128)(2,1)}), bf16[32,16,1152]{2,1,0:T(8,128)(2,1)S(1)}, u32[]{:S(2)}, u32[]{:S(2)}) async-start(bf16[32,16,1152]{2,1,0:T(8,128)(2,1)} %get-tuple-element.34), calls=%async_computation | async-start | bytes 2359296 | tf_op jit(solution)/shard_map/cond/branch_0_fun/all_to_all | solution.py:438
  17.7 0.0 copy-start.5
  17.7 2.5 %columns.2 = bf16[2,512,512]{2,1,0:T(8,128)(2,1)} custom-call(s32[64]{0:T(128)S(1)} %get-tuple-element.33.row_map, s32[2,2]{1,0:T(2,128)S(1)} %get-tuple-element.35.mask, s32[2,2]{1,0:T(2,128)S(1)} %get-tuple-element.36.ranks, bf16[2,2,512,512]{3,2,1,0:T(8,128)(2,1)S(1)} %get-tuple-element.37.near, bf16[2,2,64,512]{3,2,1,0:T(8,128)(2,1)S(1)} %get-tuple-element.38.u, ...), custom_call_target="tpu_custom_call" | custom-call | tf_op jit(solution)/shard_map/cond/branch_0_fun/columns/pallas_call | solution.py:168
  20.2 1.7 %collective-permute-start = (bf16[2,512,512]{2,1,0:T(8,128)(2,1)}, bf16[2,512,512]{2,1,0:T(8,128)(2,1)}, u32[]{:S(2)}, u32[]{:S(2)}) collective-permute-start(bf16[2,512,512]{2,1,0:T(8,128)(2,1)} %columns.2), channel_id=1, source_target_pairs={{0,2},{1,3},{8,10},{9,11},{16,18},{17,19},{24,26},{25,27},{32,34},... | collective-permute-start | bytes 3145736 | tf_op jit(solution)/shard_map/cond/branch_0_fun/ppermute | solution.py:442
  21.9 1.6 %collective-permute-start.1 = (bf16[2,512,512]{2,1,0:T(8,128)(2,1)}, bf16[2,512,512]{2,1,0:T(8,128)(2,1)}, u32[]{:S(2)}, u32[]{:S(2)}) collective-permute-start(bf16[2,512,512]{2,1,0:T(8,128)(2,1)} %columns.2), channel_id=1, source_target_pairs={{0,6},{1,7},{8,14},{9,15},{16,22},{17,23},{24,30},{25,31},{32,38},... | collective-permute-start | bytes 3145736 | tf_op jit(solution)/shard_map/cond/branch_0_fun/ppermute | solution.py:442
  23.5 0.0 copy-done.5
  23.5 3.5 %own_tiles.2 = f32[2,2,512,512]{3,2,1,0:T(8,128)} custom-call(s32[64]{0:T(128)S(1)} %get-tuple-element.33.row_map, s32[2,2]{1,0:T(2,128)S(1)} %get-tuple-element.35.mask, s32[2,2]{1,0:T(2,128)S(1)} %get-tuple-element.36.ranks, bf16[2,2,512,512]{3,2,1,0:T(8,128)(2,1)S(1)} %get-tuple-element.37.near, bf16[2,2,64,512]{3,2,1,0:T(8,128)(2,1)S(1)} %get-tuple-element.38.u, ...), custom_call_target="tpu_custom_call" | custom-call | flops 1073741824 | bytes 7340032 | tf_op jit(solution)/shard_map/cond/branch_0_fun/own_tiles/pallas_call | solution.py:268
  27.0 19.4 %all-to-all-done.got0.got1 = bf16[32,16,1152]{2,1,0:T(8,128)(2,1)S(1)} async-done(((bf16[32,16,1152]{2,1,0:T(8,128)(2,1)}), bf16[32,16,1152]{2,1,0:T(8,128)(2,1)S(1)}, u32[]{:S(2)}, u32[]{:S(2)}) %all-to-all-start) | async-done | bytes 1179680 | tf_op jit(solution)/shard_map/cond/branch_0_fun/all_to_all | solution.py:438
  46.4 1.6 %take.2 = bf16[8,16,2176]{2,1,0:T(8,128)(2,1)} custom-call(s32[64]{0:T(128)S(1)} %get-tuple-element.33.row_map, bf16[32,16,1152]{2,1,0:T(8,128)(2,1)S(1)} %all-to-all-done.got0.got1, bf16[32,16,1152]{2,1,0:T(8,128)(2,1)S(1)} %all-to-all-done.got0.got1), custom_call_target="tpu_custom_call" | custom-call | tf_op jit(solution)/shard_map/cond/branch_0_fun/take/pallas_call | solution.py:195
  48.1 0.0 collective-permute-done
  48.1 0.0 collective-permute-done.1
  48.1 22.5 %all_to_all.33.line = bf16[8,16,2176]{2,1,0:T(8,128)(2,1)S(1)} all-to-all(bf16[8,16,2176]{2,1,0:T(8,128)(2,1)} %get-tuple-element.66), channel_id=1, replica_groups={{0,8,16,24,32,40,48,56},{64,72,80,88,96,104,112,120},{128,136,144,152,1..., dimensions={0} | all-to-all | bytes 1114112 | tf_op jit(solution)/shard_map/all_to_all | solution.py:461
  70.6 1.5 %fan.1 = (bf16[8,16,1152]{2,1,0:T(8,128)(2,1)S(1)}, bf16[4,8,16,1024]{3,2,1,0:T(8,128)(2,1)}, bf16[4,8,16,1024]{3,2,1,0:T(8,128)(2,1)}) custom-call(bf16[8,16,2176]{2,1,0:T(8,128)(2,1)S(1)} %all_to_all.33.line), custom_call_target="tpu_custom_call" | custom-call | tf_op jit(solution)/shard_map/fan/pallas_call | solution.py:215
  72.1 4.6 %all-to-all-start.4 = ((bf16[4,8,16,1024]{3,2,1,0:T(8,128)(2,1)}), bf16[4,8,16,1024]{3,2,1,0:T(8,128)(2,1)S(1)}, u32[]{:S(2)}, u32[]{:S(2)}) async-start(bf16[4,8,16,1024]{3,2,1,0:T(8,128)(2,1)} %get-tuple-element.69), calls=%async_computation.4 | async-start | bytes 2097152 | tf_op jit(solution)/shard_map/all_to_all | solution.py:464
  76.7 0.7 collective-permute-start.4
  77.4 0.7 collective-permute-start.5
  78.1 1.3 collective-permute-start.6
  79.4 1.7 %add_select_fusion.cols = bf16[2,512,512]{2,1,0:T(8,128)(2,1)S(1)} fusion(bf16[2,512,512]{2,1,0:T(8,128)(2,1)} %get-tuple-element.70, bf16[2,512,512]{2,1,0:T(8,128)(2,1)} %get-tuple-element.71, bf16[2,512,512]{2,1,0:T(8,128)(2,1)} %get-tuple-element.72, pred[]{:T(512)S(6)} %eq.19), kind=kLoop, calls=%fused_computation | loop fusion | flops 1048576 | bytes 4194305 | tf_op jit(solution)/shard_map/jit(_where)/select_n | solution.py:469
  81.1 0.0 collective-permute-done.4.hop1
  81.1 0.0 collective-permute-done.5.hop3
  81.1 10.5 %collective-permute-done.6.hop2 = bf16[8,16,1152]{2,1,0:T(8,128)(2,1)S(1)} collective-permute-done((bf16[8,16,1152]{2,1,0:T(8,128)(2,1)S(1)}, bf16[8,16,1152]{2,1,0:T(8,128)(2,1)S(1)}, u32[]{:S(2)}, u32[]{:S(2)}) %collective-permute-start.6) | collective-permute-done | bytes 294944 | tf_op jit(solution)/shard_map/ppermute | solution.py:468
  91.6 0.0 all-to-all-done.4.rows1
  91.6 0.0 copy-start.7
  91.6 1.2 fan_pivots.1
  92.8 0.2 copy-done.7
  93.0 4.8 %all-to-all-start.5 = ((bf16[4,8,16,1152]{3,2,1,0:T(8,128)(2,1)}), bf16[4,8,16,1152]{3,2,1,0:T(8,128)(2,1)}, u32[]{:S(2)}, u32[]{:S(2)}) async-start(bf16[4,8,16,1152]{3,2,1,0:T(8,128)(2,1)} %fan_pivots.1), calls=%async_computation.5 | async-start | bytes 2359296 | tf_op jit(solution)/shard_map/all_to_all | solution.py:464
  97.8 0.1 slice_bitcast_fusion
  97.8 1.3 collective-permute-start.7
  99.2 1.3 collective-permute-start.8
  100.5 10.0 %collective-permute-done.7.hop1 = bf16[512,512]{1,0:T(8,128)(2,1)S(1)} collective-permute-done((bf16[512,512]{1,0:T(8,128)(2,1)S(1)}, bf16[512,512]{1,0:T(8,128)(2,1)S(1)}, u32[]{:S(2)}, u32[]{:S(2)}) %collective-permute-start.7) | collective-permute-done | bytes 524320 | tf_op jit(solution)/shard_map/ppermute | solution.py:471
  110.4 1.3 collective-permute-done.8.hop3
  111.7 0.1 second_hop.1.cols_own
  111.8 0.0 copy-start
  111.8 0.0 all-to-all-done.5.piv_own
  111.9 0.1 collective-permute-start.9
  112.0 0.5 collective-permute-start.10
  112.5 4.8 %all-to-all-start.6 = ((bf16[4,8,16,1024]{3,2,1,0:T(8,128)(2,1)}), bf16[4,8,16,1024]{3,2,1,0:T(8,128)(2,1)S(1)}, u32[]{:S(2)}, u32[]{:S(2)}) async-start(bf16[4,8,16,1024]{3,2,1,0:T(8,128)(2,1)} %get-tuple-element.77), calls=%async_computation.6 | async-start | bytes 2097152 | tf_op jit(solution)/shard_map/all_to_all | solution.py:464
  117.3 0.0 collective-permute-done.10.cols_other
  117.3 0.0 copy-start.11
  117.3 0.0 collective-permute-done.9.piv_other
  117.3 0.0 copy-done
  117.3 0.9 copy-done.11
  118.2 14.6 %panel.1 = (bf16[2,512,1024]{2,1,0:T(8,128)(2,1)S(1)}, bf16[512,512]{1,0:T(8,128)(2,1)}, bf16[2,2,512,512]{3,2,1,0:T(8,128)(2,1)}) custom-call(s32[64]{0:T(128)S(1)} %copy-done.10, bf16[4,8,16,1152]{3,2,1,0:T(8,128)(2,1)} %all-to-all-done.5.piv_own, bf16[4,8,16,1152]{3,2,1,0:T(8,128)(2,1)} %collective-permute-done.9.piv_other, bf16[2,512,512]{2,1,0:T(8,128)(2,1)} %copy-done, ...), custom_call_target="tpu_custom_call" | custom-call | flops 10200547328 | bytes 5242880 | tf_op jit(solution)/shard_map/panel/pallas_call | solution.py:361
  132.8 0.0 all-to-all-done.6.rows
  132.8 3.9 %last.1 = bf16[2,2,512,512]{3,2,1,0:T(8,128)(2,1)} custom-call(bf16[4,8,16,1024]{3,2,1,0:T(8,128)(2,1)S(1)} %all-to-all-done.6.rows, f32[2,2,512,512]{3,2,1,0:T(8,128)} %get-tuple-element.78.own, bf16[512,512]{1,0:T(8,128)(2,1)} %get-tuple-element.82.lead_in, bf16[2,512,1024]{2,1,0:T(8,128)(2,1)S(1)} %get-tuple-element.83.mult, ...), custom_call_target="tpu_custom_call", output_to_operand_aliasing={{}: (4, {})} | custom-call | flops 1610612736 | bytes 6291456 | tf_op jit(solution)/shard_map/last/pallas_call | solution.py:403
Async XLA Ops:
  1.3 4.6 %copy-start.1 = (bf16[2,2,1,512,512]{4,3,2,1,0:T(8,128)(2,1)S(1)}, bf16[2,2,1,512,512]{4,3,2,1,0:T(8,128)(2,1)}, u32[]{:S(2)}) copy-start(bf16[2,2,1,512,512]{4,3,2,1,0:T(8,128)(2,1)} %param.8) | copy-start | bytes 6291460
  1.3 4.6 %copy-start.4 = (bf16[2,2,1,64,512]{4,3,2,1,0:T(8,128)(2,1)S(1)}, bf16[2,2,1,64,512]{4,3,2,1,0:T(8,128)(2,1)}, u32[]{:S(2)}) copy-start(bf16[2,2,1,64,512]{4,3,2,1,0:T(8,128)(2,1)} %param.9) | copy-start | bytes 786436
  1.3 4.6 %copy-start.8 = (s32[2,2,1]{1,2,0:T(1,128)S(1)}, s32[2,2,1]{1,2,0:T(1,128)}, u32[]{:S(2)}) copy-start(s32[2,2,1]{1,2,0:T(1,128)} %param.11) | copy-start | bytes 52
  1.3 4.6 %copy-start.9 = (s32[2,2,1]{1,2,0:T(1,128)S(1)}, s32[2,2,1]{1,2,0:T(1,128)}, u32[]{:S(2)}) copy-start(s32[2,2,1]{1,2,0:T(1,128)} %param.12) | copy-start | bytes 52
  1.3 4.6 %copy-start.10 = (s32[64]{0:T(128)S(1)}, s32[64]{0:T(128)}, u32[]{:S(2)}) copy-start(s32[64]{0:T(128)} %row_map.1) | copy-start | bytes 772
  5.9 40.5 %all-to-all-start = ((bf16[32,16,1152]{2,1,0:T(8,128)(2,1)}), bf16[32,16,1152]{2,1,0:T(8,128)(2,1)S(1)}, u32[]{:S(2)}, u32[]{:S(2)}) async-start(bf16[32,16,1152]{2,1,0:T(8,128)(2,1)} %get-tuple-element.34), calls=%async_computation | async-start | bytes 2359296 | tf_op jit(solution)/shard_map/cond/branch_0_fun/all_to_all | solution.py:438
  17.7 5.9 %copy-start.5 = (bf16[2,2,64,512]{3,2,1,0:T(8,128)(2,1)S(1)}, bf16[2,2,64,512]{3,2,1,0:T(8,128)(2,1)}, u32[]{:S(2)}) copy-start(bf16[2,2,64,512]{3,2,1,0:T(8,128)(2,1)} %get-tuple-element.39.v) | copy-start | bytes 786436 | tf_op jit(solution)/shard_map/cond
  20.2 27.9 %collective-permute-start = (bf16[2,512,512]{2,1,0:T(8,128)(2,1)}, bf16[2,512,512]{2,1,0:T(8,128)(2,1)}, u32[]{:S(2)}, u32[]{:S(2)}) collective-permute-start(bf16[2,512,512]{2,1,0:T(8,128)(2,1)} %columns.2), channel_id=1, source_target_pairs={{0,2},{1,3},{8,10},{9,11},{16,18},{17,19},{24,26},{25,27},{32,34},... | collective-permute-start | bytes 3145736 | tf_op jit(solution)/shard_map/cond/branch_0_fun/ppermute | solution.py:442
  21.9 26.2 %collective-permute-start.1 = (bf16[2,512,512]{2,1,0:T(8,128)(2,1)}, bf16[2,512,512]{2,1,0:T(8,128)(2,1)}, u32[]{:S(2)}, u32[]{:S(2)}) collective-permute-start(bf16[2,512,512]{2,1,0:T(8,128)(2,1)} %columns.2), channel_id=1, source_target_pairs={{0,6},{1,7},{8,14},{9,15},{16,22},{17,23},{24,30},{25,31},{32,38},... | collective-permute-start | bytes 3145736 | tf_op jit(solution)/shard_map/cond/branch_0_fun/ppermute | solution.py:442
  72.1 19.5 %all-to-all-start.4 = ((bf16[4,8,16,1024]{3,2,1,0:T(8,128)(2,1)}), bf16[4,8,16,1024]{3,2,1,0:T(8,128)(2,1)S(1)}, u32[]{:S(2)}, u32[]{:S(2)}) async-start(bf16[4,8,16,1024]{3,2,1,0:T(8,128)(2,1)} %get-tuple-element.69), calls=%async_computation.4 | async-start | bytes 2097152 | tf_op jit(solution)/shard_map/all_to_all | solution.py:464
  76.7 4.4 %collective-permute-start.4 = (bf16[8,16,1152]{2,1,0:T(8,128)(2,1)S(1)}, bf16[8,16,1152]{2,1,0:T(8,128)(2,1)S(1)}, u32[]{:S(2)}, u32[]{:S(2)}) collective-permute-start(bf16[8,16,1152]{2,1,0:T(8,128)(2,1)S(1)} %get-tuple-element.68.own), channel_id=1, source_target_pairs={{0,2},{1,3},{8,10},{9,11},{16,18},{17,19},{24,26},{25,27},{32,34},... | collective-permute-start | bytes 884744 | tf_op jit(solution)/shard_map/ppermute | solution.py:468
  77.4 3.7 %collective-permute-start.5 = (bf16[8,16,1152]{2,1,0:T(8,128)(2,1)S(1)}, bf16[8,16,1152]{2,1,0:T(8,128)(2,1)S(1)}, u32[]{:S(2)}, u32[]{:S(2)}) collective-permute-start(bf16[8,16,1152]{2,1,0:T(8,128)(2,1)S(1)} %get-tuple-element.68.own), channel_id=1, source_target_pairs={{0,6},{1,7},{8,14},{9,15},{16,22},{17,23},{24,30},{25,31},{32,38},... | collective-permute-start | bytes 884744 | tf_op jit(solution)/shard_map/ppermute | solution.py:468
  78.1 13.5 %collective-permute-start.6 = (bf16[8,16,1152]{2,1,0:T(8,128)(2,1)S(1)}, bf16[8,16,1152]{2,1,0:T(8,128)(2,1)S(1)}, u32[]{:S(2)}, u32[]{:S(2)}) collective-permute-start(bf16[8,16,1152]{2,1,0:T(8,128)(2,1)S(1)} %get-tuple-element.68.own), channel_id=1, source_target_pairs={{0,4},{1,5},{8,12},{9,13},{16,20},{17,21},{24,28},{25,29},{32,36},... | collective-permute-start | bytes 884744 | tf_op jit(solution)/shard_map/ppermute | solution.py:468
  91.6 1.4 %copy-start.7 = (bf16[4,8,16,1024]{3,2,1,0:T(8,128)(2,1)}, bf16[4,8,16,1024]{3,2,1,0:T(8,128)(2,1)S(1)}, u32[]{:S(2)}) copy-start(bf16[4,8,16,1024]{3,2,1,0:T(8,128)(2,1)S(1)} %all-to-all-done.4.rows1) | copy-start | bytes 3145732
  93.0 18.9 %all-to-all-start.5 = ((bf16[4,8,16,1152]{3,2,1,0:T(8,128)(2,1)}), bf16[4,8,16,1152]{3,2,1,0:T(8,128)(2,1)}, u32[]{:S(2)}, u32[]{:S(2)}) async-start(bf16[4,8,16,1152]{3,2,1,0:T(8,128)(2,1)} %fan_pivots.1), calls=%async_computation.5 | async-start | bytes 2359296 | tf_op jit(solution)/shard_map/all_to_all | solution.py:464
  97.8 12.6 %collective-permute-start.7 = (bf16[512,512]{1,0:T(8,128)(2,1)S(1)}, bf16[512,512]{1,0:T(8,128)(2,1)S(1)}, u32[]{:S(2)}, u32[]{:S(2)}) collective-permute-start(bf16[512,512]{1,0:T(8,128)(2,1)S(1)} %get-tuple-element.86), channel_id=1, source_target_pairs={{2,4},{3,5},{10,12},{11,13},{18,20},{19,21},{26,28},{27,29},{34,36... | collective-permute-start | bytes 1572872 | tf_op jit(solution)/shard_map/ppermute | solution.py:471
  99.2 12.6 %collective-permute-start.8 = (bf16[512,512]{1,0:T(8,128)(2,1)S(1)}, bf16[512,512]{1,0:T(8,128)(2,1)S(1)}, u32[]{:S(2)}, u32[]{:S(2)}) collective-permute-start(bf16[512,512]{1,0:T(8,128)(2,1)S(1)} %get-tuple-element.85), channel_id=1, source_target_pairs={{6,4},{7,5},{14,12},{15,13},{22,20},{23,21},{30,28},{31,29},{38,36... | collective-permute-start | bytes 1572872 | tf_op jit(solution)/shard_map/ppermute | solution.py:471
  111.8 5.4 %copy-start = (bf16[2,512,512]{2,1,0:T(8,128)(2,1)}, bf16[2,512,512]{2,1,0:T(8,128)(2,1)S(1)}, u32[]{:S(2)}) copy-start(bf16[2,512,512]{2,1,0:T(8,128)(2,1)S(1)} %second_hop.1.cols_own) | copy-start | bytes 3145732
  111.9 5.4 %collective-permute-start.9 = (bf16[4,8,16,1152]{3,2,1,0:T(8,128)(2,1)}, bf16[4,8,16,1152]{3,2,1,0:T(8,128)(2,1)}, u32[]{:S(2)}, u32[]{:S(2)}) collective-permute-start(bf16[4,8,16,1152]{3,2,1,0:T(8,128)(2,1)} %all-to-all-done.5.piv_own), channel_id=1, source_target_pairs={{0,1},{1,0},{2,3},{3,2},{4,5},{5,4},{6,7},{7,6},{8,9},{9,8},{10,11... | collective-permute-start | bytes 3538952 | tf_op jit(solution)/shard_map/ppermute | solution.py:477
  112.0 5.3 %collective-permute-start.10 = (bf16[2,512,512]{2,1,0:T(8,128)(2,1)S(1)}, bf16[2,512,512]{2,1,0:T(8,128)(2,1)S(1)}, u32[]{:S(2)}, u32[]{:S(2)}) collective-permute-start(bf16[2,512,512]{2,1,0:T(8,128)(2,1)S(1)} %second_hop.1.cols_own), channel_id=1, source_target_pairs={{0,1},{1,0},{2,3},{3,2},{4,5},{5,4},{6,7},{7,6},{8,9},{9,8},{10,11... | collective-permute-start | bytes 3145736 | tf_op jit(solution)/shard_map/ppermute | solution.py:478
  112.5 20.3 %all-to-all-start.6 = ((bf16[4,8,16,1024]{3,2,1,0:T(8,128)(2,1)}), bf16[4,8,16,1024]{3,2,1,0:T(8,128)(2,1)S(1)}, u32[]{:S(2)}, u32[]{:S(2)}) async-start(bf16[4,8,16,1024]{3,2,1,0:T(8,128)(2,1)} %get-tuple-element.77), calls=%async_computation.6 | async-start | bytes 2097152 | tf_op jit(solution)/shard_map/all_to_all | solution.py:464
  117.3 1.0 copy-start.11

commit v8 on v7

--- a/solution.py
+++ b/solution.py
@@ -103,32 +103,39 @@
     return lax.fori_loop(0, NROWS, step, (0, 0), unroll=8)
 
 
-def head_kernel(second, row_map, mask, ranks, near, u, v, send, near_buf, u_buf, v_buf, sems):
+def head_kernel(second, row_map, mask, ranks, near, u, v, out, send, near_buf, u_buf, v_buf, sems, out_sems):
     row = lax.axis_index("row")
     col = lax.axis_index("col")
     owners = find_owners(row_map)
     panel = 1 if second else jnp.where(row == owners[0] >> 1, 0, 1)
     s = jnp.where(panel == 0, owners[0], owners[1]) & 1
-    copies = [
-        pltpu.make_async_copy(source.at[s], target, sems.at[i])
-        for i, (source, target) in enumerate(((u, u_buf), (v, v_buf), (near, near_buf)))
-    ]
+    moves = [(u.at[s], u_buf), (v.at[s], v_buf)]
+    moves += [(near.at[s, t], near_buf.at[t]) for t in (1, 0)]
+    copies = [pltpu.make_async_copy(*move, sems.at[i]) for i, move in enumerate(moves)]
     for copy in copies:
         copy.start()
-    for copy in copies:
-        copy.wait()
-    for t in range(2):
+    copies[0].wait()
+    copies[1].wait()
+    stores = []
+    for t in (1, 0):
         low = low_rank(kept_left(u_buf[t], ranks[s, t]), v_buf[t])
+        copies[3 - t].wait()
         tile = (near_buf[t].astype(F32) * mask[s, t].astype(F32) + low).astype(BF)
-        start = t * WIDE
-        send[:, :, start : start + TILE] = tile.reshape(PARTS, CHUNK, TILE)
-
-    @pl.when(col == panel)
-    def _():
-        tile = near_buf[0] * mask[s, 0].astype(F32).astype(BF)
-        factors = lane_blocks(kept_left(u_buf[0], ranks[s, 0]), v_buf[0])
-        send[:, :, :TILE] = tile.reshape(PARTS, CHUNK, TILE)
-        send[:, :, TILE:WIDE] = factors.reshape(PARTS, CHUNK, LANES)
+        lanes = pl.ds(t * WIDE, WIDE if t == 0 else TILE)
+        send[:, :, t * WIDE : t * WIDE + TILE] = tile.reshape(PARTS, CHUNK, TILE)
+        if t == 0:
+
+            @pl.when(col == panel)
+            def _():
+                raw = near_buf[0] * mask[s, 0].astype(F32).astype(BF)
+                factors = lane_blocks(kept_left(u_buf[0], ranks[s, 0]), v_buf[0])
+                send[:, :, :TILE] = raw.reshape(PARTS, CHUNK, TILE)
+                send[:, :, TILE:WIDE] = factors.reshape(PARTS, CHUNK, LANES)
+
+        stores.append(pltpu.make_async_copy(send.at[:, :, lanes], out.at[:, :, lanes], out_sems.at[t]))
+        stores[-1].start()
+    for store in stores:
+        store.wait()
 
 
 def head(second, row_map, mask, ranks, near, u, v):
@@ -139,12 +146,14 @@
         kernel,
         out_shape=in_hbm((PARTS, CHUNK, WIDE + TILE)),
         in_specs=[SMEM] * 3 + [ANY] * 3,
-        out_specs=VMEM,
+        out_specs=ANY,
         scratch_shapes=[
+            pltpu.VMEM((PARTS, CHUNK, WIDE + TILE), BF),
             pltpu.VMEM((2, TILE, TILE), BF),
             pltpu.VMEM((2, KMAX, TILE), BF),
             pltpu.VMEM((2, KMAX, TILE), BF),
-            pltpu.SemaphoreType.DMA((3,)),
+            pltpu.SemaphoreType.DMA((4,)),
+            pltpu.SemaphoreType.DMA((2,)),
         ],
         compiler_params=grant(12),
         name="head_again" if second else "head",
@@ -346,10 +355,10 @@
         row1 = jnp.where(lax.axis_index("col") > 1, row1, 0.0)
     pivot_rows[:TILE] = row0
     pivot_rows[TILE:] = row1.astype(BF)
-    for copy in ready:
-        copy.wait()
     stores = []
     for s in range(2):
+        if ready:
+            ready[s].wait()
         out_buf[s] = (tiles[s] - dot(mult[s], pivot_rows[...])).astype(BF)
         stores.append(pltpu.make_async_copy(out_buf.at[s], out.at[s, t], out_sems.at[s]))
         stores[-1].start()
@@ -389,7 +398,8 @@
     col = lax.axis_index("col")
     copies = [
         pltpu.make_async_copy(lead_in, lead, sems.at[0]),
-        pltpu.make_async_copy(own.at[:, 0], tiles, sems.at[1]),
+        pltpu.make_async_copy(own.at[0, 0], tiles.at[0], sems.at[1]),
+        pltpu.make_async_copy(own.at[1, 0], tiles.at[1], sems.at[2]),
     ]
     for copy in copies:
         copy.start()
@@ -411,7 +421,7 @@
             pltpu.VMEM((2, TILE, TILE), F32),
             pltpu.VMEM((2 * TILE, TILE), BF),
             pltpu.VMEM((2, TILE, TILE), BF),
-            pltpu.SemaphoreType.DMA((2,)),
+            pltpu.SemaphoreType.DMA((3,)),
             pltpu.SemaphoreType.DMA((2,)),
         ],
         compiler_params=grant(28),
@@ -437,24 +447,21 @@
     def scatter(part):
         return lax.all_to_all(part, "row", 0, 0)
 
-    def beside():
-        cols = columns(row_map, mask, ranks, near, u, v)
-        hop = [lax.ppermute(cols, "col", pairs(0, to)) for to in (1, 3)]
-        return cols, hop, own_tiles(row_map, mask, ranks, near, u, v)
+    cols = columns(row_map, mask, ranks, near, u, v)
+    hop = [lax.ppermute(cols, "col", pairs(0, to)) for to in (1, 3)]
+    own = own_tiles(row_map, mask, ranks, near, u, v)
+    device = jnp.arange(NROWS, dtype=jnp.int32) >> 1
+    apart_by = jnp.sum(jnp.where(row_map == 0, device, 0) - jnp.where(row_map == 1, device, 0))
+    got, hop, own, apart_by = lax.optimization_barrier((scatter(send), hop, own, apart_by))
 
     def apart():
         again = head(True, row_map, mask, ranks, near, u, v)
-        got = [scatter(send), scatter(again)]
-        return take(row_map, *got), beside()
+        return take(row_map, got, scatter(again))
 
     def merged():
-        got = scatter(send)
-        return take(row_map, got, got), beside()
-
-    device = jnp.arange(NROWS, dtype=jnp.int32) >> 1
-    apart_by = jnp.sum(jnp.where(row_map == 0, device, 0) - jnp.where(row_map == 1, device, 0))
-    one_device = apart_by == 0
-    line, (cols, hop, own) = lax.cond(one_device, apart, merged)
+        return take(row_map, got, got)
+
+    line = lax.cond(apart_by == 0, apart, merged)
 
     z_groups = [[y * NZ + z for z in range(NZ)] for y in range(NY)]
     y_groups = [[y * NZ + z for y in range(NY)] for z in range(NZ)]
@@ -465,7 +472,7 @@
 
     pivots, rows0, rows1 = fan(line)
     rows1 = gather(rows1)
-    hops = [lax.ppermute(pivots, "col", pairs(0, to)) for to in (1, 3, 2)]
+    hops = [lax.ppermute(pivots, "col", pairs(0, to)) for to in (3, 1, 2)]
     cols = jnp.where(x == 0, cols, hop[0] + hop[1])
     hops, rows1, cols = lax.optimization_barrier((hops, rows1, cols))
     hop = [lax.ppermute(cols[s], "col", pairs(source, 2)) for s, source in enumerate((1, 3))]

time: 137 us -> 134 us (0.978); the launches traced: 137 us -> 132 us
  waiting for transfers between devices: 41.2 us -> 36.8 us
    ppermute x5, waiting for transfers between devices: 10.5 us -> 7.64 us  [the longest x3 7.63 us: body(): hops = [lax.ppermute(pivots, 'col', pairs(0, to)) for to in (3, 1, 2)]]
  transfers between devices with their start and end apart: 13 -> 13, of which waited for: 4 -> 4; matrix products, arithmetic and copies ran while one was open for 1% -> 2% of each run, Pallas kernels for 16% -> 16%
where the time goes in v8:
time: 134 us; the launch traced here: 132 us
  waiting for transfers between devices  36.8 us (27%)
  starting transfers between devices  34.7 us (26%)
  Pallas kernels  32.6 us (24%)
  blocking collectives  22.5 us (17%)
  other arithmetic  2.34 us (2%)
  local copies, waits for them, and re-layouts  2.05 us (2%)
    all_to_all x1, blocking collectives, body(): line = lax.all_to_all(line, 'row', 0, 0, axis_index_groups=z_groups)  22.5 us
    all_to_all x1, waiting for transfers between devices, scatter(): return lax.all_to_all(part, 'row', 0, 0)  18.6 us
    all_to_all x3, starting transfers between devices, gather(): return lax.all_to_all(part, 'row', 0, 0, axis_index_groups=y_groups)  14.7 us
    pallas_call x1, Pallas kernels, panel(): pl.pallas_call(panel_kernel, out_shape=(pltpu.VMEM((2, TILE, 2 * TILE), B...  14.6 us
    all_to_all x1, starting transfers between devices, scatter(): return lax.all_to_all(part, 'row', 0, 0)  11.9 us
    ppermute x2, waiting for transfers between devices, body(): lax.ppermute(cols[s], 'col', pairs(source, 2))  10.5 us
    ppermute x3, waiting for transfers between devices, body(): hops = [lax.ppermute(pivots, 'col', pairs(0, to)) for to in (3, 1, 2)]  7.63 us
    pallas_call x1, Pallas kernels, head(): pl.pallas_call(kernel, out_shape=in_hbm((PARTS, CHUNK, WIDE + TILE)), in_...  3.87 us
  transfers between devices with their start and end apart: 13, of which 4 were waited for; matrix products, arithmetic and copies ran while one was open for 2% of the time, Pallas kernels for 16%

profile of v8, /device:TPU:12, one launch (start us, length us, event | category | flops | bytes accessed | tf_op | source)
XLA Modules:
  0.0 132.0 jit_solution(14199097563788805542)
XLA Ops:
  0.0 0.0 copy-start.6
  0.0 0.0 copy-start.7
  0.0 0.0 copy-start.8
  0.0 3.9 %head.1 = bf16[32,16,1152]{2,1,0:T(8,128)(2,1)} custom-call(s32[64]{0:T(128)} %row_map.5, s32[2,2]{1,0:T(2,128)} %bitcast.24, s32[2,2]{1,0:T(2,128)} %bitcast.28, bf16[2,2,512,512]{3,2,1,0:T(8,128)(2,1)} %bitcast.12, bf16[2,2,64,512]{3,2,1,0:T(8,128)(2,1)} %bitcast.16, bf16[2,2,64,512]{3,2,1,0:T(8,128)(2,1)} %bitcast.20), custom_call_target="tpu_custom_call" | custom-call | tf_op jit(solution)/shard_map/head/pallas_call | solution.py:145
  3.9 0.0 copy-start.1
  3.9 0.0 copy-start.3
  3.9 11.9 %all-to-all-start.1 = ((bf16[32,16,1152]{2,1,0:T(8,128)(2,1)}), bf16[32,16,1152]{2,1,0:T(8,128)(2,1)S(1)}, u32[]{:S(2)}, u32[]{:S(2)}) async-start(bf16[32,16,1152]{2,1,0:T(8,128)(2,1)} %head.1), calls=%async_computation.1 | async-start | bytes 2359296 | tf_op jit(solution)/shard_map/all_to_all | solution.py:448
  15.8 0.0 copy-done.6
  15.8 0.0 copy-done.7
  15.8 0.0 copy-done.8
  15.8 0.0 copy-done.1
  15.8 0.0 copy-done.3
  15.8 0.0 copy-start.4
  15.8 2.5 %columns.1 = bf16[2,512,512]{2,1,0:T(8,128)(2,1)} custom-call(s32[64]{0:T(128)S(1)} %copy-done.6, s32[2,2]{1,0:T(2,128)S(1)} %bitcast.25, s32[2,2]{1,0:T(2,128)S(1)} %bitcast.29, bf16[2,2,512,512]{3,2,1,0:T(8,128)(2,1)S(1)} %bitcast.13, bf16[2,2,64,512]{3,2,1,0:T(8,128)(2,1)S(1)} %bitcast.17, bf16[2,2,64,512]{3,2,1,0:T(8,128)(2,1)} %bitcast.21), custom_call_target="tpu_custom_call" | custom-call | tf_op jit(solution)/shard_map/columns/pallas_call | solution.py:177
  18.4 0.7 collective-permute-start.1
  19.1 1.6 %collective-permute-start = (bf16[2,512,512]{2,1,0:T(8,128)(2,1)}, bf16[2,512,512]{2,1,0:T(8,128)(2,1)}, u32[]{:S(2)}, u32[]{:S(2)}) collective-permute-start(bf16[2,512,512]{2,1,0:T(8,128)(2,1)} %columns.1), channel_id=1, source_target_pairs={{0,2},{1,3},{8,10},{9,11},{16,18},{17,19},{24,26},{25,27},{32,34},... | collective-permute-start | bytes 3145736 | tf_op jit(solution)/shard_map/ppermute | solution.py:451
  20.7 0.0 copy-done.4
  20.7 3.5 %own_tiles.1.own = f32[2,2,512,512]{3,2,1,0:T(8,128)} custom-call(s32[64]{0:T(128)S(1)} %copy-done.6, s32[2,2]{1,0:T(2,128)S(1)} %bitcast.26, s32[2,2]{1,0:T(2,128)S(1)} %bitcast.30, bf16[2,2,512,512]{3,2,1,0:T(8,128)(2,1)S(1)} %bitcast.14, bf16[2,2,64,512]{3,2,1,0:T(8,128)(2,1)S(1)} %bitcast.18, bf16[2,2,64,512]{3,2,1,0:T(8,128)(2,1)S(1)} %bitcast.23), custom_call_target="tpu_custom_call" | custom-call | flops 1073741824 | bytes 7340032 | tf_op jit(solution)/shard_map/own_tiles/pallas_call | solution.py:277
  24.3 0.6 fusion.1
  24.9 0.0 collective-permute-done.1
  24.9 0.0 copy-start.5
  24.9 1.0 copy-done.5
  25.9 0.0 collective-permute-done
  25.9 18.6 %all-to-all-done.1 = bf16[32,16,1152]{2,1,0:T(8,128)(2,1)S(1)} async-done(((bf16[32,16,1152]{2,1,0:T(8,128)(2,1)}), bf16[32,16,1152]{2,1,0:T(8,128)(2,1)S(1)}, u32[]{:S(2)}, u32[]{:S(2)}) %all-to-all-start.1) | async-done | bytes 1179680 | tf_op jit(solution)/shard_map/all_to_all | solution.py:448
  45.2 1.7 %conditional.1 = (bf16[8,16,2176]{2,1,0:T(8,128)(2,1)}) conditional(s32[]{:T(128)} %convert_element_type.3, (s32[64]{0:T(128)S(1)}, bf16[32,16,1152]{2,1,0:T(8,128)(2,1)S(1)}) %tuple.25, (s32[64]{0:T(128)S(1)}, s32[2,2]{1,0:T(2,128)S(1)}, s32[2,2]{1,0:T(2,128)S(1)}, bf16[2,2,512,512]{3,2,1,0:T(8,128)(2,1)S(1)}, bf16[2,2,64,512]{3,2,1,0:T(8,128)(2,1)S(1)}, ...), branch_computations={%region_1.2_spmd, %region_2.3_spmd} | conditional | bytes 2359304 | solution.py:464
  45.2 1.6 %take.2 = bf16[8,16,2176]{2,1,0:T(8,128)(2,1)} custom-call(s32[64]{0:T(128)S(1)} %get-tuple-element.26.row_map, bf16[32,16,1152]{2,1,0:T(8,128)(2,1)S(1)} %get-tuple-element.27.got0.got1, bf16[32,16,1152]{2,1,0:T(8,128)(2,1)S(1)} %get-tuple-element.27.got0.got1), custom_call_target="tpu_custom_call" | custom-call | tf_op jit(solution)/shard_map/cond/branch_0_fun/take/pallas_call | solution.py:204
  46.9 22.5 %all_to_all.30.line = bf16[8,16,2176]{2,1,0:T(8,128)(2,1)S(1)} all-to-all(bf16[8,16,2176]{2,1,0:T(8,128)(2,1)} %get-tuple-element.75), channel_id=1, replica_groups={{0,8,16,24,32,40,48,56},{64,72,80,88,96,104,112,120},{128,136,144,152,1..., dimensions={0} | all-to-all | bytes 1114112 | tf_op jit(solution)/shard_map/all_to_all | solution.py:468
  69.4 1.5 %fan.1 = (bf16[8,16,1152]{2,1,0:T(8,128)(2,1)S(1)}, bf16[4,8,16,1024]{3,2,1,0:T(8,128)(2,1)}, bf16[4,8,16,1024]{3,2,1,0:T(8,128)(2,1)}) custom-call(bf16[8,16,2176]{2,1,0:T(8,128)(2,1)S(1)} %all_to_all.30.line), custom_call_target="tpu_custom_call" | custom-call | tf_op jit(solution)/shard_map/fan/pallas_call | solution.py:224
  70.8 0.0 copy-start.2
  70.9 5.1 %all-to-all-start.3 = ((bf16[4,8,16,1024]{3,2,1,0:T(8,128)(2,1)}), bf16[4,8,16,1024]{3,2,1,0:T(8,128)(2,1)}, u32[]{:S(2)}, u32[]{:S(2)}) async-start(bf16[4,8,16,1024]{3,2,1,0:T(8,128)(2,1)} %get-tuple-element.58), calls=%async_computation.3 | async-start | bytes 2097152 | tf_op jit(solution)/shard_map/all_to_all | solution.py:471
  75.9 1.3 collective-permute-start.4
  77.2 0.7 collective-permute-start.3
  77.9 0.7 collective-permute-start.2
  78.6 0.0 copy-done.2
  78.6 1.7 %add_select_fusion.cols = bf16[2,512,512]{2,1,0:T(8,128)(2,1)S(1)} fusion(bf16[2,512,512]{2,1,0:T(8,128)(2,1)S(1)} %copy-done.2, bf16[2,512,512]{2,1,0:T(8,128)(2,1)} %collective-permute-done, bf16[2,512,512]{2,1,0:T(8,128)(2,1)} %copy-done.5, pred[]{:T(512)S(6)} %eq.19), kind=kLoop, calls=%fused_computation | loop fusion | flops 1048576 | bytes 4194305 | tf_op jit(solution)/shard_map/jit(_where)/select_n | solution.py:476
  80.3 7.6 %collective-permute-done.4.hop2 = bf16[8,16,1152]{2,1,0:T(8,128)(2,1)S(1)} collective-permute-done((bf16[8,16,1152]{2,1,0:T(8,128)(2,1)S(1)}, bf16[8,16,1152]{2,1,0:T(8,128)(2,1)S(1)}, u32[]{:S(2)}, u32[]{:S(2)}) %collective-permute-start.4) | collective-permute-done | bytes 294944 | tf_op jit(solution)/shard_map/ppermute | solution.py:475
  87.9 0.0 collective-permute-done.3.hop3
  87.9 0.0 collective-permute-done.2.hop1
  87.9 0.0 all-to-all-done.3.rows1
  87.9 1.1 fan_pivots.1
  89.0 4.8 %all-to-all-start.4 = ((bf16[4,8,16,1152]{3,2,1,0:T(8,128)(2,1)}), bf16[4,8,16,1152]{3,2,1,0:T(8,128)(2,1)}, u32[]{:S(2)}, u32[]{:S(2)}) async-start(bf16[4,8,16,1152]{3,2,1,0:T(8,128)(2,1)} %fan_pivots.1), calls=%async_computation.4 | async-start | bytes 2359296 | tf_op jit(solution)/shard_map/all_to_all | solution.py:471
  93.9 0.1 slice_bitcast_fusion
  94.0 1.3 collective-permute-start.6
  95.3 1.3 collective-permute-start.5
  96.6 9.8 %collective-permute-done.6.hop3 = bf16[512,512]{1,0:T(8,128)(2,1)S(1)} collective-permute-done((bf16[512,512]{1,0:T(8,128)(2,1)S(1)}, bf16[512,512]{1,0:T(8,128)(2,1)S(1)}, u32[]{:S(2)}, u32[]{:S(2)}) %collective-permute-start.6) | collective-permute-done | bytes 524320 | tf_op jit(solution)/shard_map/ppermute | solution.py:478
  106.3 0.7 collective-permute-done.5.hop1
  107.0 0.1 second_hop.1.cols_own
  107.2 0.0 copy-start
  107.2 0.0 all-to-all-done.4.piv_own
  107.2 0.1 collective-permute-start.7
  107.3 0.5 collective-permute-start.8
  107.8 4.8 %all-to-all-start.5 = ((bf16[4,8,16,1024]{3,2,1,0:T(8,128)(2,1)}), bf16[4,8,16,1024]{3,2,1,0:T(8,128)(2,1)S(1)}, u32[]{:S(2)}, u32[]{:S(2)}) async-start(bf16[4,8,16,1024]{3,2,1,0:T(8,128)(2,1)} %get-tuple-element.65), calls=%async_computation.5 | async-start | bytes 2097152 | tf_op jit(solution)/shard_map/all_to_all | solution.py:471
  112.6 0.0 collective-permute-done.8.cols_other
  112.6 0.0 copy-done
  112.6 0.0 copy-start.9
  112.6 1.0 copy-done.9
  113.6 0.0 collective-permute-done.7.piv_other
  113.6 14.6 %panel.1 = (bf16[2,512,1024]{2,1,0:T(8,128)(2,1)S(1)}, bf16[512,512]{1,0:T(8,128)(2,1)}, bf16[2,2,512,512]{3,2,1,0:T(8,128)(2,1)}) custom-call(s32[64]{0:T(128)S(1)} %copy-done.6, bf16[4,8,16,1152]{3,2,1,0:T(8,128)(2,1)} %all-to-all-done.4.piv_own, bf16[4,8,16,1152]{3,2,1,0:T(8,128)(2,1)} %collective-permute-done.7.piv_other, bf16[2,512,512]{2,1,0:T(8,128)(2,1)} %copy-done, ...), custom_call_target="tpu_custom_call" | custom-call | flops 10200547328 | bytes 5242880 | tf_op jit(solution)/shard_map/panel/pallas_call | solution.py:370
  128.1 0.0 all-to-all-done.5.rows
  128.1 3.7 %last.1 = bf16[2,2,512,512]{3,2,1,0:T(8,128)(2,1)} custom-call(bf16[4,8,16,1024]{3,2,1,0:T(8,128)(2,1)S(1)} %all-to-all-done.5.rows, f32[2,2,512,512]{3,2,1,0:T(8,128)} %own_tiles.1.own, bf16[512,512]{1,0:T(8,128)(2,1)} %get-tuple-element.70.lead_in, bf16[2,512,1024]{2,1,0:T(8,128)(2,1)S(1)} %get-tuple-element.71.mult, ...), custom_call_target="tpu_custom_call", output_to_operand_aliasing={{}: (4, {})} | custom-call | flops 1610612736 | bytes 6291456 | tf_op jit(solution)/shard_map/last/pallas_call | solution.py:413
Async XLA Ops:
  0.0 15.8 %copy-start.6 = (s32[64]{0:T(128)S(1)}, s32[64]{0:T(128)}, u32[]{:S(2)}) copy-start(s32[64]{0:T(128)} %row_map.5) | copy-start | bytes 772
  0.0 15.8 %copy-start.7 = (s32[2,2,1]{1,2,0:T(1,128)S(1)}, s32[2,2,1]{1,2,0:T(1,128)}, u32[]{:S(2)}) copy-start(s32[2,2,1]{1,2,0:T(1,128)} %param.11) | copy-start | bytes 52
  0.0 15.8 %copy-start.8 = (s32[2,2,1]{1,2,0:T(1,128)S(1)}, s32[2,2,1]{1,2,0:T(1,128)}, u32[]{:S(2)}) copy-start(s32[2,2,1]{1,2,0:T(1,128)} %param.12) | copy-start | bytes 52
  3.9 11.9 %copy-start.1 = (bf16[2,2,1,512,512]{4,3,2,1,0:T(8,128)(2,1)S(1)}, bf16[2,2,1,512,512]{4,3,2,1,0:T(8,128)(2,1)}, u32[]{:S(2)}) copy-start(bf16[2,2,1,512,512]{4,3,2,1,0:T(8,128)(2,1)} %param.8) | copy-start | bytes 6291460
  3.9 11.9 %copy-start.3 = (bf16[2,2,1,64,512]{4,3,2,1,0:T(8,128)(2,1)S(1)}, bf16[2,2,1,64,512]{4,3,2,1,0:T(8,128)(2,1)}, u32[]{:S(2)}) copy-start(bf16[2,2,1,64,512]{4,3,2,1,0:T(8,128)(2,1)} %param.9) | copy-start | bytes 786436
  3.9 40.6 %all-to-all-start.1 = ((bf16[32,16,1152]{2,1,0:T(8,128)(2,1)}), bf16[32,16,1152]{2,1,0:T(8,128)(2,1)S(1)}, u32[]{:S(2)}, u32[]{:S(2)}) async-start(bf16[32,16,1152]{2,1,0:T(8,128)(2,1)} %head.1), calls=%async_computation.1 | async-start | bytes 2359296 | tf_op jit(solution)/shard_map/all_to_all | solution.py:448
  15.8 4.9 %copy-start.4 = (bf16[2,2,1,64,512]{4,3,2,1,0:T(8,128)(2,1)S(1)}, bf16[2,2,1,64,512]{4,3,2,1,0:T(8,128)(2,1)}, u32[]{:S(2)}) copy-start(bf16[2,2,1,64,512]{4,3,2,1,0:T(8,128)(2,1)} %param.10) | copy-start | bytes 786436
  18.4 6.6 %collective-permute-start.1 = (bf16[2,512,512]{2,1,0:T(8,128)(2,1)}, bf16[2,512,512]{2,1,0:T(8,128)(2,1)S(1)}, u32[]{:S(2)}, u32[]{:S(2)}) collective-permute-start(bf16[2,512,512]{2,1,0:T(8,128)(2,1)} %columns.1), channel_id=1, source_target_pairs={{0,6},{1,7},{8,14},{9,15},{16,22},{17,23},{24,30},{25,31},{32,38},... | collective-permute-start | bytes 3145736 | tf_op jit(solution)/shard_map/ppermute | solution.py:451
  19.1 6.8 %collective-permute-start = (bf16[2,512,512]{2,1,0:T(8,128)(2,1)}, bf16[2,512,512]{2,1,0:T(8,128)(2,1)}, u32[]{:S(2)}, u32[]{:S(2)}) collective-permute-start(bf16[2,512,512]{2,1,0:T(8,128)(2,1)} %columns.1), channel_id=1, source_target_pairs={{0,2},{1,3},{8,10},{9,11},{16,18},{17,19},{24,26},{25,27},{32,34},... | collective-permute-start | bytes 3145736 | tf_op jit(solution)/shard_map/ppermute | solution.py:451
  24.9 1.0 copy-start.5
  70.8 7.7 %copy-start.2 = (bf16[2,512,512]{2,1,0:T(8,128)(2,1)S(1)}, bf16[2,512,512]{2,1,0:T(8,128)(2,1)}, u32[]{:S(2)}) copy-start(bf16[2,512,512]{2,1,0:T(8,128)(2,1)} %columns.1) | copy-start | bytes 3145732
  70.9 17.1 %all-to-all-start.3 = ((bf16[4,8,16,1024]{3,2,1,0:T(8,128)(2,1)}), bf16[4,8,16,1024]{3,2,1,0:T(8,128)(2,1)}, u32[]{:S(2)}, u32[]{:S(2)}) async-start(bf16[4,8,16,1024]{3,2,1,0:T(8,128)(2,1)} %get-tuple-element.58), calls=%async_computation.3 | async-start | bytes 2097152 | tf_op jit(solution)/shard_map/all_to_all | solution.py:471
  75.9 12.0 %collective-permute-start.4 = (bf16[8,16,1152]{2,1,0:T(8,128)(2,1)S(1)}, bf16[8,16,1152]{2,1,0:T(8,128)(2,1)S(1)}, u32[]{:S(2)}, u32[]{:S(2)}) collective-permute-start(bf16[8,16,1152]{2,1,0:T(8,128)(2,1)S(1)} %get-tuple-element.57.own), channel_id=1, source_target_pairs={{0,4},{1,5},{8,12},{9,13},{16,20},{17,21},{24,28},{25,29},{32,36},... | collective-permute-start | bytes 884744 | tf_op jit(solution)/shard_map/ppermute | solution.py:475
  77.2 10.7 %collective-permute-start.3 = (bf16[8,16,1152]{2,1,0:T(8,128)(2,1)S(1)}, bf16[8,16,1152]{2,1,0:T(8,128)(2,1)S(1)}, u32[]{:S(2)}, u32[]{:S(2)}) collective-permute-start(bf16[8,16,1152]{2,1,0:T(8,128)(2,1)S(1)} %get-tuple-element.57.own), channel_id=1, source_target_pairs={{0,2},{1,3},{8,10},{9,11},{16,18},{17,19},{24,26},{25,27},{32,34},... | collective-permute-start | bytes 884744 | tf_op jit(solution)/shard_map/ppermute | solution.py:475
  77.9 10.0 %collective-permute-start.2 = (bf16[8,16,1152]{2,1,0:T(8,128)(2,1)S(1)}, bf16[8,16,1152]{2,1,0:T(8,128)(2,1)S(1)}, u32[]{:S(2)}, u32[]{:S(2)}) collective-permute-start(bf16[8,16,1152]{2,1,0:T(8,128)(2,1)S(1)} %get-tuple-element.57.own), channel_id=1, source_target_pairs={{0,6},{1,7},{8,14},{9,15},{16,22},{17,23},{24,30},{25,31},{32,38},... | collective-permute-start | bytes 884744 | tf_op jit(solution)/shard_map/ppermute | solution.py:475
  89.0 18.1 %all-to-all-start.4 = ((bf16[4,8,16,1152]{3,2,1,0:T(8,128)(2,1)}), bf16[4,8,16,1152]{3,2,1,0:T(8,128)(2,1)}, u32[]{:S(2)}, u32[]{:S(2)}) async-start(bf16[4,8,16,1152]{3,2,1,0:T(8,128)(2,1)} %fan_pivots.1), calls=%async_computation.4 | async-start | bytes 2359296 | tf_op jit(solution)/shard_map/all_to_all | solution.py:471
  94.0 12.4 %collective-permute-start.6 = (bf16[512,512]{1,0:T(8,128)(2,1)S(1)}, bf16[512,512]{1,0:T(8,128)(2,1)S(1)}, u32[]{:S(2)}, u32[]{:S(2)}) collective-permute-start(bf16[512,512]{1,0:T(8,128)(2,1)S(1)} %get-tuple-element.73), channel_id=1, source_target_pairs={{6,4},{7,5},{14,12},{15,13},{22,20},{23,21},{30,28},{31,29},{38,36... | collective-permute-start | bytes 1572872 | tf_op jit(solution)/shard_map/ppermute | solution.py:478
  95.3 11.8 %collective-permute-start.5 = (bf16[512,512]{1,0:T(8,128)(2,1)S(1)}, bf16[512,512]{1,0:T(8,128)(2,1)S(1)}, u32[]{:S(2)}, u32[]{:S(2)}) collective-permute-start(bf16[512,512]{1,0:T(8,128)(2,1)S(1)} %get-tuple-element.74), channel_id=1, source_target_pairs={{2,4},{3,5},{10,12},{11,13},{18,20},{19,21},{26,28},{27,29},{34,36... | collective-permute-start | bytes 1572872 | tf_op jit(solution)/shard_map/ppermute | solution.py:478
  107.2 5.4 %copy-start = (bf16[2,512,512]{2,1,0:T(8,128)(2,1)}, bf16[2,512,512]{2,1,0:T(8,128)(2,1)S(1)}, u32[]{:S(2)}) copy-start(bf16[2,512,512]{2,1,0:T(8,128)(2,1)S(1)} %second_hop.1.cols_own) | copy-start | bytes 3145732
  107.2 6.4 %collective-permute-start.7 = (bf16[4,8,16,1152]{3,2,1,0:T(8,128)(2,1)}, bf16[4,8,16,1152]{3,2,1,0:T(8,128)(2,1)}, u32[]{:S(2)}, u32[]{:S(2)}) collective-permute-start(bf16[4,8,16,1152]{3,2,1,0:T(8,128)(2,1)} %all-to-all-done.4.piv_own), channel_id=1, source_target_pairs={{0,1},{1,0},{2,3},{3,2},{4,5},{5,4},{6,7},{7,6},{8,9},{9,8},{10,11... | collective-permute-start | bytes 3538952 | tf_op jit(solution)/shard_map/ppermute | solution.py:484
  107.3 5.3 %collective-permute-start.8 = (bf16[2,512,512]{2,1,0:T(8,128)(2,1)S(1)}, bf16[2,512,512]{2,1,0:T(8,128)(2,1)S(1)}, u32[]{:S(2)}, u32[]{:S(2)}) collective-permute-start(bf16[2,512,512]{2,1,0:T(8,128)(2,1)S(1)} %second_hop.1.cols_own), channel_id=1, source_target_pairs={{0,1},{1,0},{2,3},{3,2},{4,5},{5,4},{6,7},{7,6},{8,9},{9,8},{10,11... | collective-permute-start | bytes 3145736 | tf_op jit(solution)/shard_map/ppermute | solution.py:485
  107.8 20.3 %all-to-all-start.5 = ((bf16[4,8,16,1024]{3,2,1,0:T(8,128)(2,1)}), bf16[4,8,16,1024]{3,2,1,0:T(8,128)(2,1)S(1)}, u32[]{:S(2)}, u32[]{:S(2)}) async-start(bf16[4,8,16,1024]{3,2,1,0:T(8,128)(2,1)} %get-tuple-element.65), calls=%async_computation.5 | async-start | bytes 2097152 | tf_op jit(solution)/shard_map/all_to_all | solution.py:471
  112.6 1.0 copy-start.9
